TPU v7x, 512 devices: a whole 4x4x16 slice. The times are simulated.
512 devices in a mesh: seq: 128 (over z, y, core), head: 4 (over x).
Axes of the slice: x: 4, y: 4, z: 16, core: 2. Of those that a mesh axis runs over, the one named last changes fastest.
Arguments:
- queries: bfloat16 [73728, 512], P('seq', 'head'), may hold values from -16 to 16, as said below
- key_states: bfloat16 [73728, 512], P('seq', 'head'), may hold values from -5 to 5, as said below
- value_states: bfloat16 [73728, 512], P('seq', 'head'), may hold values from -8 to 8
- out_weight: bfloat16 [512, 1024], P(None, 'head'), may hold values from -0.25 to 0.25
- output_grad: bfloat16 [73728, 1024], P('seq', 'head'), may hold values from -6 to 6
- rand_blocks: int32 [1152, 3], P('seq'), may hold values from 0 to 1151, as said below
- global_pos: int32 [128], replicated, may hold values from 0 to 73727, as said below
Outputs:
- projected: bfloat16 [73728, 1024], P('seq', 'head')
- query_grad: bfloat16 [73728, 512], P('seq', 'head')
- key_grad: bfloat16 [73728, 512], P('seq', 'head')
- value_grad: bfloat16 [73728, 512], P('seq', 'head')
- weight_grad: float32 [512, 1024], P(None, 'head')
Inputs may be any that keep to these rules, and one draw needn't show every extreme that they name: `queries`: queries drawn for attention, of either sign. `key_states`: keys drawn for attention, of either sign. `rand_blocks`: block indices. Among the 27 entries of the 9 query blocks of one index of seq, no two name blocks of the same index of seq (block // 9); in every draw some index of seq has exactly 1 of its blocks named by the entries of every index of seq. `global_pos`: distinct token positions.
All inputs are finite; a program needn't handle non-finite values.
Results may differ from a plain program's by a relative error of at most 0.038.
Values may be sent and summed in bfloat16 or wider, within the bound.
No kernel may reach another device: no remote copies, remote signals or barrier semaphores. Data moves between devices by JAX's collectives and lax.ppermute only.
A program may use at most 128 MiB of HBM per device.

v0:
```python
import math

import jax
import jax.numpy as jnp
from jax import lax
from jax.sharding import PartitionSpec as P

HEAD_DIM = 64
BLOCK = 64
R = 3


def extended(cells, sides, width):
    for axis, dim in sides:
        count = lax.axis_size(axis)
        ends = count - 1
        head = lax.slice_in_dim(cells, 0, width, axis=dim)
        tail = lax.slice_in_dim(cells, cells.shape[dim] - width, cells.shape[dim], axis=dim)
        cells = jnp.concatenate(
            [
                lax.ppermute(tail, axis, [(i, (i + 1) % count) for i in range(ends)]),
                cells,
                lax.ppermute(head, axis, [((i + 1) % count, i) for i in range(ends)]),
            ],
            axis=dim,
        )
    return cells


def as_sent(array):
    return jax.tree.map(lambda a: a.astype(jnp.bfloat16) if a.dtype == jnp.float32 else a, array)


def shards(queries, key_states, value_states, out_weight, output_grad, rand_blocks, global_pos):
    tokens_here, columns = queries.shape
    head_count = columns // HEAD_DIM
    blocks_here = tokens_here // BLOCK
    seq_count = lax.axis_size("seq")
    position = lax.axis_index("seq")
    score_scale = 1.0 / math.sqrt(HEAD_DIM)
    all_columns = out_weight.shape[0]
    feature_count = output_grad.shape[1]
    partial_grad = lax.dot_general(
        output_grad, out_weight, (((1,), (1,)), ((), ())), preferred_element_type=jnp.float32
    )
    grad_att = lax.psum_scatter(partial_grad, "head", scatter_dimension=1, tiled=True).astype(
        jnp.bfloat16
    )
    stacked = jnp.stack([key_states, value_states])
    padded = extended(stacked, (("seq", 1),), BLOCK)
    window_views = [
        padded[:, shift_by * BLOCK : shift_by * BLOCK + tokens_here].reshape(
            2, blocks_here, BLOCK, columns
        )
        for shift_by in range(3)
    ]
    windows = jnp.concatenate(window_views, axis=2)
    block_ids = jnp.arange(blocks_here)
    left_live = (block_ids > 0) | (position > 0)
    right_live = (block_ids < blocks_here - 1) | (position < seq_count - 1)
    window_live = jnp.concatenate(
        [
            jnp.broadcast_to(left_live[:, None], (blocks_here, BLOCK)),
            jnp.ones((blocks_here, BLOCK), bool),
            jnp.broadcast_to(right_live[:, None], (blocks_here, BLOCK)),
        ],
        axis=1,
    )
    offset = position * tokens_here
    picker = global_pos[:, None] - offset == jnp.arange(tokens_here)[None, :]
    panel_terms = jnp.einsum(
        "gt,xtc->xgc", picker.astype(jnp.bfloat16), stacked, preferred_element_type=jnp.float32
    )
    panel_pair = lax.psum(panel_terms, "seq").astype(jnp.bfloat16)
    global_count = panel_pair.shape[1]
    panel_key = panel_pair[0].reshape(global_count, head_count, HEAD_DIM)
    panel_value = panel_pair[1].reshape(global_count, head_count, HEAD_DIM)
    wanted_blocks = rand_blocks.reshape(-1)
    requests = wanted_blocks.shape[0]
    capacity = (requests + seq_count - 1) // seq_count
    slot_count = seq_count * capacity
    owner_dev = wanted_blocks // blocks_here
    local_block = wanted_blocks % blocks_here
    request_order = jnp.arange(requests)
    earlier = (owner_dev[:, None] == owner_dev[None, :]) & (
        request_order[None, :] < request_order[:, None]
    )
    slot_index = owner_dev * capacity + jnp.sum(earlier.astype(jnp.int32), axis=1)
    wanted = jnp.full((slot_count,), -1, jnp.int32).at[slot_index].set(local_block)
    asked_blocks = lax.all_to_all(wanted, "seq", split_axis=0, concat_axis=0, tiled=True)
    asked_live = asked_blocks >= 0
    asked_target = jnp.clip(asked_blocks, 0, blocks_here - 1)
    own_blocks = stacked.reshape(2, blocks_here, BLOCK, columns)
    served = jnp.take(own_blocks, asked_target, axis=1)
    served = jnp.where(asked_live[None, :, None, None], served, jnp.zeros_like(served))
    fetched = lax.all_to_all(served, "seq", split_axis=1, concat_axis=1, tiled=True)
    random_pair = jnp.take(fetched, slot_index, axis=1).reshape(2, blocks_here, R * BLOCK, columns)
    group_blocks = max(
        (d for d in range(1, blocks_here + 1) if blocks_here % d == 0 and d * BLOCK <= 768)
    )
    groups = blocks_here // group_blocks

    def grouped(matrix):
        return matrix.reshape((groups, group_blocks) + matrix.shape[1:])

    def attend(group_items):
        query_part, grad_part, win_key, win_value, win_live, rnd_key, rnd_value = group_items
        score_window = (
            jnp.einsum("bqhd,bkhd->bhqk", query_part, win_key, preferred_element_type=jnp.float32)
            * score_scale
        )
        score_window = jnp.where(win_live[:, None, None, :], score_window, -jnp.inf)
        score_global = (
            jnp.einsum("bqhd,khd->bhqk", query_part, panel_key, preferred_element_type=jnp.float32)
            * score_scale
        )
        score_random = (
            jnp.einsum("bqhd,bkhd->bhqk", query_part, rnd_key, preferred_element_type=jnp.float32)
            * score_scale
        )
        row_top = jnp.maximum(
            jnp.maximum(
                jnp.max(score_window, axis=-1, keepdims=True),
                jnp.max(score_global, axis=-1, keepdims=True),
            ),
            jnp.max(score_random, axis=-1, keepdims=True),
        )
        row_total = (
            jnp.sum(jnp.exp(score_window - row_top), axis=-1, keepdims=True)
            + jnp.sum(jnp.exp(score_global - row_top), axis=-1, keepdims=True)
            + jnp.sum(jnp.exp(score_random - row_top), axis=-1, keepdims=True)
        )
        log_total = row_top + jnp.log(row_total)
        probs_window = jnp.exp(score_window - log_total)
        probs_global = jnp.exp(score_global - log_total)
        probs_random = jnp.exp(score_random - log_total)
        weight_window = probs_window.astype(jnp.bfloat16)
        weight_global = probs_global.astype(jnp.bfloat16)
        weight_random = probs_random.astype(jnp.bfloat16)
        attended = (
            jnp.einsum(
                "bhqk,bkhd->bqhd", weight_window, win_value, preferred_element_type=jnp.float32
            )
            + jnp.einsum(
                "bhqk,khd->bqhd", weight_global, panel_value, preferred_element_type=jnp.float32
            )
            + jnp.einsum(
                "bhqk,bkhd->bqhd", weight_random, rnd_value, preferred_element_type=jnp.float32
            )
        ).astype(jnp.bfloat16)
        delta = jnp.einsum(
            "bqhd,bqhd->bhq", grad_part, attended, preferred_element_type=jnp.float32
        )[..., None]
        slope_window = (
            probs_window
            * (
                jnp.einsum(
                    "bqhd,bkhd->bhqk", grad_part, win_value, preferred_element_type=jnp.float32
                )
                - delta
            )
        ).astype(jnp.bfloat16)
        slope_global = (
            probs_global
            * (
                jnp.einsum(
                    "bqhd,khd->bhqk", grad_part, panel_value, preferred_element_type=jnp.float32
                )
                - delta
            )
        ).astype(jnp.bfloat16)
        slope_random = (
            probs_random
            * (
                jnp.einsum(
                    "bqhd,bkhd->bhqk", grad_part, rnd_value, preferred_element_type=jnp.float32
                )
                - delta
            )
        ).astype(jnp.bfloat16)
        query_grad = (
            score_scale
            * (
                jnp.einsum(
                    "bhqk,bkhd->bqhd", slope_window, win_key, preferred_element_type=jnp.float32
                )
                + jnp.einsum(
                    "bhqk,khd->bqhd", slope_global, panel_key, preferred_element_type=jnp.float32
                )
                + jnp.einsum(
                    "bhqk,bkhd->bqhd", slope_random, rnd_key, preferred_element_type=jnp.float32
                )
            )
        ).astype(jnp.bfloat16)
        key_window = score_scale * jnp.einsum(
            "bhqk,bqhd->bkhd", slope_window, query_part, preferred_element_type=jnp.float32
        )
        value_window = jnp.einsum(
            "bhqk,bqhd->bkhd", weight_window, grad_part, preferred_element_type=jnp.float32
        )
        key_global = score_scale * jnp.einsum(
            "bhqk,bqhd->khd", slope_global, query_part, preferred_element_type=jnp.float32
        )
        value_global = jnp.einsum(
            "bhqk,bqhd->khd", weight_global, grad_part, preferred_element_type=jnp.float32
        )
        outputs = [
            attended,
            query_grad,
            key_window,
            value_window,
            key_global,
            value_global,
            log_total[..., 0],
            delta[..., 0],
        ]
        outputs.append(
            score_scale
            * jnp.einsum(
                "bhqk,bqhd->bkhd", slope_random, query_part, preferred_element_type=jnp.float32
            )
        )
        outputs.append(
            jnp.einsum(
                "bhqk,bqhd->bkhd", weight_random, grad_part, preferred_element_type=jnp.float32
            )
        )
        return tuple(outputs)

    results = lax.map(
        attend,
        (
            grouped(queries.reshape(blocks_here, BLOCK, head_count, HEAD_DIM)),
            grouped(grad_att.reshape(blocks_here, BLOCK, head_count, HEAD_DIM)),
            grouped(windows[0].reshape(blocks_here, 3 * BLOCK, head_count, HEAD_DIM)),
            grouped(windows[1].reshape(blocks_here, 3 * BLOCK, head_count, HEAD_DIM)),
            grouped(window_live),
            grouped(random_pair[0].reshape(blocks_here, R * BLOCK, head_count, HEAD_DIM)),
            grouped(random_pair[1].reshape(blocks_here, R * BLOCK, head_count, HEAD_DIM)),
        ),
    )
    attended = results[0].reshape(tokens_here, columns)
    query_grad = results[1].reshape(tokens_here, columns)
    pair_window = jnp.stack(
        [
            results[2].reshape(blocks_here, 3 * BLOCK, columns),
            results[3].reshape(blocks_here, 3 * BLOCK, columns),
        ]
    )
    padded_grad = jnp.zeros((2, tokens_here + 2 * BLOCK, columns), jnp.float32)
    for shift_by in range(3):
        padded_grad = padded_grad.at[:, shift_by * BLOCK : shift_by * BLOCK + tokens_here].add(
            pair_window[:, :, shift_by * BLOCK : (shift_by + 1) * BLOCK].reshape(
                2, tokens_here, columns
            )
        )
    own_grads = padded_grad[:, BLOCK : BLOCK + tokens_here]
    rim_rows = jnp.concatenate(
        [padded_grad[:, :BLOCK], padded_grad[:, BLOCK + tokens_here :]], axis=1
    )
    rim_arrived = extended(rim_rows.astype(jnp.bfloat16), (("seq", 1),), BLOCK).astype(
        rim_rows.dtype
    )
    own_grads = own_grads.at[:, :BLOCK].add(rim_arrived[:, :BLOCK])
    own_grads = own_grads.at[:, tokens_here - BLOCK :].add(rim_arrived[:, 3 * BLOCK :])
    global_part = jnp.stack([jnp.sum(results[4], axis=0), jnp.sum(results[5], axis=0)]).reshape(
        2, global_count, columns
    )
    global_summed = lax.psum(global_part, "seq")
    own_grads = own_grads + jnp.einsum(
        "gt,xgc->xtc", picker.astype(jnp.float32), global_summed, precision=lax.Precision.HIGHEST
    )
    random_grad = jnp.stack([results[8], results[9]]).reshape(2, requests, BLOCK, columns)
    outgoing = (
        jnp.zeros((2, slot_count, BLOCK, columns), jnp.float32).at[:, slot_index].set(random_grad)
    )
    returned = lax.all_to_all(
        outgoing.astype(jnp.bfloat16), "seq", split_axis=1, concat_axis=1, tiled=True
    ).astype(outgoing.dtype)
    returned = jnp.where(asked_live[None, :, None, None], returned, 0.0)
    own_grads = (
        own_grads.reshape(2, blocks_here, BLOCK, columns)
        .at[:, asked_target]
        .add(returned)
        .reshape(2, tokens_here, columns)
    )
    start_sums = (
        jnp.zeros((tokens_here, feature_count), jnp.float32),
        jnp.zeros((all_columns, feature_count), jnp.float32),
    )
    gathered_piece = jax.tree.map(
        lambda part: lax.all_gather(part, "head", axis=1, tiled=True), as_sent(attended)
    )
    first_row = jnp.int32(0)
    weight_rows = lax.dynamic_slice_in_dim(out_weight, first_row, gathered_piece.shape[1], 0)
    output_sum = start_sums[0] + jnp.dot(
        gathered_piece, weight_rows, preferred_element_type=jnp.float32
    )
    weight_piece = lax.dot_general(
        gathered_piece, output_grad, (((0,), (0,)), ((), ())), preferred_element_type=jnp.float32
    )
    weight_sum = lax.dynamic_update_slice_in_dim(start_sums[1], weight_piece, first_row, 0)
    output_sum, weight_sum = (output_sum, weight_sum)
    weight_grad = lax.psum(weight_sum * (1.0 / math.sqrt(tokens_here * seq_count)), "seq")
    return (
        output_sum.astype(jnp.bfloat16),
        query_grad,
        own_grads[0].astype(jnp.bfloat16),
        own_grads[1].astype(jnp.bfloat16),
        weight_grad,
    )


def solution(mesh):
    placed = (
        P("seq", "head"),
        P("seq", "head"),
        P("seq", "head"),
        P(None, "head"),
        P("seq", "head"),
        P("seq", None),
        P(),
    )
    return jax.shard_map(
        shards,
        mesh=mesh,
        in_specs=placed,
        out_specs=(
            P("seq", "head"),
            P("seq", "head"),
            P("seq", "head"),
            P("seq", "head"),
            P(None, "head"),
        ),
        check_vma=False,
    )
```

profile of v0, /device:TPU:1, one launch (start us, length us, event | category | flops | bytes accessed | tf_op | source)
XLA Modules:
  0.0 1293.5 jit_solution(15211980595778835950)
XLA Ops:
  11.1 20.6 %all-to-all-start = ((s32[128,1,1]{2,1,0:T(1,128)}), s32[128,1,1]{2,1,0:T(1,128)S(1)}, u32[]{:S(2)}, u32[]{:S(2)}) async-start(s32[128,1,1]{2,1,0:T(1,128)} %copy.305), calls=%async_computation | async-start | bytes 131072 | tf_op jit(solution)/shard_map/all_to_all | solution.py:90
  31.7 1.0 pad_maximum_fusion.6
  32.7 13.8 %all-to-all-done = s32[128,1,1]{2,1,0:T(1,128)S(1)} async-done(((s32[128,1,1]{2,1,0:T(1,128)}), s32[128,1,1]{2,1,0:T(1,128)S(1)}, u32[]{:S(2)}, u32[]{:S(2)}) %all-to-all-start) | async-done | bytes 544 | tf_op jit(solution)/shard_map/all_to_all | solution.py:90
  46.5 2.4 clamp_reduce_fusion
  48.9 3.1 gather_fusion
  52.0 2.4 compare_reduce_fusion
  55.0 4.1 select_bitcast_fusion.1
  59.1 6.9 all-to-all-start.1
  66.1 3.5 collective-permute-start
  69.7 1.9 collective-permute-start.1
  71.6 1.4 fusion.62
  74.3 653.6 %all-reduce.6 = bf16[2,128,128]{1,2,0:T(8,128)(2,1)S(1)} all-reduce(f32[2,128,128]{1,2,0:T(8,128)S(1)} %convolution_bitcast_fusion.8), channel_id=1, replica_groups=mesh['seq'=128,'head'=4] {'seq'}, use_global_device_ids=true, to_apply=%region_1.0 | all-reduce | flops 32768 | bytes 196608 | tf_op jit(solution)/shard_map/psum | solution.py:74
  731.5 1.2 copy.296
  732.7 1.1 copy.295
  733.8 1.1 fusion.61
  736.2 1.0 bitcast_convert_fusion
  737.2 2.2 copy.345
  739.4 5.4 copy.306
  744.8 3.9 gather_fusion.1
  748.7 1.3 select_bitcast_fusion.2
  751.0 2.9 squeeze.35
  753.9 3.0 copy.313
  756.9 2.9 squeeze.34
  759.8 3.0 copy.307
  762.8 1.5 fusion.60
  764.8 1.1 exponential_reduce_fusion.1
  766.4 1.4 convolution_bitcast_fusion
  769.1 1.1 multiply_reduce_fusion
  771.6 1.3 fusion
  772.9 3.5 copy.333
  776.4 3.1 stack.46
  779.5 3.5 copy.335
  783.0 3.3 stack.47
  786.3 1.6 maximum_bitcast_fusion
  788.0 1.4 copy.336
  789.4 4.3 broadcast_in_dim.135
  793.8 6.0 scatter_fusion
  799.7 4.5 convert_element_type.77
  804.2 3.0 copy.337
  807.2 20.2 %all-to-all-start.2 = ((bf16[2,128,64,128]{3,2,0,1:T(8,128)(2,1)}), bf16[2,128,64,128]{3,2,0,1:T(8,128)(2,1)}, u32[]{:S(2)}, u32[]{:S(2)}) async-start(bf16[2,128,64,128]{3,2,0,1:T(8,128)(2,1)} %copy.337), calls=%async_computation.3 | async-start | bytes 8388608 | tf_op jit(solution)/shard_map/all_to_all | solution.py:277
  827.5 1.9 fusion.64
  830.0 1.1 fusion.53
  831.1 1.6 copy.331
  832.7 1.9 copy.314
  834.6 1.8 reshape.419
  836.4 1.5 multiply_convert_fusion
  838.8 1.6 copy.330
  840.4 1.2 fusion.7
  842.4 1.7 pad_maximum_fusion
  844.0 1.2 copy.327
  845.2 1.6 copy.325
  846.9 1.2 copy.326
  848.1 1.0 copy-done.11
  849.2 1.0 copy-done.12
  850.5 2.9 collective-permute-start.3
  853.4 2.7 collective-permute-start.2
  856.1 14.4 %all_gather.3 = bf16[576,512]{1,0:T(8,128)(2,1)S(1)} all-gather(bf16[576,128]{1,0:T(8,128)(2,1)S(1)} %copy-done.20), channel_id=1, replica_groups=mesh['seq'=128,'head'=4] {'head'}, dimensions={1}, use_global_device_ids=true | all-gather | bytes 737280 | tf_op jit(solution)/shard_map/all_gather | solution.py:292
  870.5 1.0 convolution_convert_fusion
  871.5 1.2 convolution_multiply_fusion.4
  877.0 381.4 %all-reduce.5.cloned.1.call-done = (f32[2,128,128]{2,1,0:T(8,128)}, f32[512,256]{1,0:T(8,128)}) async-done(((f32[2,128,128]{2,1,0:T(8,128)}, f32[512,256]{1,0:T(8,128)}), (f32[2,128,128]{2,1,0:T(8,128)}, f32[512,256]{1,0:T(8,128)})) %all-reduce.5.cloned.1.call-update) | async-done | bytes 655376 | tf_op jit(solution)/shard_map/psum | solution.py:269
  1258.5 1.3 fusion.8
  1259.8 2.7 select_bitcast_fusion
  1262.5 4.1 copy.339
  1266.7 17.6 %scatter_fusion.1 = f32[2,9,64,128]{3,2,1,0:T(8,128)S(1)} fusion(f32[2,9,64,128]{3,2,1,0:T(8,128)S(1)} %bitcast.183, s32[128]{0:T(128)S(1)} %copy-done.38, f32[128,2,64,128]{3,2,1,0:T(8,128)} %copy.339), kind=kCustom, calls=%fused_computation.4 | custom fusion | flops 2097152 | bytes 25166336 | tf_op jit(solution)/shard_map/scatter-add | solution.py:284
  (167 shorter events, 23.9 us)
Async XLA Ops:
  7.2 64.4 %copy-start = (bf16[576,256]{1,0:T(8,128)(2,1)S(1)}, bf16[576,256]{1,0:T(8,128)(2,1)}, u32[]{:S(2)}) copy-start(bf16[576,256]{1,0:T(8,128)(2,1)} %param.21) | copy-start | bytes 884740
  9.7 720.0 %copy-start.35 = (s32[27]{0:T(128)}, s32[27]{0:T(128)S(1)}, u32[]{:S(2)}) copy-start(s32[27]{0:T(128)S(1)} %fusion.48) | copy-start | bytes 328
  11.1 35.4 %all-to-all-start = ((s32[128,1,1]{2,1,0:T(1,128)}), s32[128,1,1]{2,1,0:T(1,128)S(1)}, u32[]{:S(2)}, u32[]{:S(2)}) async-start(s32[128,1,1]{2,1,0:T(1,128)} %copy.305), calls=%async_computation | async-start | bytes 131072 | tf_op jit(solution)/shard_map/all_to_all | solution.py:90
  48.8 3.2 copy-start.37
  54.4 0.6 copy-start.33
  59.1 7.0 copy-start.13
  59.1 7.0 copy-start.14
  59.1 12.5 copy-start.18
  59.1 680.3 %all-to-all-start.1 = ((bf16[2,128,64,128]{3,2,0,1:T(8,128)(2,1)}), bf16[2,128,64,128]{3,2,0,1:T(8,128)(2,1)}, u32[]{:S(2)}, u32[]{:S(2)}) async-start(bf16[2,128,64,128]{3,2,0,1:T(8,128)(2,1)} %select_bitcast_fusion.1), calls=%async_computation.1 | async-start | bytes 8388608 | tf_op jit(solution)/shard_map/all_to_all | solution.py:96
  66.0 668.9 %reduce-scatter.2.cloned.1.call-start = ((), (), s32[]{:S(2)}) async-start(), calls=%async_computation.4 | async-start | bytes 1474560 | tf_op jit(solution)/shard_map/reduce_scatter | solution.py:46
  66.1 664.4 %collective-permute-start = (bf16[2,64,128]{2,1,0:T(8,128)(2,1)S(1)}, bf16[2,64,128]{2,1,0:T(8,128)(2,1)S(1)}, u32[]{:S(2)}, u32[]{:S(2)}) collective-permute-start(bf16[2,64,128]{2,1,0:T(8,128)(2,1)S(1)} %get-tuple-element.136), channel_id=1, source_target_pairs={{0,4},{4,8},{8,12},{12,16},{16,20},{20,24},{24,28},{28,32},{32,36}... | collective-permute-start | bytes 98312 | tf_op jit(solution)/shard_map/ppermute | solution.py:21
  69.7 3.4 copy-start.41
  69.7 660.8 %collective-permute-start.1 = (bf16[2,64,128]{2,1,0:T(8,128)(2,1)S(1)}, bf16[2,64,128]{2,1,0:T(8,128)(2,1)S(1)}, u32[]{:S(2)}, u32[]{:S(2)}) collective-permute-start(bf16[2,64,128]{2,1,0:T(8,128)(2,1)S(1)} %get-tuple-element.137), channel_id=1, source_target_pairs={{4,0},{8,4},{12,8},{16,12},{20,16},{24,20},{28,24},{32,28},{36,32}... | collective-permute-start | bytes 98312 | tf_op jit(solution)/shard_map/ppermute | solution.py:23
  73.1 0.9 copy-start.31
  73.1 655.6 %copy-start.39 = (s32[128]{0:T(128)}, s32[128]{0:T(128)S(1)}, u32[]{:S(2)}) copy-start(s32[128]{0:T(128)S(1)} %broadcast_subtract_fusion) | copy-start | bytes 1540
  74.1 656.2 %copy-start.9 = (bf16[9,64,2,64]{3,2,1,0:T(2,128)(2,1)}, bf16[9,64,2,64]{3,2,1,0:T(2,128)(2,1)S(1)}, u32[]{:S(2)}) copy-start(bf16[9,64,2,64]{3,2,1,0:T(2,128)(2,1)S(1)} %squeeze.33) | copy-start | bytes 442372
  728.5 2.0 copy-start.23
  762.8 1.5 copy-start.32
  764.8 1.1 copy-start.4
  766.0 1.9 copy-start.25
  766.4 1.4 copy-start.22
  767.8 1.1 copy-start.8
  767.8 1.2 copy-start.15
  770.2 0.6 copy-start.29
  770.8 0.8 copy-start.6
  789.4 4.3 copy-start.36
  807.2 452.6 %all-to-all-start.2 = ((bf16[2,128,64,128]{3,2,0,1:T(8,128)(2,1)}), bf16[2,128,64,128]{3,2,0,1:T(8,128)(2,1)}, u32[]{:S(2)}, u32[]{:S(2)}) async-start(bf16[2,128,64,128]{3,2,0,1:T(8,128)(2,1)} %copy.337), calls=%async_computation.3 | async-start | bytes 8388608 | tf_op jit(solution)/shard_map/all_to_all | solution.py:277
  827.4 431.0 %all-reduce.5.cloned.1.call-start = ((), (), s32[]{:S(2)}) async-start(), calls=%async_computation.5 | async-start | bytes 1310720 | tf_op jit(solution)/shard_map/psum | solution.py:269
  827.5 1.9 copy-start.30
  827.5 2.5 copy-start.26
  832.7 5.2 copy-start.10
  837.9 0.9 copy-start.16
  837.9 2.5 copy-start.5
  841.6 0.8 copy-start.2
  848.1 1.1 copy-start.11
  849.2 1.1 copy-start.12
  850.2 5.9 copy-start.20
  850.2 20.3 %copy-start.19 = (bf16[512,256]{1,0:T(8,128)(2,1)S(1)}, bf16[512,256]{1,0:T(8,128)(2,1)}, u32[]{:S(2)}) copy-start(bf16[512,256]{1,0:T(8,128)(2,1)} %param.20) | copy-start | bytes 786436
  850.5 26.5 %collective-permute-start.3 = (bf16[2,64,128]{2,1,0:T(8,128)(2,1)S(1)}, bf16[2,64,128]{2,1,0:T(8,128)(2,1)S(1)}, u32[]{:S(2)}, u32[]{:S(2)}) collective-permute-start(bf16[2,64,128]{2,1,0:T(8,128)(2,1)S(1)} %slice.257), channel_id=1, source_target_pairs={{4,0},{8,4},{12,8},{16,12},{20,16},{24,20},{28,24},{32,28},{36,32}... | collective-permute-start | bytes 98312 | tf_op jit(solution)/shard_map/ppermute | solution.py:23
  853.4 23.6 %collective-permute-start.2 = (bf16[2,64,128]{2,1,0:T(8,128)(2,1)S(1)}, bf16[2,64,128]{2,1,0:T(8,128)(2,1)S(1)}, u32[]{:S(2)}, u32[]{:S(2)}) collective-permute-start(bf16[2,64,128]{2,1,0:T(8,128)(2,1)S(1)} %slice.258), channel_id=1, source_target_pairs={{0,4},{4,8},{8,12},{12,16},{16,20},{20,24},{24,28},{28,32},{32,36}... | collective-permute-start | bytes 98312 | tf_op jit(solution)/shard_map/ppermute | solution.py:21
  870.5 2.2 copy-start.3
  872.7 1.0 copy-start.17
  872.7 1.0 copy-start.24
  873.1 1.1 copy-start.1
  873.1 1.3 copy-start.7
  874.3 0.8 copy-start.27
  874.3 0.9 copy-start.28
  875.9 382.6 %copy-start.40 = (s32[128]{0:T(128)S(1)}, s32[128]{0:T(128)}, u32[]{:S(2)}) copy-start(s32[128]{0:T(128)} %copy-done.39) | copy-start | bytes 1540
  876.9 382.8 %copy-start.34 = (pred[128]{0:T(512)(128)(4,1)S(1)}, pred[128]{0:T(512)(128)(4,1)}, u32[]{:S(2)}) copy-start(pred[128]{0:T(512)(128)(4,1)} %copy-done.33) | copy-start | bytes 388
  1262.5 4.1 copy-start.38
  1284.3 1.1 copy-start.21
Sparse Core Ops, SparseCore 0:
  73.2 32.4 reduce-scatter.1
  877.1 381.3 all-reduce.4
where the time goes:
time: 1300 us; the launch traced here: 1290 us
  blocking collectives  668 us (51%)
  waiting for transfers between devices  395 us (30%)
  local copies, waits for them, and re-layouts  87.6 us (7%)
  starting transfers between devices  58.8 us (5%)
  other arithmetic  48.4 us (4%)
  matrix products  20.1 us (2%)
  between operations  15.3 us (1%)
    psum x1, blocking collectives, shards(): panel_pair = lax.psum(panel_terms, 'seq').astype(jnp.bfloat16)  654 us
    psum x1, waiting for transfers between devices, shards(): global_summed = lax.psum(global_part, 'seq')  381 us
  transfers between devices with their start and end apart: 9, of which 2 were waited for; matrix products, arithmetic and copies ran while one was open for 3% of the time, Pallas kernels for 0%

commit v1 on v0

v1 whole, which is shorter than its diff:
```python
import math

import jax
import jax.numpy as jnp
from jax import lax
from jax.experimental import pallas as pl
from jax.experimental.pallas import tpu as pltpu
from jax.sharding import Mesh
from jax.sharding import PartitionSpec as P

HEAD_DIM = 64
BLOCK = 64
PAIR = 2 * BLOCK
R = 3
GLOBALS = 128
LANES = 8
TILE = 16
VMEM_LIMIT = 40 * 1024 * 1024


def whole(space=pltpu.VMEM):
    return pl.BlockSpec(memory_space=space)


def shape(dims, dtype):
    return jax.ShapeDtypeStruct(dims, dtype)


def call(kernel, out_shape, in_specs, scratch=(), flops=0, moved=0):
    return pl.pallas_call(
        kernel,
        out_shape=out_shape,
        in_specs=in_specs,
        out_specs=jax.tree.map(lambda _: whole(), out_shape),
        scratch_shapes=list(scratch),
        compiler_params=pltpu.CompilerParams(vmem_limit_bytes=VMEM_LIMIT),
        cost_estimate=pl.CostEstimate(flops=flops, bytes_accessed=moved, transcendentals=0),
    )


def serve_kernel(where, asked, global_pos, lane_blocks, send, panel):
    me, slab = where[0], where[1]
    slabs, blocks = lane_blocks.shape[:2]
    tokens = blocks * BLOCK

    def serve(number, carry):
        to = number // slabs
        source = number % slabs
        send[to, source] = lane_blocks[source, jnp.maximum(asked[number], 0)]
        return carry

    lax.fori_loop(0, LANES * slabs, serve, 0)

    panel[...] = jnp.zeros_like(panel)
    row_number = lax.broadcasted_iota(jnp.int32, (TILE, panel.shape[1]), 0)

    def pick(number, carry):
        position = global_pos[number]
        owner = position // tokens
        row = position % tokens

        @pl.when(owner % LANES == me)
        def _():
            source, block, inside = owner // LANES, row // BLOCK, row % BLOCK
            first = pl.multiple_of(inside // TILE * TILE, TILE)
            hit = row_number == inside % TILE
            for half in range(2):
                rows = lane_blocks[source, block, pl.ds(first + half * BLOCK, TILE), :]
                line = jnp.sum(
                    jnp.where(hit, rows.astype(jnp.float32), 0.0), axis=0, keepdims=True
                )
                panel[pl.ds(number + half * GLOBALS, 1), :] = line

        return carry

    lax.fori_loop(0, GLOBALS, pick, 0)
    panel_rows = panel[...].astype(send.dtype).reshape(2, PAIR, panel.shape[1])

    def rest(to, carry):
        send[to, slabs : slabs + 2] = panel_rows
        to_right = to == (me + 1) % LANES
        source = jnp.where(
            to_right,
            jnp.where(me == LANES - 1, slab - 1, slab),
            jnp.where(me == 0, slab + 1, slab),
        )
        source = jnp.clip(source, 0, slabs - 1)
        send[to, slabs + 2] = lane_blocks[source, jnp.where(to_right, blocks - 1, 0)]
        return carry

    lax.fori_loop(0, LANES, rest, 0)


def attention_kernel(
    where,
    names,
    q,
    g,
    key,
    value,
    arrived,
    attended,
    query_grad,
    key_grad,
    value_grad,
    send,
    key_pad,
    value_pad,
    panel,
    panel_grad,
):
    me, slab = where[0], where[1]
    slabs = arrived.shape[1] - 3
    tokens, columns = q.shape
    blocks = tokens // BLOCK
    scale = 1.0 / math.sqrt(HEAD_DIM)
    f32, bf16 = jnp.float32, jnp.bfloat16
    left_lane, right_lane = (me + LANES - 1) % LANES, (me + 1) % LANES
    key_pad[:BLOCK, :] = arrived[left_lane, slabs + 2, :BLOCK, :]
    value_pad[:BLOCK, :] = arrived[left_lane, slabs + 2, BLOCK:, :]
    key_pad[BLOCK : BLOCK + tokens, :] = key[...]
    value_pad[BLOCK : BLOCK + tokens, :] = value[...]
    key_pad[BLOCK + tokens :, :] = arrived[right_lane, slabs + 2, :BLOCK, :]
    value_pad[BLOCK + tokens :, :] = arrived[right_lane, slabs + 2, BLOCK:, :]
    panel_sum = jnp.zeros((2, PAIR, columns), f32)
    for lane in range(LANES):
        panel_sum += arrived[lane, slabs : slabs + 2].astype(f32)
    panel[...] = panel_sum.astype(bf16)
    key_grad[...] = jnp.zeros_like(key_grad)
    value_grad[...] = jnp.zeros_like(value_grad)
    panel_grad[...] = jnp.zeros_like(panel_grad)
    first_block = (slab * LANES + me) * blocks
    last_block = slabs * LANES * blocks - 1
    first_head = lax.broadcasted_iota(jnp.int32, (BLOCK, columns), 1) < HEAD_DIM
    window = 3 * BLOCK
    keys = window + GLOBALS + R * BLOCK
    key_column = lax.broadcasted_iota(jnp.int32, (1, keys), 1)

    def by_head(rows):
        zero = jnp.zeros_like(rows)
        return jnp.concatenate(
            [jnp.where(first_head, rows, zero), jnp.where(first_head, zero, rows)], axis=0
        )

    def joined(pair):
        return jnp.where(first_head, pair[:BLOCK], pair[BLOCK:])

    def dot(a, b, dims):
        return lax.dot_general(a, b, (dims, ((), ())), preferred_element_type=f32)

    def one(block, carry):
        row = pl.multiple_of(block * BLOCK, BLOCK)
        here = pl.ds(row, BLOCK)
        around = pl.ds(row, window)
        owners = [names[block * R + j] // blocks for j in range(R)]
        slots = [(owner % LANES, owner // LANES) for owner in owners]
        kk = jnp.concatenate(
            [key_pad[around, :], panel[0]] + [arrived[a, b, :BLOCK, :] for a, b in slots], axis=0
        )
        vv = jnp.concatenate(
            [value_pad[around, :], panel[1]] + [arrived[a, b, BLOCK:, :] for a, b in slots], axis=0
        )
        q2 = by_head(q[here, :])
        g2 = by_head(g[here, :])
        number = first_block + block
        dead = ((key_column < BLOCK) & (number == 0)) | (
            (key_column >= 2 * BLOCK) & (key_column < window) & (number == last_block)
        )
        scores = dot(q2, kk, ((1,), (1,))) * scale
        scores = jnp.where(dead, -jnp.inf, scores)
        top = jnp.max(scores, axis=-1, keepdims=True)
        raised = jnp.exp(scores - top)
        probs = raised * (1.0 / jnp.sum(raised, axis=-1, keepdims=True))
        probs_b = probs.astype(bf16)
        att = joined(dot(probs_b, vv, ((1,), (0,)))).astype(bf16)
        attended[here, :] = att
        att_f = att.astype(f32)
        delta = jnp.sum(
            g2.astype(f32) * jnp.concatenate([att_f, att_f], axis=0), axis=-1, keepdims=True
        )
        slope = (probs * (dot(g2, vv, ((1,), (1,))) - delta)).astype(bf16)
        query_grad[here, :] = (scale * joined(dot(slope, kk, ((1,), (0,))))).astype(bf16)
        dk = scale * dot(slope, q2, ((0,), (0,)))
        dv = dot(probs_b, g2, ((0,), (0,)))
        key_grad[around, :] += dk[:window]
        value_grad[around, :] += dv[:window]
        panel_grad[0] += dk[window : window + GLOBALS]
        panel_grad[1] += dv[window : window + GLOBALS]
        for j, (a, b) in enumerate(slots):
            first = window + GLOBALS + j * BLOCK
            send[a, b, :BLOCK, :] = dk[first : first + BLOCK].astype(bf16)
            send[a, b, BLOCK:, :] = dv[first : first + BLOCK].astype(bf16)
        return carry

    lax.fori_loop(0, blocks, one, 0)
    panel_rows = panel_grad[...].astype(bf16)
    for lane in range(LANES):
        send[lane, slabs : slabs + 2] = panel_rows
    send[left_lane, slabs + 2, :BLOCK, :] = key_grad[:BLOCK, :].astype(bf16)
    send[left_lane, slabs + 2, BLOCK:, :] = value_grad[:BLOCK, :].astype(bf16)
    send[right_lane, slabs + 2, :BLOCK, :] = key_grad[BLOCK + tokens :, :].astype(bf16)
    send[right_lane, slabs + 2, BLOCK:, :] = value_grad[BLOCK + tokens :, :].astype(bf16)


def collect_kernel(where, asked, global_pos, returned, lane_grads, sums, panel):
    me, slab = where[0], where[1]
    slabs, blocks = lane_grads.shape[:2]
    tokens = blocks * BLOCK
    f32 = jnp.float32
    sums[...] = jnp.zeros_like(sums)

    def add(number, carry):
        wanted = asked[number]

        @pl.when(wanted >= 0)
        def _():
            source = number % slabs
            sums[source * blocks + wanted] += returned[number // slabs, source].astype(f32)

        return carry

    lax.fori_loop(0, LANES * slabs, add, 0)
    total = jnp.zeros((2, PAIR, panel.shape[1]), f32)
    for lane in range(LANES):
        total += returned[lane, slabs : slabs + 2].astype(f32)
    panel[...] = total.reshape(panel.shape)

    def spread(number, carry):
        position = global_pos[number]
        owner = position // tokens
        row = position % tokens

        @pl.when(owner % LANES == me)
        def _():
            to = owner // LANES * blocks + row // BLOCK
            for half in range(2):
                line = panel[pl.ds(number + half * GLOBALS, 1), :]
                sums[to, pl.ds(row % BLOCK + half * BLOCK, 1), :] += line

        return carry

    lax.fori_loop(0, GLOBALS, spread, 0)
    right_slab = jnp.where(me == LANES - 1, slab - 1, slab)
    left_slab = jnp.where(me == 0, slab + 1, slab)

    @pl.when(right_slab >= 0)
    def _():
        lane = (me + 1) % LANES
        sums[right_slab * blocks + blocks - 1] += returned[lane, slabs + 2].astype(f32)

    @pl.when(left_slab < slabs)
    def _():
        lane = (me + LANES - 1) % LANES
        sums[left_slab * blocks] += returned[lane, slabs + 2].astype(f32)

    def write(number, carry):
        lane_grads[number // blocks, number % blocks] = sums[number].astype(lane_grads.dtype)
        return carry

    lax.fori_loop(0, slabs * blocks, write, 0)


def shards(queries, key_states, value_states, out_weight, output_grad, rand_blocks, global_pos):
    bf16, f32 = jnp.bfloat16, jnp.float32
    tokens, columns = queries.shape
    blocks = tokens // BLOCK
    slabs = lax.axis_size("slab")
    slab, me = lax.axis_index("slab"), lax.axis_index("lane")
    smem, vmem = whole(pltpu.SMEM), whole()
    where = jnp.stack([me, slab]).astype(jnp.int32)
    slots = slabs + 3

    names = rand_blocks.reshape(-1)
    owner = names // blocks
    index = jnp.arange(LANES)[:, None] + LANES * jnp.arange(slabs)[None, :]
    hit = owner[None, None, :] == index[:, :, None]
    wanted = jnp.max(jnp.where(hit, (names % blocks)[None, None, :], -1), axis=-1)
    asked = lax.all_to_all(wanted, "lane", split_axis=0, concat_axis=0, tiled=True).reshape(-1)

    own = jnp.concatenate(
        [key_states.reshape(blocks, BLOCK, columns), value_states.reshape(blocks, BLOCK, columns)],
        axis=1,
    )
    lane_blocks = lax.all_gather(own, "slab", axis=0, tiled=False)

    lane_blocks, late_grad = lax.optimization_barrier((lane_blocks, output_grad))
    partial_grad = lax.dot_general(
        late_grad, out_weight, (((1,), (1,)), ((), ())), preferred_element_type=f32
    )
    grad_att = lax.psum_scatter(partial_grad, "head", scatter_dimension=1, tiled=True).astype(bf16)

    served = call(
        serve_kernel,
        shape((LANES, slots, PAIR, columns), bf16),
        [smem, smem, smem, vmem],
        [pltpu.VMEM((2 * GLOBALS, columns), f32)],
        moved=10 << 20,
    )(where, asked, global_pos, lane_blocks)
    arrived = lax.all_to_all(served, "lane", split_axis=0, concat_axis=0, tiled=True)

    padded = tokens + PAIR
    attended, query_grad, key_part, value_part, sent = call(
        attention_kernel,
        (
            shape((tokens, columns), bf16),
            shape((tokens, columns), bf16),
            shape((padded, columns), f32),
            shape((padded, columns), f32),
            shape((LANES, slots, PAIR, columns), bf16),
        ),
        [smem, smem] + [vmem] * 5,
        [
            pltpu.VMEM((padded, columns), bf16),
            pltpu.VMEM((padded, columns), bf16),
            pltpu.VMEM((2, GLOBALS, columns), bf16),
            pltpu.VMEM((2, GLOBALS, columns), f32),
        ],
        flops=1 << 30,
        moved=12 << 20,
    )(where, names, queries, grad_att, key_states, value_states, arrived)
    returned = lax.all_to_all(sent, "lane", split_axis=0, concat_axis=0, tiled=True)

    everywhere = lax.all_gather(attended, "head", axis=1, tiled=True)
    projected = jnp.dot(everywhere, out_weight, preferred_element_type=f32).astype(bf16)
    weight_part = lax.dot_general(
        everywhere, output_grad, (((0,), (0,)), ((), ())), preferred_element_type=f32
    ) * (1.0 / math.sqrt(tokens * slabs * LANES))
    features = weight_part.shape[1]
    weight_part = weight_part.reshape(slabs, LANES, -1, features).transpose(1, 0, 2, 3)
    weight_part = lax.all_to_all(weight_part, "lane", split_axis=0, concat_axis=0, tiled=True)
    weight_part = jnp.sum(weight_part, axis=0)
    weight_part = lax.all_to_all(weight_part, "slab", split_axis=0, concat_axis=0, tiled=True)
    weight_part = jnp.sum(weight_part, axis=0)
    weight_grad = lax.all_gather(weight_part, ("slab", "lane"), axis=0, tiled=True)

    lane_grads = call(
        collect_kernel,
        shape((slabs, blocks, PAIR, columns), bf16),
        [smem, smem, smem, vmem],
        [
            pltpu.VMEM((slabs * blocks, PAIR, columns), f32),
            pltpu.VMEM((2 * GLOBALS, columns), f32),
        ],
        moved=10 << 20,
    )(where, asked, global_pos, returned)
    others = lax.psum_scatter(lane_grads, "slab", scatter_dimension=0, tiled=False).astype(f32)
    key_grad = key_part[BLOCK:-BLOCK] + others[:, :BLOCK].reshape(tokens, columns)
    value_grad = value_part[BLOCK:-BLOCK] + others[:, BLOCK:].reshape(tokens, columns)
    return projected, query_grad, key_grad.astype(bf16), value_grad.astype(bf16), weight_grad


def solution(mesh):
    seq_count, head_count = mesh.devices.shape
    fine = Mesh(
        mesh.devices.reshape(seq_count // LANES, LANES, head_count), ("slab", "lane", "head")
    )
    seq = ("slab", "lane")
    placed = (
        P(seq, "head"),
        P(seq, "head"),
        P(seq, "head"),
        P(None, "head"),
        P(seq, "head"),
        P(seq, None),
        P(),
    )
    return jax.shard_map(
        shards,
        mesh=fine,
        in_specs=placed,
        out_specs=(
            P(seq, "head"),
            P(seq, "head"),
            P(seq, "head"),
            P(seq, "head"),
            P(None, "head"),
        ),
        check_vma=False,
    )
```

time: 1300 us -> 396 us (0.30)
  blocking collectives: 668 us -> 173 us
  waiting for transfers between devices: 395 us -> 132 us
  local copies, waits for them, and re-layouts: 87.6 us -> 10 us
  other arithmetic: 48.4 us -> 6.89 us
  starting transfers between devices: 58.8 us -> 30.1 us
  Pallas kernels: 0 us -> 27 us
  matrix products: 20.1 us -> 2.8 us
    psum x1 -> x0, blocking collectives: 654 us -> none  [shards(): panel_pair = lax.psum(panel_terms, 'seq').astype(jnp.bfloat16)]
    psum x1 -> x0, waiting for transfers between devices: 381 us -> none  [shards(): global_summed = lax.psum(global_part, 'seq')]
    all_gather x1 -> x2, blocking collectives: 14.4 us -> 96.4 us  [the longest x1 83.8 us: shards(): lax.all_gather(weight_part, ('slab', 'lane'), axis=0, tiled=True)]
    all_to_all x0 -> x2, blocking collectives: none -> 76.1 us  [the longest x1 61.3 us: shards(): lax.all_to_all(sent, 'lane', split_axis=0, concat_axis=0, tiled=True)]
    all_gather x0 -> x1, waiting for transfers between devices: none -> 61.5 us  [shards(): lane_blocks = lax.all_gather(own, 'slab', axis=0, tiled=False)]
    all_to_all x3, waiting for transfers between devices: 13.8 us -> 42.3 us  [the longest x1 26.7 us: shards(): lax.all_to_all(served, 'lane', split_axis=0, concat_axis=0, tiled=True)]
    reduce_scatter x1, waiting for transfers between devices: 0.01 us -> 28.2 us  [shards(): lax.psum_scatter(partial_grad, 'head', scatter_dimension=1, tiled=True)]
    pallas_call x0 -> x3, Pallas kernels: none -> 27 us  [the longest x1 10.9 us: shards(): call(attention_kernel, (shape((tokens, columns), bf16), shape((tokens, co...]
  transfers between devices with their start and end apart: 9 -> 6, of which waited for: 2 -> 5; matrix products, arithmetic and copies ran while one was open for 3% -> 2% of each run, Pallas kernels for 0% -> 0%
where the time goes in v1:
time: 396 us; the launch traced here: 395 us
  blocking collectives  173 us (44%)
  waiting for transfers between devices  132 us (33%)
  starting transfers between devices  30.1 us (8%)
  Pallas kernels  27 us (7%)
  between operations  13.9 us (4%)
  local copies, waits for them, and re-layouts  10 us (3%)
  other arithmetic  6.89 us (2%)
    all_gather x1, blocking collectives, shards(): lax.all_gather(weight_part, ('slab', 'lane'), axis=0, tiled=True)  83.8 us
    all_gather x1, waiting for transfers between devices, shards(): lane_blocks = lax.all_gather(own, 'slab', axis=0, tiled=False)  61.5 us
    all_to_all x1, blocking collectives, shards(): lax.all_to_all(sent, 'lane', split_axis=0, concat_axis=0, tiled=True)  61.3 us
    reduce_scatter x1, waiting for transfers between devices, shards(): lax.psum_scatter(partial_grad, 'head', scatter_dimension=1, tiled=True)  28.2 us
    all_to_all x1, waiting for transfers between devices, shards(): lax.all_to_all(served, 'lane', split_axis=0, concat_axis=0, tiled=True)  26.7 us
    all_to_all x1, blocking collectives, shards(): lax.all_to_all(weight_part, 'lane', split_axis=0, concat_axis=0, tiled=True)  14.8 us
    all_to_all x1, starting transfers between devices, shards(): lax.all_to_all(served, 'lane', split_axis=0, concat_axis=0, tiled=True)  13.1 us
    all_gather x1, blocking collectives, shards(): everywhere = lax.all_gather(attended, 'head', axis=1, tiled=True)  12.6 us
  transfers between devices with their start and end apart: 6, of which 5 were waited for; matrix products, arithmetic and copies ran while one was open for 2% of the time, Pallas kernels for 0%

profile of v1, /device:TPU:1, one launch (start us, length us, event | category | flops | bytes accessed | tf_op | source)
XLA Modules:
  0.0 395.2 jit_solution(9439660717531910595)
XLA Ops:
  7.2 0.0 copy-start
  7.2 0.0 all-gather.4.cloned.1.call-start
  7.2 1.8 pad_maximum_fusion
  9.0 0.0 all-gather.4.cloned.1.call-update
  9.0 0.8 copy.20
  9.8 0.1 reshape.85.names
  9.9 0.9 select_reduce_fusion
  10.8 10.1 %all-to-all-start = ((s32[8,1,16]{2,1,0:T(1,128)}), s32[8,1,16]{2,1,0:T(1,128)S(1)}, u32[]{:S(2)}, u32[]{:S(2)}) async-start(s32[8,1,16]{2,1,0:T(1,128)} %bitcast.6), calls=%async_computation.1 | async-start | bytes 8192 | tf_op jit(solution)/shard_map/all_to_all | solution.py:278
  20.9 0.1 pad_add_fusion.where
  20.9 4.4 %all-to-all-done = s32[8,1,16]{2,1,0:T(1,128)S(1)} async-done(((s32[8,1,16]{2,1,0:T(1,128)}), s32[8,1,16]{2,1,0:T(1,128)S(1)}, u32[]{:S(2)}, u32[]{:S(2)}) %all-to-all-start) | async-done | bytes 544 | tf_op jit(solution)/shard_map/all_to_all | solution.py:278
  25.4 0.5 broadcast.64
  25.9 0.7 reduce.3
  26.6 0.1 reshape.88.asked
  26.6 61.5 %all-gather.4.cloned.1.call-done = bf16[144,128,128]{2,1,0:T(8,128)(2,1)} async-done(((bf16[9,128,128]{2,1,0:T(8,128)(2,1)}), bf16[144,128,128]{2,1,0:T(8,128)(2,1)}) %all-gather.4.cloned.1.call-update) | async-done | bytes 4718608 | tf_op jit(solution)/shard_map/all_gather | solution.py:284
  88.1 0.0 copy-start.3
  88.1 2.3 copy-done.3
  90.5 0.0 copy-start.7
  90.5 0.7 copy-done.7
  91.1 6.6 %shard_map.110 = bf16[8,19,128,128]{3,2,1,0:T(8,128)(2,1)S(1)} custom-call(s32[2]{0:T(128)S(1)} %pad_add_fusion.where, s32[128]{0:T(128)S(1)} %reshape.88.asked, s32[128]{0:T(128)S(1)} %copy-done.7, bf16[16,9,128,128]{3,2,1,0:T(8,128)(2,1)S(1)} %bitcast.29), custom_call_target="tpu_custom_call" | custom-call | bytes 10485760 | tf_op jit(solution)/shard_map/pallas_call | solution.py:292
  97.7 0.0 copy-start.1
  97.7 2.2 copy-done.1
  99.9 0.0 copy-start.9
  99.9 0.0 copy-start.4
  99.9 0.0 copy-start.5
  99.9 0.0 copy-start.6
  99.9 13.1 %all-to-all-start.1 = ((bf16[8,19,128,128]{3,2,1,0:T(8,128)(2,1)}), bf16[8,19,128,128]{3,2,1,0:T(8,128)(2,1)}, u32[]{:S(2)}, u32[]{:S(2)}) async-start(bf16[8,19,128,128]{3,2,1,0:T(8,128)(2,1)} %copy-done.1), calls=%async_computation.2 | async-start | bytes 9961472 | tf_op jit(solution)/shard_map/all_to_all | solution.py:299
  113.0 0.0 reduce-scatter.3.cloned.1.call-start
  113.0 0.0 copy-done
  113.1 0.0 copy-done.9
  113.1 1.4 fusion.3
  114.4 0.0 reduce-scatter.3.cloned.1.call-update
  114.5 0.0 reduce-scatter.5.cloned.1.call-start
  114.5 28.2 %reduce-scatter.3.cloned.1.call-done = f32[576,128]{1,0:T(8,128)} async-done(((f32[576,512]{1,0:T(8,128)}), f32[576,128]{1,0:T(8,128)}) %reduce-scatter.3.cloned.1.call-update) | async-done | bytes 294928 | tf_op jit(solution)/shard_map/reduce_scatter | solution.py:290
  142.7 1.0 convert_element_type.18.g
  143.7 26.7 %all-to-all-done.1.arrived = bf16[8,19,128,128]{3,2,1,0:T(8,128)(2,1)} async-done(((bf16[8,19,128,128]{3,2,1,0:T(8,128)(2,1)}), bf16[8,19,128,128]{3,2,1,0:T(8,128)(2,1)}, u32[]{:S(2)}, u32[]{:S(2)}) %all-to-all-start.1) | async-done | bytes 4980768 | tf_op jit(solution)/shard_map/all_to_all | solution.py:299
  170.4 0.0 copy-done.4
  170.4 0.0 copy-done.5
  170.4 0.0 copy-done.6
  170.4 10.9 %shard_map.111 = (bf16[576,128]{1,0:T(8,128)(2,1)S(1)}, bf16[576,128]{1,0:T(8,128)(2,1)}, f32[704,128]{1,0:T(8,128)S(1)}, f32[704,128]{1,0:T(8,128)S(1)}, bf16[8,19,128,128]{3,2,1,0:T(8,128)(2,1)S(1)}) custom-call(s32[2]{0:T(128)S(1)} %pad_add_fusion.where, s32[27]{0:T(128)S(1)} %reshape.85.names, bf16[576,128]{1,0:T(8,128)(2,1)S(1)} %copy-done.6, ...), custom_call_target="tpu_custom_call" | custom-call | flops 1073741824 | bytes 12582912 | tf_op jit(solution)/shard_map/pallas_call | solution.py:302
  181.3 0.0 copy-start.8
  181.3 61.3 %all_to_all.29.returned = bf16[8,19,128,128]{3,2,1,0:T(8,128)(2,1)S(1)} all-to-all(bf16[8,19,128,128]{3,2,1,0:T(8,128)(2,1)S(1)} %get-tuple-element.17), channel_id=1, replica_groups=mesh['slab'=16,'lane'=8,'head'=4] {'lane'}, dimensions={0} | all-to-all | bytes 9961472 | tf_op jit(solution)/shard_map/all_to_all | solution.py:321
  242.7 0.0 copy-done.8
  242.7 9.5 %shard_map.112 = bf16[16,9,128,128]{3,2,1,0:T(8,128)(2,1)S(1)} custom-call(s32[2]{0:T(128)S(1)} %pad_add_fusion.where, s32[128]{0:T(128)S(1)} %reshape.88.asked, s32[128]{0:T(128)S(1)} %copy-done.8, bf16[8,19,128,128]{3,2,1,0:T(8,128)(2,1)S(1)} %all_to_all.29.returned), custom_call_target="tpu_custom_call" | custom-call | bytes 10485760 | tf_op jit(solution)/shard_map/pallas_call | solution.py:336
  252.2 0.0 copy-start.2
  252.2 2.1 copy-done.2
  254.3 0.0 reduce-scatter.5.cloned.1.call-update
  254.4 12.6 %all_gather.14 = bf16[576,512]{1,0:T(8,128)(2,1)S(1)} all-gather(bf16[576,128]{1,0:T(8,128)(2,1)S(1)} %get-tuple-element.14), channel_id=1, replica_groups=mesh['slab'=16,'lane'=8,'head'=4] {'head'}, dimensions={1}, use_global_device_ids=true | all-gather | bytes 737280 | tf_op jit(solution)/shard_map/all_gather | solution.py:323
  267.0 0.4 convolution_multiply_fusion
  267.4 0.1 reshape.91
  267.6 14.8 %all_to_all.30 = f32[8,16,4,256]{3,2,1,0:T(4,128)S(1)} all-to-all(f32[8,16,4,256]{3,2,1,0:T(4,128)S(1)} %bitcast.32), channel_id=1, replica_groups=mesh['slab'=16,'lane'=8,'head'=4] {'lane'}, dimensions={0} | all-to-all | bytes 1048576 | tf_op jit(solution)/shard_map/all_to_all | solution.py:330
  282.4 0.7 reduce_sum.18
  283.1 6.8 %all-to-all-start.4 = ((f32[16,4,256]{2,1,0:T(4,128)}), f32[16,4,256]{2,1,0:T(4,128)S(1)}, u32[]{:S(2)}, u32[]{:S(2)}) async-start(f32[16,4,256]{2,1,0:T(4,128)} %reduce_sum.18), calls=%async_computation.6 | async-start | bytes 131072 | tf_op jit(solution)/shard_map/all_to_all | solution.py:332
  289.9 1.0 convolution_convert_fusion
  291.0 11.1 %all-to-all-done.4 = f32[16,4,256]{2,1,0:T(4,128)S(1)} async-done(((f32[16,4,256]{2,1,0:T(4,128)}), f32[16,4,256]{2,1,0:T(4,128)S(1)}, u32[]{:S(2)}, u32[]{:S(2)}) %all-to-all-start.4) | async-done | bytes 65568 | tf_op jit(solution)/shard_map/all_to_all | solution.py:332
  302.1 83.8 %all-gather.1 = f32[128,4,256]{2,1,0:T(4,128)S(1)} all-gather(f32[1,4,256]{2,1,0:T(4,128)S(1)} %bitcast.33), channel_id=1, replica_groups=mesh['slab'=16,'lane'=8,'head'=4] {'slab','lane'}, dimensions={0}, use_global_device_ids=true | all-gather | bytes 528384 | tf_op jit(solution)/shard_map/all_gather | solution.py:334
  385.9 1.0 reshape.95
  386.9 0.0 reduce-scatter.5.cloned.1.call-done
  386.9 1.0 bitcast_convert_fusion
  387.9 0.8 fusion
  (6 shorter events, 0.1 us)
Async XLA Ops:
  7.2 105.9 %copy-start = (bf16[576,256]{1,0:T(8,128)(2,1)S(1)}, bf16[576,256]{1,0:T(8,128)(2,1)}, u32[]{:S(2)}) copy-start(bf16[576,256]{1,0:T(8,128)(2,1)} %param.11) | copy-start | bytes 884740
  7.2 81.0 %all-gather.4.cloned.1.call-start = ((), (), s32[]{:S(2)}) async-start(), calls=%async_computation.9 | async-start | bytes 5013504 | tf_op jit(solution)/shard_map/all_gather | solution.py:284
  10.8 14.6 %all-to-all-start = ((s32[8,1,16]{2,1,0:T(1,128)}), s32[8,1,16]{2,1,0:T(1,128)S(1)}, u32[]{:S(2)}, u32[]{:S(2)}) async-start(s32[8,1,16]{2,1,0:T(1,128)} %bitcast.6), calls=%async_computation.1 | async-start | bytes 8192 | tf_op jit(solution)/shard_map/all_to_all | solution.py:278
  88.1 2.3 copy-start.3
  90.5 0.7 copy-start.7
  97.7 2.2 copy-start.1
  99.9 13.1 %copy-start.9 = (bf16[512,256]{1,0:T(8,128)(2,1)S(1)}, bf16[512,256]{1,0:T(8,128)(2,1)}, u32[]{:S(2)}) copy-start(bf16[512,256]{1,0:T(8,128)(2,1)} %param.10) | copy-start | bytes 786436
  99.9 70.5 %copy-start.4 = (bf16[576,128]{1,0:T(8,128)(2,1)S(1)}, bf16[576,128]{1,0:T(8,128)(2,1)}, u32[]{:S(2)}) copy-start(bf16[576,128]{1,0:T(8,128)(2,1)} %value.1) | copy-start | bytes 442372
  99.9 70.5 %copy-start.5 = (bf16[576,128]{1,0:T(8,128)(2,1)S(1)}, bf16[576,128]{1,0:T(8,128)(2,1)}, u32[]{:S(2)}) copy-start(bf16[576,128]{1,0:T(8,128)(2,1)} %key.1) | copy-start | bytes 442372
  99.9 70.5 %copy-start.6 = (bf16[576,128]{1,0:T(8,128)(2,1)S(1)}, bf16[576,128]{1,0:T(8,128)(2,1)}, u32[]{:S(2)}) copy-start(bf16[576,128]{1,0:T(8,128)(2,1)} %q.1) | copy-start | bytes 442372
  99.9 70.5 %all-to-all-start.1 = ((bf16[8,19,128,128]{3,2,1,0:T(8,128)(2,1)}), bf16[8,19,128,128]{3,2,1,0:T(8,128)(2,1)}, u32[]{:S(2)}, u32[]{:S(2)}) async-start(bf16[8,19,128,128]{3,2,1,0:T(8,128)(2,1)} %copy-done.1), calls=%async_computation.2 | async-start | bytes 9961472 | tf_op jit(solution)/shard_map/all_to_all | solution.py:299
  113.0 29.7 %reduce-scatter.3.cloned.1.call-start = ((), (), s32[]{:S(2)}) async-start(), calls=%async_computation.7 | async-start | bytes 1474560 | tf_op jit(solution)/shard_map/reduce_scatter | solution.py:290
  114.5 272.4 %reduce-scatter.5.cloned.1.call-start = ((), (), s32[]{:S(2)}) async-start(), calls=%async_computation.8 | async-start | bytes 5013504 | tf_op jit(solution)/shard_map/reduce_scatter | solution.py:346
  181.3 61.3 %copy-start.8 = (s32[128]{0:T(128)S(1)}, s32[128]{0:T(128)}, u32[]{:S(2)}) copy-start(s32[128]{0:T(128)} %global_pos.3) | copy-start | bytes 1540
  252.2 2.1 copy-start.2
  283.1 19.0 %all-to-all-start.4 = ((f32[16,4,256]{2,1,0:T(4,128)}), f32[16,4,256]{2,1,0:T(4,128)S(1)}, u32[]{:S(2)}, u32[]{:S(2)}) async-start(f32[16,4,256]{2,1,0:T(4,128)} %reduce_sum.18), calls=%async_computation.6 | async-start | bytes 131072 | tf_op jit(solution)/shard_map/all_to_all | solution.py:332
Sparse Core Ops, SparseCore 0:
  10.7 77.4 all-gather.3
  116.7 25.9 reduce-scatter.2
  254.5 69.0 reduce-scatter.4

commit v2 on v1

v2 whole, which is shorter than its diff:
```python
import math

import jax
import jax.numpy as jnp
from jax import lax
from jax.experimental import pallas as pl
from jax.experimental.pallas import tpu as pltpu
from jax.sharding import Mesh
from jax.sharding import PartitionSpec as P

HEAD_DIM = 64
GLOBALS = 128
BLOCK = 64
EXTRA = GLOBALS // BLOCK + 1
R = 3
LANES = 8
TILE = 16
VMEM_LIMIT = 40 * 1024 * 1024


def whole(space=pltpu.VMEM):
    return pl.BlockSpec(memory_space=space)


def shape(dims, dtype):
    return jax.ShapeDtypeStruct(dims, dtype)


def call(kernel, out_shape, in_specs, scratch=(), flops=0, moved=0):
    return pl.pallas_call(
        kernel,
        out_shape=out_shape,
        in_specs=in_specs,
        out_specs=jax.tree.map(lambda _: whole(), out_shape),
        scratch_shapes=list(scratch),
        compiler_params=pltpu.CompilerParams(vmem_limit_bytes=VMEM_LIMIT),
        cost_estimate=pl.CostEstimate(flops=flops, bytes_accessed=moved, transcendentals=0),
    )


def serve_kernel(where, asked, global_pos, lane_blocks, send, panel):
    me, slab = where[0], where[1]
    slabs, blocks = lane_blocks.shape[:2]
    columns = panel.shape[1]
    tokens = blocks * BLOCK

    def serve(number, carry):
        source = number % slabs
        send[number // slabs, source] = lane_blocks[source, jnp.maximum(asked[number], 0)]
        return carry

    lax.fori_loop(0, LANES * slabs, serve, 0)

    panel[...] = jnp.zeros_like(panel)
    row_number = lax.broadcasted_iota(jnp.int32, (TILE, columns), 0)

    def pick(number, carry):
        position = global_pos[number]
        owner = position // tokens
        row = position % tokens

        @pl.when(owner % LANES == me)
        def _():
            inside = row % BLOCK
            first = pl.multiple_of(inside // TILE * TILE, TILE)
            rows = lane_blocks[owner // LANES, row // BLOCK, pl.ds(first, TILE), :]
            hit = row_number == inside % TILE
            panel[pl.ds(number, 1), :] = jnp.sum(
                jnp.where(hit, rows.astype(jnp.float32), 0.0), axis=0, keepdims=True
            )

        return carry

    lax.fori_loop(0, GLOBALS, pick, 0)
    panel_rows = panel[...].astype(send.dtype).reshape(EXTRA - 1, BLOCK, columns)

    def rest(to, carry):
        send[to, slabs : slabs + EXTRA - 1] = panel_rows
        to_right = to == (me + 1) % LANES
        source = jnp.where(
            to_right,
            jnp.where(me == LANES - 1, slab - 1, slab),
            jnp.where(me == 0, slab + 1, slab),
        )
        source = jnp.clip(source, 0, slabs - 1)
        send[to, slabs + EXTRA - 1] = lane_blocks[source, jnp.where(to_right, blocks - 1, 0)]
        return carry

    lax.fori_loop(0, LANES, rest, 0)


def attention_kernel(
    where,
    names,
    q,
    g,
    key,
    value,
    keys_arrived,
    values_arrived,
    attended,
    query_grad,
    key_grad,
    value_grad,
    send_keys,
    send_values,
    key_pad,
    value_pad,
    panel,
    panel_grad,
):
    me, slab = where[0], where[1]
    slabs = keys_arrived.shape[1] - EXTRA
    edge = slabs + EXTRA - 1
    tokens, columns = q.shape
    blocks = tokens // BLOCK
    scale = 1.0 / math.sqrt(HEAD_DIM)
    f32, bf16 = jnp.float32, jnp.bfloat16
    left_lane, right_lane = (me + LANES - 1) % LANES, (me + 1) % LANES
    key_pad[:BLOCK, :] = keys_arrived[left_lane, edge]
    value_pad[:BLOCK, :] = values_arrived[left_lane, edge]
    key_pad[BLOCK : BLOCK + tokens, :] = key[...]
    value_pad[BLOCK : BLOCK + tokens, :] = value[...]
    key_pad[BLOCK + tokens :, :] = keys_arrived[right_lane, edge]
    value_pad[BLOCK + tokens :, :] = values_arrived[right_lane, edge]
    for half, arrived in enumerate((keys_arrived, values_arrived)):
        panel_sum = jnp.zeros((EXTRA - 1, BLOCK, columns), f32)
        for lane in range(LANES):
            panel_sum += arrived[lane, slabs:edge].astype(f32)
        panel[half] = panel_sum.reshape(GLOBALS, columns).astype(bf16)
    key_grad[...] = jnp.zeros_like(key_grad)
    value_grad[...] = jnp.zeros_like(value_grad)
    panel_grad[...] = jnp.zeros_like(panel_grad)
    first_block = (slab * LANES + me) * blocks
    last_block = slabs * LANES * blocks - 1
    first_head = lax.broadcasted_iota(jnp.int32, (BLOCK, columns), 1) < HEAD_DIM
    window = 3 * BLOCK
    keys = window + GLOBALS + R * BLOCK
    key_column = lax.broadcasted_iota(jnp.int32, (1, keys), 1)

    def by_head(rows):
        zero = jnp.zeros_like(rows)
        return jnp.concatenate(
            [jnp.where(first_head, rows, zero), jnp.where(first_head, zero, rows)], axis=0
        )

    def joined(pair):
        return jnp.where(first_head, pair[:BLOCK], pair[BLOCK:])

    def dot(a, b, dims):
        return lax.dot_general(a, b, (dims, ((), ())), preferred_element_type=f32)

    def one(block, carry):
        row = pl.multiple_of(block * BLOCK, BLOCK)
        here = pl.ds(row, BLOCK)
        around = pl.ds(row, window)
        owners = [names[block * R + j] // blocks for j in range(R)]
        slots = [(owner % LANES, owner // LANES) for owner in owners]
        kk = jnp.concatenate(
            [key_pad[around, :], panel[0]] + [keys_arrived[a, b] for a, b in slots], axis=0
        )
        vv = jnp.concatenate(
            [value_pad[around, :], panel[1]] + [values_arrived[a, b] for a, b in slots], axis=0
        )
        q2 = by_head(q[here, :])
        g2 = by_head(g[here, :])
        number = first_block + block
        dead = ((key_column < BLOCK) & (number == 0)) | (
            (key_column >= 2 * BLOCK) & (key_column < window) & (number == last_block)
        )
        scores = dot(q2, kk, ((1,), (1,))) * scale
        scores = jnp.where(dead, -jnp.inf, scores)
        top = jnp.max(scores, axis=-1, keepdims=True)
        raised = jnp.exp(scores - top)
        probs = raised * (1.0 / jnp.sum(raised, axis=-1, keepdims=True))
        probs_b = probs.astype(bf16)
        att = joined(dot(probs_b, vv, ((1,), (0,)))).astype(bf16)
        attended[here, :] = att
        att_f = att.astype(f32)
        delta = jnp.sum(
            g2.astype(f32) * jnp.concatenate([att_f, att_f], axis=0), axis=-1, keepdims=True
        )
        slope = (probs * (dot(g2, vv, ((1,), (1,))) - delta)).astype(bf16)
        query_grad[here, :] = (scale * joined(dot(slope, kk, ((1,), (0,))))).astype(bf16)
        dk = scale * dot(slope, q2, ((0,), (0,)))
        dv = dot(probs_b, g2, ((0,), (0,)))
        key_grad[around, :] += dk[:window]
        value_grad[around, :] += dv[:window]
        panel_grad[0] += dk[window : window + GLOBALS]
        panel_grad[1] += dv[window : window + GLOBALS]
        for j, (a, b) in enumerate(slots):
            first = window + GLOBALS + j * BLOCK
            send_keys[a, b] = dk[first : first + BLOCK].astype(bf16)
            send_values[a, b] = dv[first : first + BLOCK].astype(bf16)
        return carry

    lax.fori_loop(0, blocks, one, 0)
    for half, (send, grad) in enumerate(((send_keys, key_grad), (send_values, value_grad))):
        panel_rows = panel_grad[half].astype(bf16).reshape(EXTRA - 1, BLOCK, columns)
        for lane in range(LANES):
            send[lane, slabs:edge] = panel_rows
        send[left_lane, edge] = grad[:BLOCK, :].astype(bf16)
        send[right_lane, edge] = grad[BLOCK + tokens :, :].astype(bf16)


def collect_kernel(where, asked, global_pos, returned, lane_grads, sums, panel):
    me, slab = where[0], where[1]
    slabs, blocks = lane_grads.shape[:2]
    tokens = blocks * BLOCK
    f32 = jnp.float32
    sums[...] = jnp.zeros_like(sums)

    def add(number, carry):
        wanted = asked[number]

        @pl.when(wanted >= 0)
        def _():
            source = number % slabs
            sums[source * blocks + wanted] += returned[number // slabs, source].astype(f32)

        return carry

    lax.fori_loop(0, LANES * slabs, add, 0)
    edge = slabs + EXTRA - 1
    total = jnp.zeros((EXTRA - 1, BLOCK, panel.shape[1]), f32)
    for lane in range(LANES):
        total += returned[lane, slabs:edge].astype(f32)
    panel[...] = total.reshape(panel.shape)

    def spread(number, carry):
        position = global_pos[number]
        owner = position // tokens
        row = position % tokens

        @pl.when(owner % LANES == me)
        def _():
            to = owner // LANES * blocks + row // BLOCK
            sums[to, pl.ds(row % BLOCK, 1), :] += panel[pl.ds(number, 1), :]

        return carry

    lax.fori_loop(0, GLOBALS, spread, 0)
    right_slab = jnp.where(me == LANES - 1, slab - 1, slab)
    left_slab = jnp.where(me == 0, slab + 1, slab)

    @pl.when(right_slab >= 0)
    def _():
        lane = (me + 1) % LANES
        sums[right_slab * blocks + blocks - 1] += returned[lane, edge].astype(f32)

    @pl.when(left_slab < slabs)
    def _():
        lane = (me + LANES - 1) % LANES
        sums[left_slab * blocks] += returned[lane, edge].astype(f32)

    def write(number, carry):
        lane_grads[number // blocks, number % blocks] = sums[number].astype(lane_grads.dtype)
        return carry

    lax.fori_loop(0, slabs * blocks, write, 0)


def shards(queries, key_states, value_states, out_weight, output_grad, rand_blocks, global_pos):
    bf16, f32 = jnp.bfloat16, jnp.float32
    tokens, columns = queries.shape
    blocks = tokens // BLOCK
    slabs, heads = lax.axis_size("slab"), lax.axis_size("head")
    slab, me, head = lax.axis_index("slab"), lax.axis_index("lane"), lax.axis_index("head")
    smem, vmem = whole(pltpu.SMEM), whole()
    where = jnp.stack([me, slab]).astype(jnp.int32)
    slots = slabs + EXTRA
    run = (blocks, BLOCK, columns)

    lane_keys = lax.all_gather(key_states.reshape(run), "slab", axis=0, tiled=False)

    names = rand_blocks.reshape(-1)
    owner = names // blocks
    index = jnp.arange(LANES)[:, None] + LANES * jnp.arange(slabs)[None, :]
    hit = owner[None, None, :] == index[:, :, None]
    wanted = jnp.max(jnp.where(hit, (names % blocks)[None, None, :], -1), axis=-1)
    late_values, wanted = lax.optimization_barrier((value_states, wanted))
    lane_values = lax.all_gather(late_values.reshape(run), "slab", axis=0, tiled=False)
    asked = lax.all_to_all(wanted, "lane", split_axis=0, concat_axis=0, tiled=True).reshape(-1)

    partial_grad = lax.dot_general(
        output_grad, out_weight, (((1,), (1,)), ((), ())), preferred_element_type=f32
    )
    partial_grad = partial_grad.reshape(tokens, heads, columns).transpose(1, 0, 2)
    partial_grad = lax.all_to_all(partial_grad, "head", split_axis=0, concat_axis=0, tiled=True)
    grad_att = jnp.sum(partial_grad, axis=0).astype(bf16)
    lane_keys, grad_att, asked = lax.optimization_barrier((lane_keys, grad_att, asked))

    def serve(lane_blocks):
        served = call(
            serve_kernel,
            shape((LANES, slots, BLOCK, columns), bf16),
            [smem, smem, smem, vmem],
            [pltpu.VMEM((GLOBALS, columns), f32)],
            moved=5 << 20,
        )(where, asked, global_pos, lane_blocks)
        return lax.all_to_all(served, "lane", split_axis=0, concat_axis=0, tiled=True)

    keys_arrived = serve(lane_keys)
    lane_values, keys_arrived = lax.optimization_barrier((lane_values, keys_arrived))
    values_arrived = serve(lane_values)

    padded = tokens + 2 * BLOCK
    attended, query_grad, key_part, value_part, keys_sent, values_sent = call(
        attention_kernel,
        (
            shape((tokens, columns), bf16),
            shape((tokens, columns), bf16),
            shape((padded, columns), f32),
            shape((padded, columns), f32),
            shape((LANES, slots, BLOCK, columns), bf16),
            shape((LANES, slots, BLOCK, columns), bf16),
        ),
        [smem, smem] + [vmem] * 6,
        [
            pltpu.VMEM((padded, columns), bf16),
            pltpu.VMEM((padded, columns), bf16),
            pltpu.VMEM((2, GLOBALS, columns), bf16),
            pltpu.VMEM((2, GLOBALS, columns), f32),
        ],
        flops=1 << 30,
        moved=12 << 20,
    )(where, names, queries, grad_att, key_states, value_states, keys_arrived, values_arrived)

    keys_returned = lax.all_to_all(keys_sent, "lane", split_axis=0, concat_axis=0, tiled=True)

    pieces = [attended] + [
        lax.ppermute(attended, "head", [(i, (i + k) % heads) for i in range(heads)])
        for k in range(1, heads)
    ]
    everywhere = jnp.concatenate(pieces, axis=1)
    order = (head - jnp.arange(heads)) % heads
    weight_rows = out_weight.reshape(heads, columns, -1).at[order].get(mode="promise_in_bounds")
    weight_rows = weight_rows.reshape(out_weight.shape)
    weight_part = lax.dot_general(
        everywhere, output_grad, (((0,), (0,)), ((), ())), preferred_element_type=f32
    ) * (1.0 / math.sqrt(tokens * slabs * LANES))
    features = weight_part.shape[1]
    keys_returned, weight_part = lax.optimization_barrier((keys_returned, weight_part))

    def collect(returned):
        return call(
            collect_kernel,
            shape((slabs,) + run, bf16),
            [smem, smem, smem, vmem],
            [pltpu.VMEM((slabs * blocks, BLOCK, columns), f32), pltpu.VMEM((GLOBALS, columns), f32)],
            moved=5 << 20,
        )(where, asked, global_pos, returned)

    def sum_slabs(lane_grads):
        return lax.psum_scatter(lane_grads, "slab", scatter_dimension=0, tiled=False)

    lane_grads = collect(keys_returned)
    lane_grads, values_sent = lax.optimization_barrier((lane_grads, values_sent))
    key_others = sum_slabs(lane_grads)
    values_returned = lax.all_to_all(values_sent, "lane", split_axis=0, concat_axis=0, tiled=True)

    weight_part = weight_part.reshape(LANES, -1, features)
    weight_part = lax.all_to_all(weight_part, "lane", split_axis=0, concat_axis=0, tiled=True)
    weight_part = jnp.sum(weight_part, axis=0)
    values_returned, weight_part, key_others = lax.optimization_barrier(
        (values_returned, weight_part, key_others)
    )
    lane_grads = collect(values_returned)
    lane_grads, weight_part = lax.optimization_barrier((lane_grads, weight_part))
    value_others = sum_slabs(lane_grads)

    weight_part = weight_part.reshape(slabs, -1, features)
    weight_part = lax.all_to_all(weight_part, "slab", split_axis=0, concat_axis=0, tiled=True)
    weight_part = jnp.sum(weight_part, axis=0)
    for axis in ("slab", "lane"):
        weight_part = jnp.broadcast_to(weight_part, (lax.axis_size(axis),) + weight_part.shape)
        weight_part = lax.all_to_all(weight_part, axis, split_axis=0, concat_axis=0, tiled=True)
        weight_part = weight_part.reshape(-1, features)
    weight_part = weight_part.reshape(heads, columns, features)
    weight_grad = weight_part.at[order].get(mode="promise_in_bounds")

    projected = jnp.dot(everywhere, weight_rows, preferred_element_type=f32).astype(bf16)
    key_others = key_others.astype(f32).reshape(tokens, columns)
    value_others = value_others.astype(f32).reshape(tokens, columns)
    key_grad = (key_part[BLOCK:-BLOCK] + key_others).astype(bf16)
    value_grad = (value_part[BLOCK:-BLOCK] + value_others).astype(bf16)
    return (
        projected,
        query_grad,
        key_grad,
        value_grad,
        weight_grad.reshape(heads * columns, features),
    )


def solution(mesh):
    seq_count, head_count = mesh.devices.shape
    fine = Mesh(
        mesh.devices.reshape(seq_count // LANES, LANES, head_count), ("slab", "lane", "head")
    )
    seq = ("slab", "lane")
    placed = (
        P(seq, "head"),
        P(seq, "head"),
        P(seq, "head"),
        P(None, "head"),
        P(seq, "head"),
        P(seq, None),
        P(),
    )
    return jax.shard_map(
        shards,
        mesh=fine,
        in_specs=placed,
        out_specs=(
            P(seq, "head"),
            P(seq, "head"),
            P(seq, "head"),
            P(seq, "head"),
            P(None, "head"),
        ),
        check_vma=False,
    )
```

time: 396 us -> 426 us (1.076)
  the two profiles are of different devices: /device:TPU:1 before, /device:TPU:22 now
where the time goes in v2:
time: 426 us; the launch traced here: 425 us
  waiting for transfers between devices  227 us (53%)
  blocking collectives  68.9 us (16%)
  starting transfers between devices  47.8 us (11%)
  Pallas kernels  39.4 us (9%)
  local copies, waits for them, and re-layouts  19.2 us (5%)
  between operations  14 us (3%)
  other arithmetic  5.12 us (1%)
    all_gather x1, waiting for transfers between devices, shards(): lax.all_gather(late_values.reshape(run), 'slab', axis=0, tiled=False)  59.1 us
    all_gather x1, waiting for transfers between devices, shards(): lax.all_gather(key_states.reshape(run), 'slab', axis=0, tiled=False)  48.1 us
    reduce_scatter x2, waiting for transfers between devices, sum_slabs(): lax.psum_scatter(lane_grads, 'slab', scatter_dimension=0, tiled=False)  42.7 us
    all_to_all x1, blocking collectives, serve(): lax.all_to_all(served, 'lane', split_axis=0, concat_axis=0, tiled=True)  33.8 us
    all_to_all x1, waiting for transfers between devices, shards(): lax.all_to_all(values_sent, 'lane', split_axis=0, concat_axis=0, tiled=True)  27.1 us
    all_to_all x1, blocking collectives, shards(): lax.all_to_all(weight_part, 'slab', split_axis=0, concat_axis=0, tiled=True)  21.6 us
    all_to_all x2, waiting for transfers between devices, shards(): lax.all_to_all(weight_part, axis, split_axis=0, concat_axis=0, tiled=True)  18 us
    pallas_call x2, Pallas kernels, collect(): call(collect_kernel, shape((slabs,) + run, bf16), [smem, smem, smem, vmem...  17.9 us
  transfers between devices with their start and end apart: 14, of which 12 were waited for; matrix products, arithmetic and copies ran while one was open for 3% of the time, Pallas kernels for 1%

profile of v2, /device:TPU:22, one launch (start us, length us, event | category | flops | bytes accessed | tf_op | source)
XLA Modules:
  0.0 424.8 jit_solution(8154955596446890729)
XLA Ops:
  7.2 0.0 all-gather.3.cloned.1.call-start
  7.2 0.7 all-gather.3.cloned.1.call-update
  7.9 0.0 all-gather.5.cloned.1.call-start
  8.0 0.8 copy.20
  8.7 0.1 reshape.148.names
  8.8 0.9 select_reduce_fusion
  9.7 0.0 all-gather.5.cloned.1.call-update
  9.7 4.8 %all-to-all-start.1 = ((s32[8,1,16]{2,1,0:T(1,128)}), s32[8,1,16]{2,1,0:T(1,128)S(1)}, u32[]{:S(2)}, u32[]{:S(2)}) async-start(s32[8,1,16]{2,1,0:T(1,128)} %bitcast.5), calls=%async_computation.1 | async-start | bytes 8192 | tf_op jit(solution)/shard_map/all_to_all | solution.py:283
  14.6 1.3 convolution_bitcast_fusion
  15.9 1.1 copy.27
  17.0 0.4 all-to-all-done.1
  17.4 8.1 %all-to-all-start = ((f32[4,576,128]{2,1,0:T(8,128)}), f32[4,576,128]{2,1,0:T(8,128)S(1)}, u32[]{:S(2)}, u32[]{:S(2)}) async-start(f32[4,576,128]{2,1,0:T(8,128)} %bitcast.34), calls=%async_computation | async-start | bytes 2359296 | tf_op jit(solution)/shard_map/all_to_all | solution.py:289
  25.5 0.1 pad_add_fusion.where
  25.6 0.5 broadcast.135
  26.1 0.7 reduce.3
  26.8 0.1 reshape.150.asked
  26.8 13.4 %all-to-all-done = f32[4,576,128]{2,1,0:T(8,128)S(1)} async-done(((f32[4,576,128]{2,1,0:T(8,128)}), f32[4,576,128]{2,1,0:T(8,128)S(1)}, u32[]{:S(2)}, u32[]{:S(2)}) %all-to-all-start) | async-done | bytes 1179680 | tf_op jit(solution)/shard_map/all_to_all | solution.py:289
  40.2 0.1 reduce_sum.27.g
  40.3 48.1 %all-gather.3.cloned.1.call-done.lane_blocks = bf16[16,9,64,128]{3,2,1,0:T(8,128)(2,1)} async-done(((bf16[1,9,64,128]{3,2,1,0:T(8,128)(2,1)}), bf16[16,9,64,128]{3,2,1,0:T(8,128)(2,1)}) %all-gather.3.cloned.1.call-update) | async-done | bytes 2359312 | tf_op jit(solution)/shard_map/all_gather | solution.py:274
  88.4 1.7 copy-done.6
  90.0 6.2 %shard_map.110 = bf16[8,19,64,128]{3,2,1,0:T(8,128)(2,1)S(1)} custom-call(s32[2]{0:T(128)S(1)} %pad_add_fusion.where, s32[128]{0:T(128)S(1)} %reshape.150.asked, s32[128]{0:T(128)S(1)} %copy-done.13, bf16[16,9,64,128]{3,2,1,0:T(8,128)(2,1)S(1)} %copy-done.6), custom_call_target="tpu_custom_call" | custom-call | bytes 5242880 | tf_op jit(solution)/shard_map/pallas_call | solution.py:294
  96.3 1.5 copy-done.1
  97.7 4.8 %all-to-all-start.2 = ((bf16[8,19,64,128]{3,2,1,0:T(8,128)(2,1)}), bf16[8,19,64,128]{3,2,1,0:T(8,128)(2,1)S(1)}, u32[]{:S(2)}, u32[]{:S(2)}) async-start(bf16[8,19,64,128]{3,2,1,0:T(8,128)(2,1)} %copy-done.1), calls=%async_computation.2 | async-start | bytes 4980736 | tf_op jit(solution)/shard_map/all_to_all | solution.py:301
  102.5 59.1 %all-gather.5.cloned.1.call-done.lane_blocks = bf16[16,9,64,128]{3,2,1,0:T(8,128)(2,1)} async-done(((bf16[1,9,64,128]{3,2,1,0:T(8,128)(2,1)}), bf16[16,9,64,128]{3,2,1,0:T(8,128)(2,1)}) %all-gather.5.cloned.1.call-update) | async-done | bytes 2359312 | tf_op jit(solution)/shard_map/all_gather | solution.py:282
  161.6 1.7 copy-done.7
  163.3 6.2 %shard_map.111 = bf16[8,19,64,128]{3,2,1,0:T(8,128)(2,1)S(1)} custom-call(s32[2]{0:T(128)S(1)} %pad_add_fusion.where, s32[128]{0:T(128)S(1)} %reshape.150.asked, s32[128]{0:T(128)S(1)} %copy-done.13, bf16[16,9,64,128]{3,2,1,0:T(8,128)(2,1)S(1)} %copy-done.7), custom_call_target="tpu_custom_call" | custom-call | bytes 5242880 | tf_op jit(solution)/shard_map/pallas_call | solution.py:294
  169.6 33.8 %all_to_all.54.values_arrived = bf16[8,19,64,128]{3,2,1,0:T(8,128)(2,1)S(1)} all-to-all(bf16[8,19,64,128]{3,2,1,0:T(8,128)(2,1)S(1)} %shard_map.111), channel_id=1, replica_groups=mesh['slab'=16,'lane'=8,'head'=4] {'lane'}, dimensions={0} | all-to-all | bytes 4980736 | tf_op jit(solution)/shard_map/all_to_all | solution.py:301
  203.4 9.1 %shard_map.112 = (bf16[576,128]{1,0:T(8,128)(2,1)S(1)}, bf16[576,128]{1,0:T(8,128)(2,1)}, f32[704,128]{1,0:T(8,128)S(1)}, f32[704,128]{1,0:T(8,128)S(1)}, bf16[8...) custom-call(s32[2]{0:T(128)S(1)} %pad_add_fusion.where, s32[27]{0:T(128)S(1)} %reshape.148.names, ...), custom_call_target="tpu_custom_call" | custom-call | flops 1073741824 | bytes 12582912 | tf_op jit(solution)/shard_map/pallas_call | solution.py:308
  212.5 1.4 copy-done.4
  213.9 1.4 copy-done.5
  215.3 0.7 copy-done.10
  216.1 6.3 %all-to-all-start.4 = ((bf16[8,19,64,128]{3,2,1,0:T(8,128)(2,1)}), bf16[8,19,64,128]{3,2,1,0:T(8,128)(2,1)S(1)}, u32[]{:S(2)}, u32[]{:S(2)}) async-start(bf16[8,19,64,128]{3,2,1,0:T(8,128)(2,1)} %copy-done.5), calls=%async_computation.4 | async-start | bytes 4980736 | tf_op jit(solution)/shard_map/all_to_all | solution.py:329
  222.3 2.4 collective-permute-start
  224.8 4.3 %collective-permute-start.1 = (bf16[576,128]{1,0:T(8,128)(2,1)S(1)}, bf16[576,128]{1,0:T(8,128)(2,1)S(1)}, u32[]{:S(2)}, u32[]{:S(2)}) collective-permute-start(bf16[576,128]{1,0:T(8,128)(2,1)S(1)} %get-tuple-element.34), channel_id=1, source_target_pairs={{0,2},{1,3},{2,0},{3,1},{4,6},{5,7},{6,4},{7,5},{8,10},{9,11},{10,... | collective-permute-start | bytes 442376 | tf_op jit(solution)/shard_map/ppermute | solution.py:332
  229.1 1.9 collective-permute-start.2
  231.1 2.7 collective-permute-done.1
  233.8 3.7 collective-permute-done.2
  237.6 0.8 copy-done.15
  238.4 1.2 convolution_multiply_fusion
  239.6 11.0 %all-to-all-done.4.returned = bf16[8,19,64,128]{3,2,1,0:T(8,128)(2,1)S(1)} async-done(((bf16[8,19,64,128]{3,2,1,0:T(8,128)(2,1)}), bf16[8,19,64,128]{3,2,1,0:T(8,128)(2,1)S(1)}, u32[]{:S(2)}, u32[]{:S(2)}) %all-to-all-start.4) | async-done | bytes 2490400 | tf_op jit(solution)/shard_map/all_to_all | solution.py:329
  250.6 8.9 %shard_map.113 = bf16[16,9,64,128]{3,2,1,0:T(8,128)(2,1)S(1)} custom-call(s32[2]{0:T(128)S(1)} %pad_add_fusion.where, s32[128]{0:T(128)S(1)} %reshape.150.asked, s32[128]{0:T(128)S(1)} %copy-done.13, bf16[8,19,64,128]{3,2,1,0:T(8,128)(2,1)S(1)} %all-to-all-done.4.returned), custom_call_target="tpu_custom_call" | custom-call | bytes 5242880 | tf_op jit(solution)/shard_map/pallas_call | solution.py:346
  259.5 1.4 copy-done.3
  260.9 0.0 reduce-scatter.3.cloned.1.call-update
  260.9 1.0 copy-done.17
  262.0 13.4 %all_to_all.55 = f32[8,64,256]{2,1,0:T(8,128)} all-to-all(f32[8,64,256]{2,1,0:T(8,128)S(1)} %bitcast.40), channel_id=1, replica_groups=mesh['slab'=16,'lane'=8,'head'=4] {'lane'}, dimensions={0} | all-to-all | bytes 1048576 | tf_op jit(solution)/shard_map/all_to_all | solution.py:363
  275.4 6.7 %all-to-all-start.5 = ((bf16[8,19,64,128]{3,2,1,0:T(8,128)(2,1)}), bf16[8,19,64,128]{3,2,1,0:T(8,128)(2,1)S(1)}, u32[]{:S(2)}, u32[]{:S(2)}) async-start(bf16[8,19,64,128]{3,2,1,0:T(8,128)(2,1)} %copy-done.4), calls=%async_computation.5 | async-start | bytes 4980736 | tf_op jit(solution)/shard_map/all_to_all | solution.py:360
  282.1 1.1 reduce_sum.28
  283.2 27.1 %all-to-all-done.5.returned = bf16[8,19,64,128]{3,2,1,0:T(8,128)(2,1)S(1)} async-done(((bf16[8,19,64,128]{3,2,1,0:T(8,128)(2,1)}), bf16[8,19,64,128]{3,2,1,0:T(8,128)(2,1)S(1)}, u32[]{:S(2)}, u32[]{:S(2)}) %all-to-all-start.5) | async-done | bytes 2490400 | tf_op jit(solution)/shard_map/all_to_all | solution.py:360
  310.4 22.2 %reduce-scatter.3.cloned.1.call-done = bf16[1,9,64,128]{3,2,1,0:T(8,128)(2,1)} async-done(((bf16[16,9,64,128]{3,2,1,0:T(8,128)(2,1)}), bf16[1,9,64,128]{3,2,1,0:T(8,128)(2,1)}) %reduce-scatter.3.cloned.1.call-update) | async-done | bytes 147472 | tf_op jit(solution)/shard_map/reduce_scatter | solution.py:355
  332.6 8.9 %shard_map.114 = bf16[16,9,64,128]{3,2,1,0:T(8,128)(2,1)S(1)} custom-call(s32[2]{0:T(128)S(1)} %pad_add_fusion.where, s32[128]{0:T(128)S(1)} %reshape.150.asked, s32[128]{0:T(128)S(1)} %copy-done.13, bf16[8,19,64,128]{3,2,1,0:T(8,128)(2,1)S(1)} %all-to-all-done.5.returned), custom_call_target="tpu_custom_call" | custom-call | bytes 5242880 | tf_op jit(solution)/shard_map/pallas_call | solution.py:346
  341.5 1.4 copy-done.2
  343.0 21.6 %all_to_all.56 = f32[16,4,256]{2,1,0:T(4,128)S(1)} all-to-all(f32[16,4,256]{2,1,0:T(4,128)S(1)} %reshape.156), channel_id=1, replica_groups=mesh['slab'=16,'lane'=8,'head'=4] {'slab'}, dimensions={0} | all-to-all | bytes 131072 | tf_op jit(solution)/shard_map/all_to_all | solution.py:373
  364.7 0.6 broadcast_in_dim.27
  365.3 3.5 all-to-all-start.8
  368.9 0.6 gather_fusion
  369.4 12.6 %all-to-all-done.8 = f32[16,4,256]{2,1,0:T(4,128)S(1)} async-done(((f32[16,4,256]{2,1,0:T(4,128)}), f32[16,4,256]{2,1,0:T(4,128)S(1)}, u32[]{:S(2)}, u32[]{:S(2)}) %all-to-all-start.8) | async-done | bytes 65568 | tf_op jit(solution)/shard_map/all_to_all | solution.py:377
  382.0 0.8 broadcast_in_dim.28
  382.9 4.8 %all-to-all-start.9 = ((f32[8,64,256]{2,1,0:T(8,128)}), f32[8,64,256]{2,1,0:T(8,128)S(1)}, u32[]{:S(2)}, u32[]{:S(2)}) async-start(f32[8,64,256]{2,1,0:T(8,128)} %broadcast_in_dim.28), calls=%async_computation.11 | async-start | bytes 1048576 | tf_op jit(solution)/shard_map/all_to_all | solution.py:377
  387.7 1.0 convolution_convert_fusion
  388.7 0.7 fusion.1
  389.4 5.5 %all-to-all-done.9 = f32[8,64,256]{2,1,0:T(8,128)S(1)} async-done(((f32[8,64,256]{2,1,0:T(8,128)}), f32[8,64,256]{2,1,0:T(8,128)S(1)}, u32[]{:S(2)}, u32[]{:S(2)}) %all-to-all-start.9) | async-done | bytes 524320 | tf_op jit(solution)/shard_map/all_to_all | solution.py:377
  394.9 1.4 gather_fusion.1
  396.2 20.5 %reduce-scatter.5.cloned.1.call-done = bf16[1,9,64,128]{3,2,1,0:T(8,128)(2,1)} async-done(((bf16[16,9,64,128]{3,2,1,0:T(8,128)(2,1)}), bf16[1,9,64,128]{3,2,1,0:T(8,128)(2,1)}) %reduce-scatter.5.cloned.1.call-update) | async-done | bytes 147472 | tf_op jit(solution)/shard_map/reduce_scatter | solution.py:355
  416.7 1.6 fusion
  (45 shorter events, 0.3 us)
Async XLA Ops:
  7.2 7.4 %copy-start = (bf16[576,256]{1,0:T(8,128)(2,1)S(1)}, bf16[576,256]{1,0:T(8,128)(2,1)}, u32[]{:S(2)}) copy-start(bf16[576,256]{1,0:T(8,128)(2,1)} %param.11) | copy-start | bytes 884740
  7.2 81.2 %all-gather.3.cloned.1.call-start = ((), (), s32[]{:S(2)}) async-start(), calls=%async_computation.12 | async-start | bytes 2506752 | tf_op jit(solution)/shard_map/all_gather | solution.py:274
  7.9 153.7 %all-gather.5.cloned.1.call-start = ((), (), s32[]{:S(2)}) async-start(), calls=%async_computation.13 | async-start | bytes 2506752 | tf_op jit(solution)/shard_map/all_gather | solution.py:282
  9.7 7.6 %all-to-all-start.1 = ((s32[8,1,16]{2,1,0:T(1,128)}), s32[8,1,16]{2,1,0:T(1,128)S(1)}, u32[]{:S(2)}, u32[]{:S(2)}) async-start(s32[8,1,16]{2,1,0:T(1,128)} %bitcast.5), calls=%async_computation.1 | async-start | bytes 8192 | tf_op jit(solution)/shard_map/all_to_all | solution.py:283
  15.9 72.5 %copy-start.13 = (s32[128]{0:T(128)S(1)}, s32[128]{0:T(128)}, u32[]{:S(2)}) copy-start(s32[128]{0:T(128)} %global_pos.7) | copy-start | bytes 1540
  17.4 22.8 %all-to-all-start = ((f32[4,576,128]{2,1,0:T(8,128)}), f32[4,576,128]{2,1,0:T(8,128)S(1)}, u32[]{:S(2)}, u32[]{:S(2)}) async-start(f32[4,576,128]{2,1,0:T(8,128)} %bitcast.34), calls=%async_computation | async-start | bytes 2359296 | tf_op jit(solution)/shard_map/all_to_all | solution.py:289
  88.3 1.7 copy-start.6
  96.3 1.5 copy-start.1
  97.7 63.9 %all-to-all-start.2 = ((bf16[8,19,64,128]{3,2,1,0:T(8,128)(2,1)}), bf16[8,19,64,128]{3,2,1,0:T(8,128)(2,1)S(1)}, u32[]{:S(2)}, u32[]{:S(2)}) async-start(bf16[8,19,64,128]{3,2,1,0:T(8,128)(2,1)} %copy-done.1), calls=%async_computation.2 | async-start | bytes 4980736 | tf_op jit(solution)/shard_map/all_to_all | solution.py:301
  161.6 1.7 copy-start.7
  169.5 33.9 %copy-start.8 = (bf16[576,128]{1,0:T(8,128)(2,1)S(1)}, bf16[576,128]{1,0:T(8,128)(2,1)}, u32[]{:S(2)}) copy-start(bf16[576,128]{1,0:T(8,128)(2,1)} %key.1) | copy-start | bytes 442372
  169.5 33.9 %copy-start.9 = (bf16[576,128]{1,0:T(8,128)(2,1)S(1)}, bf16[576,128]{1,0:T(8,128)(2,1)}, u32[]{:S(2)}) copy-start(bf16[576,128]{1,0:T(8,128)(2,1)} %value.1) | copy-start | bytes 442372
  169.5 33.9 %copy-start.12 = (bf16[576,128]{1,0:T(8,128)(2,1)S(1)}, bf16[576,128]{1,0:T(8,128)(2,1)}, u32[]{:S(2)}) copy-start(bf16[576,128]{1,0:T(8,128)(2,1)} %q.1) | copy-start | bytes 442372
  212.5 1.4 copy-start.4
  213.9 1.4 copy-start.5
  215.3 0.7 copy-start.10
  216.1 34.5 %all-to-all-start.4 = ((bf16[8,19,64,128]{3,2,1,0:T(8,128)(2,1)}), bf16[8,19,64,128]{3,2,1,0:T(8,128)(2,1)S(1)}, u32[]{:S(2)}, u32[]{:S(2)}) async-start(bf16[8,19,64,128]{3,2,1,0:T(8,128)(2,1)} %copy-done.5), calls=%async_computation.4 | async-start | bytes 4980736 | tf_op jit(solution)/shard_map/all_to_all | solution.py:329
  222.3 110.2 %reduce-scatter.3.cloned.1.call-start = ((), (), s32[]{:S(2)}) async-start(), calls=%async_computation.14 | async-start | bytes 2506752 | tf_op jit(solution)/shard_map/reduce_scatter | solution.py:355
  222.3 8.7 %collective-permute-start = (bf16[576,128]{1,0:T(8,128)(2,1)S(1)}, bf16[576,128]{1,0:T(8,128)(2,1)S(1)}, u32[]{:S(2)}, u32[]{:S(2)}) collective-permute-start(bf16[576,128]{1,0:T(8,128)(2,1)S(1)} %get-tuple-element.34), channel_id=1, source_target_pairs={{0,1},{1,2},{2,3},{3,0},{4,5},{5,6},{6,7},{7,4},{8,9},{9,10},{10,1... | collective-permute-start | bytes 442376 | tf_op jit(solution)/shard_map/ppermute | solution.py:332
  224.8 9.0 %collective-permute-start.1 = (bf16[576,128]{1,0:T(8,128)(2,1)S(1)}, bf16[576,128]{1,0:T(8,128)(2,1)S(1)}, u32[]{:S(2)}, u32[]{:S(2)}) collective-permute-start(bf16[576,128]{1,0:T(8,128)(2,1)S(1)} %get-tuple-element.34), channel_id=1, source_target_pairs={{0,2},{1,3},{2,0},{3,1},{4,6},{5,7},{6,4},{7,5},{8,10},{9,11},{10,... | collective-permute-start | bytes 442376 | tf_op jit(solution)/shard_map/ppermute | solution.py:332
  229.1 8.4 %collective-permute-start.2 = (bf16[576,128]{1,0:T(8,128)(2,1)S(1)}, bf16[576,128]{1,0:T(8,128)(2,1)S(1)}, u32[]{:S(2)}, u32[]{:S(2)}) collective-permute-start(bf16[576,128]{1,0:T(8,128)(2,1)S(1)} %get-tuple-element.34), channel_id=1, source_target_pairs={{0,3},{1,0},{2,1},{3,2},{4,7},{5,4},{6,5},{7,6},{8,11},{9,8},{10,9... | collective-permute-start | bytes 442376 | tf_op jit(solution)/shard_map/ppermute | solution.py:332
  237.6 0.8 copy-start.15
  259.5 1.4 copy-start.3
  260.9 1.0 copy-start.17
  275.4 35.0 %all-to-all-start.5 = ((bf16[8,19,64,128]{3,2,1,0:T(8,128)(2,1)}), bf16[8,19,64,128]{3,2,1,0:T(8,128)(2,1)S(1)}, u32[]{:S(2)}, u32[]{:S(2)}) async-start(bf16[8,19,64,128]{3,2,1,0:T(8,128)(2,1)} %copy-done.4), calls=%async_computation.5 | async-start | bytes 4980736 | tf_op jit(solution)/shard_map/all_to_all | solution.py:360
  282.1 134.6 %reduce-scatter.5.cloned.1.call-start = ((), (), s32[]{:S(2)}) async-start(), calls=%async_computation.15 | async-start | bytes 2506752 | tf_op jit(solution)/shard_map/reduce_scatter | solution.py:355
  341.5 1.4 copy-start.2
  342.9 25.9 %copy-start.14 = (bf16[512,256]{1,0:T(8,128)(2,1)S(1)}, bf16[512,256]{1,0:T(8,128)(2,1)}, u32[]{:S(2)}) copy-start(bf16[512,256]{1,0:T(8,128)(2,1)} %param.10) | copy-start | bytes 786436
  342.9 44.8 %copy-start.16 = (bf16[576,512]{1,0:T(8,128)(2,1)S(1)}, bf16[576,512]{1,0:T(8,128)(2,1)}, u32[]{:S(2)}) copy-start(bf16[576,512]{1,0:T(8,128)(2,1)} %copy-done.15) | copy-start | bytes 1769476
  342.9 45.8 %copy-start.11 = (f32[704,128]{1,0:T(8,128)S(1)}, f32[704,128]{1,0:T(8,128)}, u32[]{:S(2)}) copy-start(f32[704,128]{1,0:T(8,128)} %copy-done.10) | copy-start | bytes 1081348
  342.9 45.8 %copy-start.18 = (bf16[1,9,64,128]{3,2,1,0:T(8,128)(2,1)S(1)}, bf16[1,9,64,128]{3,2,1,0:T(8,128)(2,1)}, u32[]{:S(2)}) copy-start(bf16[1,9,64,128]{3,2,1,0:T(8,128)(2,1)} %reduce-scatter.3.cloned.1.call-done) | copy-start | bytes 442372
  365.3 16.7 %all-to-all-start.8 = ((f32[16,4,256]{2,1,0:T(4,128)}), f32[16,4,256]{2,1,0:T(4,128)S(1)}, u32[]{:S(2)}, u32[]{:S(2)}) async-start(f32[16,4,256]{2,1,0:T(4,128)} %broadcast_in_dim.27), calls=%async_computation.10 | async-start | bytes 131072 | tf_op jit(solution)/shard_map/all_to_all | solution.py:377
  382.9 12.0 %all-to-all-start.9 = ((f32[8,64,256]{2,1,0:T(8,128)}), f32[8,64,256]{2,1,0:T(8,128)S(1)}, u32[]{:S(2)}, u32[]{:S(2)}) async-start(f32[8,64,256]{2,1,0:T(8,128)} %broadcast_in_dim.28), calls=%async_computation.11 | async-start | bytes 1048576 | tf_op jit(solution)/shard_map/all_to_all | solution.py:377
Sparse Core Ops, SparseCore 0:
  10.1 78.2 all-gather.2
  90.4 71.1 all-gather.4
  261.1 71.4 reduce-scatter.2
  343.1 73.5 reduce-scatter.4

commit v3 on v1

v3 whole, which is shorter than its diff:
```python
import math

import jax
import jax.numpy as jnp
from jax import lax
from jax.experimental import pallas as pl
from jax.experimental.pallas import tpu as pltpu
from jax.sharding import Mesh
from jax.sharding import PartitionSpec as P

HEAD_DIM = 64
BLOCK = 64
PAIR = 2 * BLOCK
LANES = 16
R = 3
GLOBALS = 128
VMEM_LIMIT = 40 * 1024 * 1024


def whole(space=pltpu.VMEM):
    return pl.BlockSpec(memory_space=space)


def shape(dims, dtype):
    return jax.ShapeDtypeStruct(dims, dtype)


def call(kernel, out_shape, in_specs, scratch=(), flops=0, moved=0):
    return pl.pallas_call(
        kernel,
        out_shape=out_shape,
        in_specs=in_specs,
        out_specs=jax.tree.map(lambda _: whole(), out_shape),
        scratch_shapes=list(scratch),
        compiler_params=pltpu.CompilerParams(vmem_limit_bytes=VMEM_LIMIT),
        cost_estimate=pl.CostEstimate(flops=flops, bytes_accessed=moved, transcendentals=0),
    )


def panel_kernel(token_row, key, value, panel, key_wide, value_wide, panel_wide):
    tokens = key.shape[0]
    key_wide[...] = key[...].astype(jnp.float32)
    value_wide[...] = value[...].astype(jnp.float32)
    panel_wide[...] = jnp.zeros_like(panel_wide)

    def one(number, carry):
        row = token_row[number]

        @pl.when((row >= 0) & (row < tokens))
        def _():
            panel_wide[pl.ds(number, 1), :] = key_wide[pl.ds(row, 1), :]
            panel_wide[pl.ds(number + GLOBALS, 1), :] = value_wide[pl.ds(row, 1), :]

        return carry

    lax.fori_loop(0, GLOBALS, one, 0)
    panel[...] = panel_wide[...].astype(panel.dtype)


def serve_kernel(asked, lane_blocks, send):
    slabs = lane_blocks.shape[0]

    def serve(number, carry):
        source = number % slabs
        send[number // slabs, source] = lane_blocks[source, jnp.maximum(asked[number], 0)]
        return carry

    lax.fori_loop(0, LANES * slabs, serve, 0)


def attention_kernel(
    place,
    names,
    q,
    g,
    key,
    value,
    left,
    right,
    panel,
    arrived,
    attended,
    query_grad,
    key_grad,
    value_grad,
    panel_grad,
    rims,
    send,
    key_pad,
    value_pad,
):
    tokens, columns = q.shape
    blocks = tokens // BLOCK
    scale = 1.0 / math.sqrt(HEAD_DIM)
    f32, bf16 = jnp.float32, jnp.bfloat16
    key_pad[:BLOCK, :] = left[:BLOCK, :]
    value_pad[:BLOCK, :] = left[BLOCK:, :]
    key_pad[BLOCK : BLOCK + tokens, :] = key[...]
    value_pad[BLOCK : BLOCK + tokens, :] = value[...]
    key_pad[BLOCK + tokens :, :] = right[:BLOCK, :]
    value_pad[BLOCK + tokens :, :] = right[BLOCK:, :]
    key_grad[...] = jnp.zeros_like(key_grad)
    value_grad[...] = jnp.zeros_like(value_grad)
    panel_grad[...] = jnp.zeros_like(panel_grad)
    first_block, last_block = place[0], place[1]
    first_head = lax.broadcasted_iota(jnp.int32, (BLOCK, columns), 1) < HEAD_DIM
    window = 3 * BLOCK
    keys = window + GLOBALS + R * BLOCK
    key_column = lax.broadcasted_iota(jnp.int32, (1, keys), 1)

    def by_head(rows):
        zero = jnp.zeros_like(rows)
        return jnp.concatenate(
            [jnp.where(first_head, rows, zero), jnp.where(first_head, zero, rows)], axis=0
        )

    def joined(pair):
        return jnp.where(first_head, pair[:BLOCK], pair[BLOCK:])

    def dot(a, b, dims):
        return lax.dot_general(a, b, (dims, ((), ())), preferred_element_type=f32)

    def one(block, carry):
        row = pl.multiple_of(block * BLOCK, BLOCK)
        here = pl.ds(row, BLOCK)
        around = pl.ds(row, window)
        owners = [names[block * R + j] // blocks for j in range(R)]
        slots = [(owner % LANES, owner // LANES) for owner in owners]
        kk = jnp.concatenate(
            [key_pad[around, :], panel[:GLOBALS, :]] + [arrived[a, b, :BLOCK, :] for a, b in slots], axis=0
        )
        vv = jnp.concatenate(
            [value_pad[around, :], panel[GLOBALS:, :]] + [arrived[a, b, BLOCK:, :] for a, b in slots], axis=0
        )
        q2 = by_head(q[here, :])
        g2 = by_head(g[here, :])
        number = first_block + block
        dead = ((key_column < BLOCK) & (number == 0)) | (
            (key_column >= 2 * BLOCK) & (key_column < window) & (number == last_block)
        )
        scores = dot(q2, kk, ((1,), (1,))) * scale
        scores = jnp.where(dead, -jnp.inf, scores)
        top = jnp.max(scores, axis=-1, keepdims=True)
        raised = jnp.exp(scores - top)
        probs = raised * (1.0 / jnp.sum(raised, axis=-1, keepdims=True))
        probs_b = probs.astype(bf16)
        att = joined(dot(probs_b, vv, ((1,), (0,)))).astype(bf16)
        attended[here, :] = att
        att_f = att.astype(f32)
        delta = jnp.sum(
            g2.astype(f32) * jnp.concatenate([att_f, att_f], axis=0), axis=-1, keepdims=True
        )
        slope = (probs * (dot(g2, vv, ((1,), (1,))) - delta)).astype(bf16)
        query_grad[here, :] = (scale * joined(dot(slope, kk, ((1,), (0,))))).astype(bf16)
        dk = scale * dot(slope, q2, ((0,), (0,)))
        dv = dot(probs_b, g2, ((0,), (0,)))
        key_grad[around, :] += dk[:window]
        value_grad[around, :] += dv[:window]
        panel_grad[:GLOBALS, :] += dk[window : window + GLOBALS]
        panel_grad[GLOBALS:, :] += dv[window : window + GLOBALS]
        for j, (a, b) in enumerate(slots):
            first = window + GLOBALS + j * BLOCK
            send[a, b, :BLOCK, :] = dk[first : first + BLOCK].astype(bf16)
            send[a, b, BLOCK:, :] = dv[first : first + BLOCK].astype(bf16)
        return carry

    lax.fori_loop(0, blocks, one, 0)
    for side, rows in enumerate((pl.ds(0, BLOCK), pl.ds(BLOCK + tokens, BLOCK))):
        rims[side, :BLOCK, :] = key_grad[rows, :].astype(bf16)
        rims[side, BLOCK:, :] = value_grad[rows, :].astype(bf16)


def collect_kernel(asked, returned, lane_grads, sums):
    slabs, blocks = lane_grads.shape[:2]
    sums[...] = jnp.zeros_like(sums)

    def add(number, carry):
        wanted = asked[number]

        @pl.when(wanted >= 0)
        def _():
            source = number % slabs
            sums[source * blocks + wanted] += returned[number // slabs, source].astype(jnp.float32)

        return carry

    lax.fori_loop(0, LANES * slabs, add, 0)

    def write(number, carry):
        lane_grads[number // blocks, number % blocks] = sums[number].astype(lane_grads.dtype)
        return carry

    lax.fori_loop(0, slabs * blocks, write, 0)


def finish_kernel(
    token_row,
    key_grad,
    value_grad,
    from_left,
    from_right,
    panel_grad,
    others,
    key_out,
    value_out,
    key_sum,
    value_sum,
):
    tokens = key_out.shape[0]
    f32 = jnp.float32

    def own(block, carry):
        row = pl.multiple_of(block * BLOCK, BLOCK)
        here, padded = pl.ds(row, BLOCK), pl.ds(row + BLOCK, BLOCK)
        key_sum[here, :] = key_grad[padded, :] + others[block, :BLOCK, :].astype(f32)
        value_sum[here, :] = value_grad[padded, :] + others[block, BLOCK:, :].astype(f32)
        return carry

    lax.fori_loop(0, others.shape[0], own, 0)
    key_sum[:BLOCK, :] += from_left[:BLOCK, :].astype(f32)
    value_sum[:BLOCK, :] += from_left[BLOCK:, :].astype(f32)
    key_sum[tokens - BLOCK :, :] += from_right[:BLOCK, :].astype(f32)
    value_sum[tokens - BLOCK :, :] += from_right[BLOCK:, :].astype(f32)

    def add_row(number, carry):
        row = token_row[number]

        @pl.when((row >= 0) & (row < tokens))
        def _():
            key_sum[pl.ds(row, 1), :] += panel_grad[pl.ds(number, 1), :]
            value_sum[pl.ds(row, 1), :] += panel_grad[pl.ds(number + GLOBALS, 1), :]

        return carry

    lax.fori_loop(0, GLOBALS, add_row, 0)
    key_out[...] = key_sum[...].astype(key_out.dtype)
    value_out[...] = value_sum[...].astype(value_out.dtype)


def exchange(array, axis):
    return lax.all_to_all(array, axis, split_axis=0, concat_axis=0, tiled=True)


def total(array):
    return jnp.sum(array.astype(jnp.float32), axis=0).astype(array.dtype)


def sum_over_slabs_and_spread(share):
    share = total(exchange(jnp.broadcast_to(share, (lax.axis_size("slab"),) + share.shape), "slab"))
    return exchange(jnp.broadcast_to(share, (LANES,) + share.shape), "lane")


def shards(queries, key_states, value_states, out_weight, output_grad, rand_blocks, global_pos):
    bf16, f32 = jnp.bfloat16, jnp.float32
    tokens, columns = queries.shape
    blocks = tokens // BLOCK
    slabs, heads = lax.axis_size("slab"), lax.axis_size("head")
    slab, me, head = lax.axis_index("slab"), lax.axis_index("lane"), lax.axis_index("head")
    position, seq_count = slab * LANES + me, slabs * LANES
    smem, vmem = whole(pltpu.SMEM), whole()
    token_row = global_pos - position * tokens

    own = jnp.concatenate(
        [key_states.reshape(blocks, BLOCK, columns), value_states.reshape(blocks, BLOCK, columns)],
        axis=1,
    )
    lane_blocks = lax.all_gather(own, "slab", axis=0, tiled=False)

    names = rand_blocks.reshape(-1)
    owner = names // blocks
    index = jnp.arange(LANES)[:, None] + LANES * jnp.arange(slabs)[None, :]
    hit = owner[None, None, :] == index[:, :, None]
    wanted = jnp.max(jnp.where(hit, (names % blocks)[None, None, :], -1), axis=-1)
    asked = exchange(wanted, "lane").reshape(-1)

    seq = ("slab", "lane")
    forth = [(i, i + 1) for i in range(seq_count - 1)]
    back = [(i + 1, i) for i in range(seq_count - 1)]
    left = lax.ppermute(own[blocks - 1], seq, forth)
    right = lax.ppermute(own[0], seq, back)

    panel = call(
        panel_kernel,
        shape((2 * GLOBALS, columns), bf16),
        [smem, vmem, vmem],
        [pltpu.VMEM((tokens, columns), f32)] * 2 + [pltpu.VMEM((2 * GLOBALS, columns), f32)],
        moved=1 << 20,
    )(token_row, key_states, value_states)
    panel = total(exchange(panel.reshape(LANES, -1, columns), "lane"))
    panel = sum_over_slabs_and_spread(panel).reshape(2 * GLOBALS, columns)

    lane_blocks, asked, left, right, panel, late_grad = lax.optimization_barrier(
        (lane_blocks, asked, left, right, panel, output_grad)
    )
    partial_grad = lax.dot_general(
        late_grad, out_weight, (((1,), (1,)), ((), ())), preferred_element_type=f32
    )
    grad_att = lax.psum_scatter(partial_grad, "head", scatter_dimension=1, tiled=True).astype(bf16)

    served = call(
        serve_kernel, shape((LANES, slabs, PAIR, columns), bf16), [smem, vmem], moved=8 << 20
    )(asked, lane_blocks)
    arrived = exchange(served, "lane")

    place = jnp.stack([position * blocks, seq_count * blocks - 1]).astype(jnp.int32)
    padded = tokens + PAIR
    attended, query_grad, key_part, value_part, panel_part, rims, sent = call(
        attention_kernel,
        (
            shape((tokens, columns), bf16),
            shape((tokens, columns), bf16),
            shape((padded, columns), f32),
            shape((padded, columns), f32),
            shape((2 * GLOBALS, columns), f32),
            shape((2, PAIR, columns), bf16),
            shape((LANES, slabs, PAIR, columns), bf16),
        ),
        [smem, smem] + [vmem] * 8,
        [pltpu.VMEM((padded, columns), bf16)] * 2,
        flops=1 << 30,
        moved=12 << 20,
    )(place, names, queries, grad_att, key_states, value_states, left, right, panel, arrived)

    returned = exchange(sent, "lane")
    from_left = lax.ppermute(rims[1], seq, forth)
    from_right = lax.ppermute(rims[0], seq, back)

    pieces = [attended] + [
        lax.ppermute(attended, "head", [(i, (i + k) % heads) for i in range(heads)])
        for k in range(1, heads)
    ]
    everywhere = jnp.concatenate(pieces, axis=1)
    order = (head - jnp.arange(heads)) % heads
    weight_rows = out_weight.reshape(heads, columns, -1).at[order].get(mode="promise_in_bounds")
    weight_rows = weight_rows.reshape(out_weight.shape)
    weight_part = lax.dot_general(
        everywhere, output_grad, (((0,), (0,)), ((), ())), preferred_element_type=f32
    ) * (1.0 / math.sqrt(tokens * seq_count))
    features = weight_part.shape[1]
    returned, from_left, from_right, weight_part = lax.optimization_barrier(
        (returned, from_left, from_right, weight_part)
    )
    lane_grads = call(
        collect_kernel,
        shape((slabs, blocks, PAIR, columns), bf16),
        [smem, vmem],
        [pltpu.VMEM((slabs * blocks, PAIR, columns), f32)],
        moved=10 << 20,
    )(asked, returned)
    lane_grads, weight_part, panel_part = lax.optimization_barrier(
        (lane_grads, weight_part, panel_part)
    )
    others = lax.psum_scatter(lane_grads, "slab", scatter_dimension=0, tiled=False)

    parts = [weight_part[:, at : at + columns] for at in range(0, features, columns)]
    parts = [part.reshape(LANES, -1, columns) for part in parts + [panel_part]]
    share = total(exchange(jnp.concatenate(parts, axis=1), "lane"))
    sums = sum_over_slabs_and_spread(share).reshape(LANES, -1, columns)
    lane_rows = heads * columns // LANES
    weight_grad = jnp.concatenate(
        [
            sums[:, at : at + lane_rows].reshape(heads, columns, columns)
            for at in range(0, lane_rows * (features // columns), lane_rows)
        ],
        axis=2,
    )
    weight_grad = weight_grad.at[order].get(mode="promise_in_bounds")
    weight_grad = weight_grad.reshape(heads * columns, features)
    panel_grad = sums[:, lane_rows * (features // columns) :].reshape(2 * GLOBALS, columns)

    projected = jnp.dot(everywhere, weight_rows, preferred_element_type=f32).astype(bf16)
    key_grad, value_grad = call(
        finish_kernel,
        (shape((tokens, columns), bf16), shape((tokens, columns), bf16)),
        [smem] + [vmem] * 6,
        [pltpu.VMEM((tokens, columns), f32)] * 2,
        moved=2 << 20,
    )(token_row, key_part, value_part, from_left, from_right, panel_grad, others)
    return projected, query_grad, key_grad, value_grad, weight_grad


def solution(mesh):
    seq_count, head_count = mesh.devices.shape
    fine = Mesh(
        mesh.devices.reshape(seq_count // LANES, LANES, head_count), ("slab", "lane", "head")
    )
    seq = ("slab", "lane")
    placed = (
        P(seq, "head"),
        P(seq, "head"),
        P(seq, "head"),
        P(None, "head"),
        P(seq, "head"),
        P(seq, None),
        P(),
    )
    return jax.shard_map(
        shards,
        mesh=fine,
        in_specs=placed,
        out_specs=(
            P(seq, "head"),
            P(seq, "head"),
            P(seq, "head"),
            P(seq, "head"),
            P(None, "head"),
        ),
        check_vma=False,
    )
```

time: 396 us -> 357 us (0.902)
  blocking collectives: 173 us -> 38.4 us
  starting transfers between devices: 30.1 us -> 87.8 us
  waiting for transfers between devices: 132 us -> 161 us
  local copies, waits for them, and re-layouts: 10 us -> 14.3 us
    all_gather x2 -> x0, blocking collectives: 96.4 us -> none  [the longest x1 83.8 us: shards(): lax.all_gather(weight_part, ('slab', 'lane'), axis=0, tiled=True)]
    all_gather x1, waiting for transfers between devices: 61.5 us -> 5.67 us  [shards(): lane_blocks = lax.all_gather(own, 'slab', axis=0, tiled=False)]
    all_to_all x3 -> x8, waiting for transfers between devices: 42.3 us -> 87.6 us  [exchange(): return lax.all_to_all(array, axis, split_axis=0, concat_axis=0, tiled=True)]
    all_to_all x2 -> x1, blocking collectives: 76.1 us -> 38.4 us  [exchange(): return lax.all_to_all(array, axis, split_axis=0, concat_axis=0, tiled=True)]
    all_to_all x3 -> x8, starting transfers between devices: 30 us -> 66.4 us  [exchange(): return lax.all_to_all(array, axis, split_axis=0, concat_axis=0, tiled=True)]
    ppermute x0 -> x7, waiting for transfers between devices: none -> 31.6 us  [the longest x1 29.8 us: shards(): from_right = lax.ppermute(rims[0], seq, back)]
    ppermute x0 -> x7, starting transfers between devices: none -> 21.3 us  [the longest x3 9.68 us: shards(): lax.ppermute(attended, 'head', [(i, (i + k) % heads) for i in range(heads)])]
    reduce_scatter x1, waiting for transfers between devices: 0.01 us -> 5.14 us  [shards(): lax.psum_scatter(lane_grads, 'slab', scatter_dimension=0, tiled=False)]
  transfers between devices with their start and end apart: 6 -> 18, of which waited for: 5 -> 13; matrix products, arithmetic and copies ran while one was open for 2% -> 4% of each run, Pallas kernels for 0% -> 1%
where the time goes in v3:
time: 357 us; the launch traced here: 353 us
  waiting for transfers between devices  161 us (45%)
  starting transfers between devices  87.8 us (25%)
  blocking collectives  38.4 us (11%)
  Pallas kernels  26.3 us (7%)
  local copies, waits for them, and re-layouts  14.3 us (4%)
  between operations  14 us (4%)
  other arithmetic  6.99 us (2%)
  matrix products  3.96 us (1%)
    all_to_all x8, waiting for transfers between devices, exchange(): return lax.all_to_all(array, axis, split_axis=0, concat_axis=0, tiled=True)  87.6 us
    all_to_all x8, starting transfers between devices, exchange(): return lax.all_to_all(array, axis, split_axis=0, concat_axis=0, tiled=True)  66.4 us
    all_to_all x1, blocking collectives, exchange(): return lax.all_to_all(array, axis, split_axis=0, concat_axis=0, tiled=True)  38.4 us
    reduce_scatter x1, waiting for transfers between devices, shards(): lax.psum_scatter(partial_grad, 'head', scatter_dimension=1, tiled=True)  30.1 us
    ppermute x1, waiting for transfers between devices, shards(): from_right = lax.ppermute(rims[0], seq, back)  29.8 us
    pallas_call x1, Pallas kernels, shards(): call(attention_kernel, (shape((tokens, columns), bf16), shape((tokens, co...  10.6 us
    ppermute x3, starting transfers between devices, shards(): lax.ppermute(attended, 'head', [(i, (i + k) % heads) for i in range(heads)])  9.68 us
    unnamed x28, local copies, waits for them, and re-layouts  9.37 us
  transfers between devices with their start and end apart: 18, of which 13 were waited for; matrix products, arithmetic and copies ran while one was open for 4% of the time, Pallas kernels for 1%

profile of v3, /device:TPU:1, one launch (start us, length us, event | category | flops | bytes accessed | tf_op | source)
XLA Modules:
  0.0 352.5 jit_solution(8706275883056413004)
XLA Ops:
  7.2 0.0 all-gather.3.cloned.1.call-start
  7.2 1.8 pad_maximum_fusion.2
  9.0 0.7 broadcast_subtract_fusion.token_row
  9.7 0.9 copy-done.3
  10.6 0.9 copy-done.5
  11.5 3.1 shard_map.110
  14.6 10.2 %all-to-all-start.1 = ((bf16[16,16,128]{2,1,0:T(8,128)(2,1)}), bf16[16,16,128]{2,1,0:T(8,128)(2,1)S(1)}, u32[]{:S(2)}, u32[]{:S(2)}) async-start(bf16[16,16,128]{2,1,0:T(8,128)(2,1)} %bitcast.7), calls=%async_computation.1 | async-start | bytes 131072 | tf_op jit(solution)/shard_map/all_to_all | solution.py:241
  24.8 0.8 copy.18
  25.5 0.1 reshape.156.names
  25.7 5.0 %all-to-all-done.1 = bf16[16,16,128]{2,1,0:T(8,128)(2,1)S(1)} async-done(((bf16[16,16,128]{2,1,0:T(8,128)(2,1)}), bf16[16,16,128]{2,1,0:T(8,128)(2,1)S(1)}, u32[]{:S(2)}, u32[]{:S(2)}) %all-to-all-start.1) | async-done | bytes 65568 | tf_op jit(solution)/shard_map/all_to_all | solution.py:241
  30.7 0.6 broadcast_in_dim.33
  31.3 11.0 %all-to-all-start.2 = ((bf16[8,16,128]{2,1,0:T(8,128)(2,1)}), bf16[8,16,128]{2,1,0:T(8,128)(2,1)S(1)}, u32[]{:S(2)}, u32[]{:S(2)}) async-start(bf16[8,16,128]{2,1,0:T(8,128)(2,1)} %broadcast_in_dim.33), calls=%async_computation.2 | async-start | bytes 65536 | tf_op jit(solution)/shard_map/all_to_all | solution.py:241
  42.3 1.0 select_reduce_fusion
  43.3 13.0 %all-to-all-done.2 = bf16[8,16,128]{2,1,0:T(8,128)(2,1)S(1)} async-done(((bf16[8,16,128]{2,1,0:T(8,128)(2,1)}), bf16[8,16,128]{2,1,0:T(8,128)(2,1)S(1)}, u32[]{:S(2)}, u32[]{:S(2)}) %all-to-all-start.2) | async-done | bytes 32800 | tf_op jit(solution)/shard_map/all_to_all | solution.py:241
  56.3 4.4 %all-to-all-start = ((s32[16,1,8]{2,1,0:T(1,128)}), s32[16,1,8]{2,1,0:T(1,128)S(1)}, u32[]{:S(2)}, u32[]{:S(2)}) async-start(s32[16,1,8]{2,1,0:T(1,128)} %bitcast.22), calls=%async_computation | async-start | bytes 16384 | tf_op jit(solution)/shard_map/all_to_all | solution.py:241
  60.7 6.5 %all-to-all-done = s32[16,1,8]{2,1,0:T(1,128)S(1)} async-done(((s32[16,1,8]{2,1,0:T(1,128)}), s32[16,1,8]{2,1,0:T(1,128)S(1)}, u32[]{:S(2)}, u32[]{:S(2)}) %all-to-all-start) | async-done | bytes 544 | tf_op jit(solution)/shard_map/all_to_all | solution.py:241
  67.2 0.6 broadcast_in_dim.34
  67.9 3.7 %all-to-all-start.3 = ((bf16[16,16,128]{2,1,0:T(8,128)(2,1)}), bf16[16,16,128]{2,1,0:T(8,128)(2,1)S(1)}, u32[]{:S(2)}, u32[]{:S(2)}) async-start(bf16[16,16,128]{2,1,0:T(8,128)(2,1)} %broadcast_in_dim.34), calls=%async_computation.3 | async-start | bytes 131072 | tf_op jit(solution)/shard_map/all_to_all | solution.py:241
  71.5 0.8 fusion.2
  72.3 2.1 collective-permute-start.1
  74.4 3.4 collective-permute-start
  77.9 0.5 broadcast.135
  78.4 0.7 reduce.5
  79.1 0.1 reshape.159.asked
  79.2 1.0 all-to-all-done.3
  80.2 5.7 %all-gather.3.cloned.1.call-done = bf16[72,128,128]{2,1,0:T(8,128)(2,1)} async-done(((bf16[9,128,128]{2,1,0:T(8,128)(2,1)}), bf16[72,128,128]{2,1,0:T(8,128)(2,1)}) %all-gather.3.cloned.1.call-update) | async-done | bytes 2359312 | tf_op jit(solution)/shard_map/all_gather | solution.py:267
  85.9 1.7 copy-done.7
  87.6 2.1 shard_map.111
  89.7 2.0 copy-done.1
  91.7 6.1 %all-to-all-start.4 = ((bf16[16,8,128,128]{3,2,1,0:T(8,128)(2,1)}), bf16[16,8,128,128]{3,2,1,0:T(8,128)(2,1)}, u32[]{:S(2)}, u32[]{:S(2)}) async-start(bf16[16,8,128,128]{3,2,1,0:T(8,128)(2,1)} %copy-done.1), calls=%async_computation.5 | async-start | bytes 8388608 | tf_op jit(solution)/shard_map/all_to_all | solution.py:241
  97.8 0.0 reduce-scatter.3.cloned.1.call-start
  97.8 1.5 fusion.8
  99.3 0.1 pad_add_fusion.place
  99.4 30.1 %reduce-scatter.3.cloned.1.call-done = f32[576,128]{1,0:T(8,128)} async-done(((f32[576,512]{1,0:T(8,128)}), f32[576,128]{1,0:T(8,128)}) %reduce-scatter.3.cloned.1.call-update) | async-done | bytes 294928 | tf_op jit(solution)/shard_map/reduce_scatter | solution.py:298
  129.5 1.0 convert_element_type.4.g
  130.4 23.0 %all-to-all-done.4.arrived = bf16[16,8,128,128]{3,2,1,0:T(8,128)(2,1)} async-done(((bf16[16,8,128,128]{3,2,1,0:T(8,128)(2,1)}), bf16[16,8,128,128]{3,2,1,0:T(8,128)(2,1)}, u32[]{:S(2)}, u32[]{:S(2)}) %all-to-all-start.4) | async-done | bytes 4194336 | tf_op jit(solution)/shard_map/all_to_all | solution.py:241
  153.5 10.6 %shard_map.112 = (bf16[576,128]{1,0:T(8,128)(2,1)S(1)}, bf16[576,128]{1,0:T(8,128)(2,1)}, f32[704,128]{1,0:T(8,128)S(1)}, f32[704,128]{1,0:T(8,128)S(1)}, f32[25...) custom-call(s32[2]{0:T(128)S(1)} %pad_add_fusion.place, ...), custom_call_target="tpu_custom_call" | custom-call | flops 1073741824 | bytes 12582912 | tf_op jit(solution)/shard_map/pallas_call | solution.py:307
  164.1 2.0 copy-done.2
  166.1 11.4 %all-to-all-start.5 = ((bf16[16,8,128,128]{3,2,1,0:T(8,128)(2,1)}), bf16[16,8,128,128]{3,2,1,0:T(8,128)(2,1)}, u32[]{:S(2)}, u32[]{:S(2)}) async-start(bf16[16,8,128,128]{3,2,1,0:T(8,128)(2,1)} %copy-done.2), calls=%async_computation.6 | async-start | bytes 8388608 | tf_op jit(solution)/shard_map/all_to_all | solution.py:241
  177.5 5.3 %collective-permute-start.4 = (bf16[576,128]{1,0:T(8,128)(2,1)S(1)}, bf16[576,128]{1,0:T(8,128)(2,1)S(1)}, u32[]{:S(2)}, u32[]{:S(2)}) collective-permute-start(bf16[576,128]{1,0:T(8,128)(2,1)S(1)} %get-tuple-element.33), channel_id=1, source_target_pairs={{0,3},{1,0},{2,1},{3,2},{4,7},{5,4},{6,5},{7,6},{8,11},{9,8},{10,9... | collective-permute-start | bytes 442376 | tf_op jit(solution)/shard_map/ppermute | solution.py:329
  182.8 2.0 collective-permute-start.3
  184.8 2.4 collective-permute-start.2
  187.2 2.6 collective-permute-start.6
  189.9 3.4 collective-permute-start.5
  193.3 1.7 collective-permute-done.2
  195.2 0.4 convolution_multiply_fusion
  195.6 29.8 %collective-permute-done.6.from_right = bf16[128,128]{1,0:T(8,128)(2,1)S(1)} collective-permute-done((bf16[128,128]{1,0:T(8,128)(2,1)S(1)}, bf16[128,128]{1,0:T(8,128)(2,1)S(1)}, u32[]{:S(2)}, u32[]{:S(2)}) %collective-permute-start.6) | collective-permute-done | bytes 32800 | tf_op jit(solution)/shard_map/ppermute | solution.py:326
  225.4 7.8 %all-to-all-done.5.returned = bf16[16,8,128,128]{3,2,1,0:T(8,128)(2,1)} async-done(((bf16[16,8,128,128]{3,2,1,0:T(8,128)(2,1)}), bf16[16,8,128,128]{3,2,1,0:T(8,128)(2,1)}, u32[]{:S(2)}, u32[]{:S(2)}) %all-to-all-start.5) | async-done | bytes 4194336 | tf_op jit(solution)/shard_map/all_to_all | solution.py:241
  233.2 7.3 %shard_map.113 = bf16[8,9,128,128]{3,2,1,0:T(8,128)(2,1)} custom-call(s32[128]{0:T(128)S(1)} %reshape.159.asked, bf16[16,8,128,128]{3,2,1,0:T(8,128)(2,1)} %all-to-all-done.5.returned), custom_call_target="tpu_custom_call" | custom-call | bytes 10485760 | tf_op jit(solution)/shard_map/pallas_call | solution.py:343
  240.5 0.9 pad_maximum_fusion
  241.4 11.5 %all-to-all-start.6 = ((f32[16,80,128]{2,1,0:T(8,128)}), f32[16,80,128]{2,1,0:T(8,128)S(1)}, u32[]{:S(2)}, u32[]{:S(2)}) async-start(f32[16,80,128]{2,1,0:T(8,128)} %pad_maximum_fusion), calls=%async_computation.7 | async-start | bytes 1310720 | tf_op jit(solution)/shard_map/all_to_all | solution.py:241
  252.9 0.0 reduce-scatter.5.cloned.1.call-start
  252.9 0.7 reduce-scatter.5.cloned.1.call-update
  253.6 10.5 %all-to-all-done.6 = f32[16,80,128]{2,1,0:T(8,128)S(1)} async-done(((f32[16,80,128]{2,1,0:T(8,128)}), f32[16,80,128]{2,1,0:T(8,128)S(1)}, u32[]{:S(2)}, u32[]{:S(2)}) %all-to-all-start.6) | async-done | bytes 655392 | tf_op jit(solution)/shard_map/all_to_all | solution.py:241
  264.2 38.4 %all_to_all.49 = f32[8,80,128]{2,1,0:T(8,128)S(1)} all-to-all(f32[8,80,128]{2,1,0:T(8,128)S(1)} %broadcast_in_dim.35), channel_id=1, replica_groups=mesh['slab'=8,'lane'=16,'head'=4] {'slab'}, dimensions={0} | all-to-all | bytes 655360 | tf_op jit(solution)/shard_map/all_to_all | solution.py:241
  302.6 0.9 broadcast_in_dim.36
  303.5 8.2 %all-to-all-start.8 = ((f32[16,80,128]{2,1,0:T(8,128)}), f32[16,80,128]{2,1,0:T(8,128)S(1)}, u32[]{:S(2)}, u32[]{:S(2)}) async-start(f32[16,80,128]{2,1,0:T(8,128)} %broadcast_in_dim.36), calls=%async_computation.9 | async-start | bytes 1310720 | tf_op jit(solution)/shard_map/all_to_all | solution.py:241
  311.8 0.6 gather_fusion
  312.3 2.1 convolution_convert_fusion
  314.4 20.7 %all-to-all-done.8 = f32[16,80,128]{2,1,0:T(8,128)S(1)} async-done(((f32[16,80,128]{2,1,0:T(8,128)}), f32[16,80,128]{2,1,0:T(8,128)S(1)}, u32[]{:S(2)}, u32[]{:S(2)}) %all-to-all-start.8) | async-done | bytes 655392 | tf_op jit(solution)/shard_map/all_to_all | solution.py:241
  335.3 1.4 gather_fusion.1
  336.7 5.1 %reduce-scatter.5.cloned.1.call-done = bf16[1,9,128,128]{3,2,1,0:T(8,128)(2,1)} async-done(((bf16[8,9,128,128]{3,2,1,0:T(8,128)(2,1)}), bf16[1,9,128,128]{3,2,1,0:T(8,128)(2,1)}) %reduce-scatter.5.cloned.1.call-update) | async-done | bytes 294928 | tf_op jit(solution)/shard_map/reduce_scatter | solution.py:353
  341.8 1.0 copy-done.8
  342.8 3.2 shard_map.114
  (44 shorter events, 0.5 us)
Async XLA Ops:
  7.2 90.7 %copy-start = (bf16[576,256]{1,0:T(8,128)(2,1)S(1)}, bf16[576,256]{1,0:T(8,128)(2,1)}, u32[]{:S(2)}) copy-start(bf16[576,256]{1,0:T(8,128)(2,1)} %param.11) | copy-start | bytes 884740
  7.2 78.7 %all-gather.3.cloned.1.call-start = ((), (), s32[]{:S(2)}) async-start(), calls=%async_computation.13 | async-start | bytes 2654208 | tf_op jit(solution)/shard_map/all_gather | solution.py:267
  9.7 0.9 copy-start.3
  10.6 0.9 copy-start.5
  14.6 16.1 %all-to-all-start.1 = ((bf16[16,16,128]{2,1,0:T(8,128)(2,1)}), bf16[16,16,128]{2,1,0:T(8,128)(2,1)S(1)}, u32[]{:S(2)}, u32[]{:S(2)}) async-start(bf16[16,16,128]{2,1,0:T(8,128)(2,1)} %bitcast.7), calls=%async_computation.1 | async-start | bytes 131072 | tf_op jit(solution)/shard_map/all_to_all | solution.py:241
  31.3 25.0 %all-to-all-start.2 = ((bf16[8,16,128]{2,1,0:T(8,128)(2,1)}), bf16[8,16,128]{2,1,0:T(8,128)(2,1)S(1)}, u32[]{:S(2)}, u32[]{:S(2)}) async-start(bf16[8,16,128]{2,1,0:T(8,128)(2,1)} %broadcast_in_dim.33), calls=%async_computation.2 | async-start | bytes 65536 | tf_op jit(solution)/shard_map/all_to_all | solution.py:241
  56.3 10.9 %all-to-all-start = ((s32[16,1,8]{2,1,0:T(1,128)}), s32[16,1,8]{2,1,0:T(1,128)S(1)}, u32[]{:S(2)}, u32[]{:S(2)}) async-start(s32[16,1,8]{2,1,0:T(1,128)} %bitcast.22), calls=%async_computation | async-start | bytes 16384 | tf_op jit(solution)/shard_map/all_to_all | solution.py:241
  67.9 12.4 %all-to-all-start.3 = ((bf16[16,16,128]{2,1,0:T(8,128)(2,1)}), bf16[16,16,128]{2,1,0:T(8,128)(2,1)S(1)}, u32[]{:S(2)}, u32[]{:S(2)}) async-start(bf16[16,16,128]{2,1,0:T(8,128)(2,1)} %broadcast_in_dim.34), calls=%async_computation.3 | async-start | bytes 131072 | tf_op jit(solution)/shard_map/all_to_all | solution.py:241
  72.3 6.8 %collective-permute-start.1 = (bf16[128,128]{1,0:T(8,128)(2,1)S(1)}, bf16[128,128]{1,0:T(8,128)(2,1)S(1)}, u32[]{:S(2)}, u32[]{:S(2)}) collective-permute-start(bf16[128,128]{1,0:T(8,128)(2,1)S(1)} %get-tuple-element.53), channel_id=1, source_target_pairs={{4,0},{8,4},{12,8},{16,12},{20,16},{24,20},{28,24},{32,28},{36,32}... | collective-permute-start | bytes 98312 | tf_op jit(solution)/shard_map/ppermute | solution.py:280
  74.4 4.7 %collective-permute-start = (bf16[128,128]{1,0:T(8,128)(2,1)S(1)}, bf16[128,128]{1,0:T(8,128)(2,1)S(1)}, u32[]{:S(2)}, u32[]{:S(2)}) collective-permute-start(bf16[128,128]{1,0:T(8,128)(2,1)S(1)} %get-tuple-element.54), channel_id=1, source_target_pairs={{0,4},{4,8},{8,12},{12,16},{16,20},{20,24},{24,28},{28,32},{32,36}... | collective-permute-start | bytes 98312 | tf_op jit(solution)/shard_map/ppermute | solution.py:279
  85.9 1.7 copy-start.7
  89.7 2.0 copy-start.1
  91.7 6.2 %copy-start.10 = (bf16[512,256]{1,0:T(8,128)(2,1)S(1)}, bf16[512,256]{1,0:T(8,128)(2,1)}, u32[]{:S(2)}) copy-start(bf16[512,256]{1,0:T(8,128)(2,1)} %param.10) | copy-start | bytes 786436
  91.7 61.8 %copy-start.4 = (bf16[576,128]{1,0:T(8,128)(2,1)S(1)}, bf16[576,128]{1,0:T(8,128)(2,1)}, u32[]{:S(2)}) copy-start(bf16[576,128]{1,0:T(8,128)(2,1)} %value.3) | copy-start | bytes 442372
  91.7 61.8 %copy-start.6 = (bf16[576,128]{1,0:T(8,128)(2,1)S(1)}, bf16[576,128]{1,0:T(8,128)(2,1)}, u32[]{:S(2)}) copy-start(bf16[576,128]{1,0:T(8,128)(2,1)} %key.3) | copy-start | bytes 442372
  91.7 61.8 %copy-start.9 = (bf16[576,128]{1,0:T(8,128)(2,1)S(1)}, bf16[576,128]{1,0:T(8,128)(2,1)}, u32[]{:S(2)}) copy-start(bf16[576,128]{1,0:T(8,128)(2,1)} %q.1) | copy-start | bytes 442372
  91.7 61.8 %all-to-all-start.4 = ((bf16[16,8,128,128]{3,2,1,0:T(8,128)(2,1)}), bf16[16,8,128,128]{3,2,1,0:T(8,128)(2,1)}, u32[]{:S(2)}, u32[]{:S(2)}) async-start(bf16[16,8,128,128]{3,2,1,0:T(8,128)(2,1)} %copy-done.1), calls=%async_computation.5 | async-start | bytes 8388608 | tf_op jit(solution)/shard_map/all_to_all | solution.py:241
  97.8 31.7 %reduce-scatter.3.cloned.1.call-start = ((), (), s32[]{:S(2)}) async-start(), calls=%async_computation.11 | async-start | bytes 1474560 | tf_op jit(solution)/shard_map/reduce_scatter | solution.py:298
  164.1 2.0 copy-start.2
  166.1 67.1 %all-to-all-start.5 = ((bf16[16,8,128,128]{3,2,1,0:T(8,128)(2,1)}), bf16[16,8,128,128]{3,2,1,0:T(8,128)(2,1)}, u32[]{:S(2)}, u32[]{:S(2)}) async-start(bf16[16,8,128,128]{3,2,1,0:T(8,128)(2,1)} %copy-done.2), calls=%async_computation.6 | async-start | bytes 8388608 | tf_op jit(solution)/shard_map/all_to_all | solution.py:241
  177.5 17.6 %collective-permute-start.4 = (bf16[576,128]{1,0:T(8,128)(2,1)S(1)}, bf16[576,128]{1,0:T(8,128)(2,1)S(1)}, u32[]{:S(2)}, u32[]{:S(2)}) collective-permute-start(bf16[576,128]{1,0:T(8,128)(2,1)S(1)} %get-tuple-element.33), channel_id=1, source_target_pairs={{0,3},{1,0},{2,1},{3,2},{4,7},{5,4},{6,5},{7,6},{8,11},{9,8},{10,9... | collective-permute-start | bytes 442376 | tf_op jit(solution)/shard_map/ppermute | solution.py:329
  182.8 12.3 %collective-permute-start.3 = (bf16[576,128]{1,0:T(8,128)(2,1)S(1)}, bf16[576,128]{1,0:T(8,128)(2,1)S(1)}, u32[]{:S(2)}, u32[]{:S(2)}) collective-permute-start(bf16[576,128]{1,0:T(8,128)(2,1)S(1)} %get-tuple-element.33), channel_id=1, source_target_pairs={{0,2},{1,3},{2,0},{3,1},{4,6},{5,7},{6,4},{7,5},{8,10},{9,11},{10,... | collective-permute-start | bytes 442376 | tf_op jit(solution)/shard_map/ppermute | solution.py:329
  184.8 10.3 %collective-permute-start.2 = (bf16[576,128]{1,0:T(8,128)(2,1)S(1)}, bf16[576,128]{1,0:T(8,128)(2,1)S(1)}, u32[]{:S(2)}, u32[]{:S(2)}) collective-permute-start(bf16[576,128]{1,0:T(8,128)(2,1)S(1)} %get-tuple-element.33), channel_id=1, source_target_pairs={{0,1},{1,2},{2,3},{3,0},{4,5},{5,6},{6,7},{7,4},{8,9},{9,10},{10,1... | collective-permute-start | bytes 442376 | tf_op jit(solution)/shard_map/ppermute | solution.py:329
  187.2 38.2 %collective-permute-start.6 = (bf16[128,128]{1,0:T(8,128)(2,1)S(1)}, bf16[128,128]{1,0:T(8,128)(2,1)S(1)}, u32[]{:S(2)}, u32[]{:S(2)}) collective-permute-start(bf16[128,128]{1,0:T(8,128)(2,1)S(1)} %get-tuple-element.55), channel_id=1, source_target_pairs={{4,0},{8,4},{12,8},{16,12},{20,16},{24,20},{28,24},{32,28},{36,32}... | collective-permute-start | bytes 98312 | tf_op jit(solution)/shard_map/ppermute | solution.py:326
  189.9 35.5 %collective-permute-start.5 = (bf16[128,128]{1,0:T(8,128)(2,1)S(1)}, bf16[128,128]{1,0:T(8,128)(2,1)S(1)}, u32[]{:S(2)}, u32[]{:S(2)}) collective-permute-start(bf16[128,128]{1,0:T(8,128)(2,1)S(1)} %get-tuple-element.56), channel_id=1, source_target_pairs={{0,4},{4,8},{8,12},{12,16},{16,20},{20,24},{24,28},{28,32},{32,36}... | collective-permute-start | bytes 98312 | tf_op jit(solution)/shard_map/ppermute | solution.py:325
  195.2 45.3 %copy-start.11 = (bf16[576,512]{1,0:T(8,128)(2,1)}, bf16[576,512]{1,0:T(8,128)(2,1)S(1)}, u32[]{:S(2)}) copy-start(bf16[576,512]{1,0:T(8,128)(2,1)S(1)} %constant_dynamic-update-slice_fusion) | copy-start | bytes 1769476
  241.4 22.7 %all-to-all-start.6 = ((f32[16,80,128]{2,1,0:T(8,128)}), f32[16,80,128]{2,1,0:T(8,128)S(1)}, u32[]{:S(2)}, u32[]{:S(2)}) async-start(f32[16,80,128]{2,1,0:T(8,128)} %pad_maximum_fusion), calls=%async_computation.7 | async-start | bytes 1310720 | tf_op jit(solution)/shard_map/all_to_all | solution.py:241
  252.9 88.9 %reduce-scatter.5.cloned.1.call-start = ((), (), s32[]{:S(2)}) async-start(), calls=%async_computation.12 | async-start | bytes 2654208 | tf_op jit(solution)/shard_map/reduce_scatter | solution.py:353
  303.5 31.7 %all-to-all-start.8 = ((f32[16,80,128]{2,1,0:T(8,128)}), f32[16,80,128]{2,1,0:T(8,128)S(1)}, u32[]{:S(2)}, u32[]{:S(2)}) async-start(f32[16,80,128]{2,1,0:T(8,128)} %broadcast_in_dim.36), calls=%async_computation.9 | async-start | bytes 1310720 | tf_op jit(solution)/shard_map/all_to_all | solution.py:241
  341.8 1.0 copy-start.8
Sparse Core Ops, SparseCore 0:
  10.7 75.1 all-gather.2
  101.5 27.9 reduce-scatter.2
  256.6 85.1 reduce-scatter.4

commit v4 on v3

v4 whole, which is shorter than its diff:
```python
import math

import jax
import jax.numpy as jnp
from jax import lax
from jax.experimental import pallas as pl
from jax.experimental.pallas import tpu as pltpu
from jax.sharding import Mesh
from jax.sharding import PartitionSpec as P

HEAD_DIM = 64
BLOCK = 64
PAIR = 2 * BLOCK
LANES = 8
TILE = 16
PANEL = 2
FEW = 10
R = 3
GLOBALS = 128
VMEM_LIMIT = 40 * 1024 * 1024


def whole(space=pltpu.VMEM):
    return pl.BlockSpec(memory_space=space)


def shape(dims, dtype):
    return jax.ShapeDtypeStruct(dims, dtype)


def call(kernel, out_shape, in_specs, scratch=(), flops=0, moved=0):
    return pl.pallas_call(
        kernel,
        out_shape=out_shape,
        in_specs=in_specs,
        out_specs=jax.tree.map(lambda _: whole(), out_shape),
        scratch_shapes=list(scratch),
        compiler_params=pltpu.CompilerParams(vmem_limit_bytes=VMEM_LIMIT),
        cost_estimate=pl.CostEstimate(flops=flops, bytes_accessed=moved, transcendentals=0),
    )


def serve_kernel(where, asked, global_pos, lane_blocks, send, panel):
    me, blocks = where[0], where[1]
    tokens = blocks * BLOCK
    most = asked.shape[0] // LANES
    slots = send.shape[1] - PANEL

    def serve(number, carry):
        to = number // slots
        rank = number % slots
        send[to, rank] = lane_blocks[jnp.maximum(asked[to * most + rank], 0)]
        return carry

    lax.fori_loop(0, LANES * slots, serve, 0)

    panel[...] = jnp.zeros_like(panel)
    row_number = lax.broadcasted_iota(jnp.int32, (TILE, panel.shape[1]), 0)

    def pick(number, carry):
        position = global_pos[number]
        owner = position // tokens
        row = position % tokens

        @pl.when(owner % LANES == me)
        def _():
            source = owner // LANES * blocks + row // BLOCK
            inside = row % BLOCK
            first = pl.multiple_of(inside // TILE * TILE, TILE)
            hit = row_number == inside % TILE
            for half in range(2):
                rows = lane_blocks[source, pl.ds(first + half * BLOCK, TILE), :]
                panel[pl.ds(number + half * GLOBALS, 1), :] = jnp.sum(
                    jnp.where(hit, rows.astype(jnp.float32), 0.0), axis=0, keepdims=True
                )

        return carry

    lax.fori_loop(0, GLOBALS, pick, 0)
    panel_rows = panel[...].astype(send.dtype).reshape(PANEL, PAIR, panel.shape[1])
    for to in range(LANES):
        send[to, slots:] = panel_rows


def attention_kernel(
    place,
    names,
    ranks,
    q,
    g,
    key,
    value,
    left,
    right,
    arrived,
    attended,
    query_grad,
    key_grad,
    value_grad,
    rims,
    send,
    key_pad,
    value_pad,
    panel,
    panel_grad,
):
    tokens, columns = q.shape
    blocks = tokens // BLOCK
    scale = 1.0 / math.sqrt(HEAD_DIM)
    f32, bf16 = jnp.float32, jnp.bfloat16
    key_pad[:BLOCK, :] = left[:BLOCK, :]
    value_pad[:BLOCK, :] = left[BLOCK:, :]
    key_pad[BLOCK : BLOCK + tokens, :] = key[...]
    value_pad[BLOCK : BLOCK + tokens, :] = value[...]
    key_pad[BLOCK + tokens :, :] = right[:BLOCK, :]
    value_pad[BLOCK + tokens :, :] = right[BLOCK:, :]
    slots = arrived.shape[1] - PANEL
    panel_sum = jnp.zeros((PANEL, PAIR, columns), f32)
    for lane in range(LANES):
        panel_sum += arrived[lane, slots:].astype(f32)
    panel[...] = panel_sum.reshape(panel.shape).astype(bf16)
    key_grad[...] = jnp.zeros_like(key_grad)
    value_grad[...] = jnp.zeros_like(value_grad)
    panel_grad[...] = jnp.zeros_like(panel_grad)
    first_block, last_block = place[0], place[1]
    first_head = lax.broadcasted_iota(jnp.int32, (BLOCK, columns), 1) < HEAD_DIM
    window = 3 * BLOCK
    keys = window + GLOBALS + R * BLOCK
    key_column = lax.broadcasted_iota(jnp.int32, (1, keys), 1)

    def by_head(rows):
        zero = jnp.zeros_like(rows)
        return jnp.concatenate(
            [jnp.where(first_head, rows, zero), jnp.where(first_head, zero, rows)], axis=0
        )

    def joined(pair):
        return jnp.where(first_head, pair[:BLOCK], pair[BLOCK:])

    def dot(a, b, dims):
        return lax.dot_general(a, b, (dims, ((), ())), preferred_element_type=f32)

    def one(block, carry):
        row = pl.multiple_of(block * BLOCK, BLOCK)
        here = pl.ds(row, BLOCK)
        around = pl.ds(row, window)
        named = [block * R + j for j in range(R)]
        places = [(names[n] // blocks % LANES, ranks[n]) for n in named]
        kk = jnp.concatenate(
            [key_pad[around, :], panel[:GLOBALS, :]] + [arrived[a, b, :BLOCK, :] for a, b in places], axis=0
        )
        vv = jnp.concatenate(
            [value_pad[around, :], panel[GLOBALS:, :]] + [arrived[a, b, BLOCK:, :] for a, b in places], axis=0
        )
        q2 = by_head(q[here, :])
        g2 = by_head(g[here, :])
        number = first_block + block
        dead = ((key_column < BLOCK) & (number == 0)) | (
            (key_column >= 2 * BLOCK) & (key_column < window) & (number == last_block)
        )
        scores = dot(q2, kk, ((1,), (1,))) * scale
        scores = jnp.where(dead, -jnp.inf, scores)
        top = jnp.max(scores, axis=-1, keepdims=True)
        raised = jnp.exp(scores - top)
        probs = raised * (1.0 / jnp.sum(raised, axis=-1, keepdims=True))
        probs_b = probs.astype(bf16)
        att = joined(dot(probs_b, vv, ((1,), (0,)))).astype(bf16)
        attended[here, :] = att
        att_f = att.astype(f32)
        delta = jnp.sum(
            g2.astype(f32) * jnp.concatenate([att_f, att_f], axis=0), axis=-1, keepdims=True
        )
        slope = (probs * (dot(g2, vv, ((1,), (1,))) - delta)).astype(bf16)
        query_grad[here, :] = (scale * joined(dot(slope, kk, ((1,), (0,))))).astype(bf16)
        dk = scale * dot(slope, q2, ((0,), (0,)))
        dv = dot(probs_b, g2, ((0,), (0,)))
        key_grad[around, :] += dk[:window]
        value_grad[around, :] += dv[:window]
        panel_grad[:GLOBALS, :] += dk[window : window + GLOBALS]
        panel_grad[GLOBALS:, :] += dv[window : window + GLOBALS]
        for j, (a, b) in enumerate(places):
            first = window + GLOBALS + j * BLOCK
            send[a, b, :BLOCK, :] = dk[first : first + BLOCK].astype(bf16)
            send[a, b, BLOCK:, :] = dv[first : first + BLOCK].astype(bf16)
        return carry

    lax.fori_loop(0, blocks, one, 0)
    for side, rows in enumerate((pl.ds(0, BLOCK), pl.ds(BLOCK + tokens, BLOCK))):
        rims[side, :BLOCK, :] = key_grad[rows, :].astype(bf16)
        rims[side, BLOCK:, :] = value_grad[rows, :].astype(bf16)
    panel_rows = panel_grad[...].astype(bf16).reshape(PANEL, PAIR, columns)
    for lane in range(LANES):
        send[lane, slots:] = panel_rows


def collect_kernel(where, asked, global_pos, returned, lane_grads, sums, panel):
    me, blocks = where[0], where[1]
    tokens = blocks * BLOCK
    most = asked.shape[0] // LANES
    slots = returned.shape[1] - PANEL
    f32 = jnp.float32
    sums[...] = jnp.zeros_like(sums)

    def add(number, carry):
        source = number // slots
        rank = number % slots
        wanted = asked[source * most + rank]

        @pl.when(wanted >= 0)
        def _():
            sums[wanted] += returned[source, rank].astype(f32)

        return carry

    lax.fori_loop(0, LANES * slots, add, 0)
    total_rows = jnp.zeros((PANEL, PAIR, panel.shape[1]), f32)
    for lane in range(LANES):
        total_rows += returned[lane, slots:].astype(f32)
    panel[...] = total_rows.reshape(panel.shape)

    def spread(number, carry):
        position = global_pos[number]
        owner = position // tokens
        row = position % tokens

        @pl.when(owner % LANES == me)
        def _():
            to = owner // LANES * blocks + row // BLOCK
            for half in range(2):
                sums[to, pl.ds(row % BLOCK + half * BLOCK, 1), :] += panel[
                    pl.ds(number + half * GLOBALS, 1), :
                ]

        return carry

    lax.fori_loop(0, GLOBALS, spread, 0)

    def write(number, carry):
        lane_grads[number] = sums[number].astype(lane_grads.dtype)
        return carry

    lax.fori_loop(0, lane_grads.shape[0], write, 0)


def finish_kernel(
    key_grad,
    value_grad,
    from_left,
    from_right,
    others,
    key_out,
    value_out,
    key_sum,
    value_sum,
):
    tokens = key_out.shape[0]
    f32 = jnp.float32

    def own(block, carry):
        row = pl.multiple_of(block * BLOCK, BLOCK)
        here, padded = pl.ds(row, BLOCK), pl.ds(row + BLOCK, BLOCK)
        key_sum[here, :] = key_grad[padded, :] + others[block, :BLOCK, :].astype(f32)
        value_sum[here, :] = value_grad[padded, :] + others[block, BLOCK:, :].astype(f32)
        return carry

    lax.fori_loop(0, others.shape[0], own, 0)
    key_sum[:BLOCK, :] += from_left[:BLOCK, :].astype(f32)
    value_sum[:BLOCK, :] += from_left[BLOCK:, :].astype(f32)
    key_sum[tokens - BLOCK :, :] += from_right[:BLOCK, :].astype(f32)
    value_sum[tokens - BLOCK :, :] += from_right[BLOCK:, :].astype(f32)

    key_out[...] = key_sum[...].astype(key_out.dtype)
    value_out[...] = value_sum[...].astype(value_out.dtype)


def exchange(array, axis):
    return lax.all_to_all(array, axis, split_axis=0, concat_axis=0, tiled=True)


def spread(array, axis):
    return exchange(jnp.broadcast_to(array, (lax.axis_size(axis),) + array.shape), axis)


def shards(queries, key_states, value_states, out_weight, output_grad, rand_blocks, global_pos):
    bf16, f32 = jnp.bfloat16, jnp.float32
    tokens, columns = queries.shape
    blocks = tokens // BLOCK
    slabs, heads = lax.axis_size("slab"), lax.axis_size("head")
    slab, me, head = lax.axis_index("slab"), lax.axis_index("lane"), lax.axis_index("head")
    position, seq_count = slab * LANES + me, slabs * LANES
    smem, vmem = whole(pltpu.SMEM), whole()
    where = jnp.stack([me, jnp.int32(blocks)]).astype(jnp.int32)

    own = jnp.concatenate(
        [key_states.reshape(blocks, BLOCK, columns), value_states.reshape(blocks, BLOCK, columns)],
        axis=1,
    )
    lane_blocks = lax.all_gather(own, "slab", axis=0, tiled=True)

    names = rand_blocks.reshape(-1)
    owner = names // blocks
    lane, code = owner % LANES, owner // LANES * blocks + names % blocks
    number = jnp.arange(names.shape[0])
    same = (lane[:, None] == lane[None, :]) & (number[None, :] < number[:, None])
    ranks = jnp.sum(same.astype(jnp.int32), axis=1)
    index = jnp.arange(LANES * slabs)
    hit = (lane * slabs + ranks)[None, :] == index[:, None]
    wanted = jnp.max(jnp.where(hit, code[None, :], -1), axis=1).reshape(LANES, slabs)
    load = jnp.broadcast_to(jnp.max(ranks) + 1, (LANES, 1))
    heard = exchange(jnp.concatenate([wanted, load], axis=1), "lane")
    asked = heard[:, :slabs].reshape(-1)
    load = jnp.max(spread(jnp.max(heard[:, slabs:]).reshape(1), "slab"))

    partial_grad = lax.dot_general(
        output_grad, out_weight, (((1,), (1,)), ((), ())), preferred_element_type=f32
    )
    partial_grad = partial_grad.reshape(tokens, heads, columns).transpose(1, 0, 2)
    grad_att = jnp.sum(exchange(partial_grad, "head"), axis=0).astype(bf16)

    seq = ("slab", "lane")
    forth = [(i, i + 1) for i in range(seq_count - 1)]
    back = [(i + 1, i) for i in range(seq_count - 1)]
    left = lax.ppermute(own[blocks - 1], seq, forth)
    right = lax.ppermute(own[0], seq, back)

    order = (head - jnp.arange(heads)) % heads
    weight_rows = out_weight.reshape(heads, columns, -1).at[order].get(mode="promise_in_bounds")
    weight_rows = weight_rows.reshape(out_weight.shape)
    lane_blocks, asked, load, grad_att, left, right, weight_rows = lax.optimization_barrier(
        (lane_blocks, asked, load, grad_att, left, right, weight_rows)
    )
    place = jnp.stack([position * blocks, seq_count * blocks - 1]).astype(jnp.int32)
    padded = tokens + PAIR

    def middle(slots):
        slots += PANEL
        served = call(
            serve_kernel,
            shape((LANES, slots, PAIR, columns), bf16),
            [smem, smem, smem, vmem],
            [pltpu.VMEM((2 * GLOBALS, columns), f32)],
            moved=8 << 20,
        )(where, asked, global_pos, lane_blocks)
        arrived = exchange(served, "lane")
        attended, query_grad, key_part, value_part, rims, sent = call(
            attention_kernel,
            (
                shape((tokens, columns), bf16),
                shape((tokens, columns), bf16),
                shape((padded, columns), f32),
                shape((padded, columns), f32),
                shape((2, PAIR, columns), bf16),
                shape((LANES, slots, PAIR, columns), bf16),
            ),
            [smem, smem, smem] + [vmem] * 7,
            [pltpu.VMEM((padded, columns), bf16)] * 2
            + [
                pltpu.VMEM((2 * GLOBALS, columns), bf16),
                pltpu.VMEM((2 * GLOBALS, columns), f32),
            ],
            flops=1 << 30,
            moved=12 << 20,
        )(place, names, ranks, queries, grad_att, key_states, value_states, left, right, arrived)
        returned = exchange(sent, "lane")

        pieces = [attended] + [
            lax.ppermute(attended, "head", [(i, (i + k) % heads) for i in range(heads)])
            for k in range(1, heads)
        ]
        from_left = lax.ppermute(rims[1], seq, forth)
        from_right = lax.ppermute(rims[0], seq, back)
        everywhere = jnp.concatenate(pieces, axis=1)
        weight_part = lax.dot_general(
            everywhere, output_grad, (((0,), (0,)), ((), ())), preferred_element_type=f32
        ) * (1.0 / math.sqrt(tokens * seq_count))
        weight_part = weight_part.reshape(LANES, -1, weight_part.shape[1])
        step = LANES // 2
        while step:
            pair = weight_part.reshape((2, step) + weight_part.shape[1:])
            mine = me // step % 2
            kept = lax.dynamic_index_in_dim(pair, mine, 0, keepdims=False)
            other = lax.dynamic_index_in_dim(pair, 1 - mine, 0, keepdims=False)
            other = lax.ppermute(other, "lane", [(i, i ^ step) for i in range(LANES)])
            weight_part = kept + other
            step //= 2
        returned, from_left, from_right, weight_part = lax.optimization_barrier(
            (returned, from_left, from_right, weight_part)
        )
        lane_grads = call(
            collect_kernel,
            shape((slabs * blocks, PAIR, columns), bf16),
            [smem, smem, smem, vmem],
            [
                pltpu.VMEM((slabs * blocks, PAIR, columns), f32),
                pltpu.VMEM((2 * GLOBALS, columns), f32),
            ],
            moved=10 << 20,
        )(where, asked, global_pos, returned)
        return (
            everywhere,
            query_grad,
            key_part,
            value_part,
            from_left,
            from_right,
            weight_part,
            lane_grads,
        )

    few = lambda: middle(FEW)
    all_slots = lambda: middle(slabs)
    everywhere, query_grad, key_part, value_part, from_left, from_right, weight_part, lane_grads = (
        lax.cond(load <= FEW, few, all_slots) if FEW < slabs else all_slots()
    )
    others = lax.psum_scatter(lane_grads, "slab", scatter_dimension=0, tiled=True)

    features = weight_part.shape[-1]
    share = jnp.sum(exchange(weight_part.reshape(slabs, -1, features), "slab"), axis=0)
    share = spread(share, "slab").reshape(-1, features)
    weight_grad = spread(share, "lane").reshape(heads, columns, features)
    weight_grad = weight_grad.at[order].get(mode="promise_in_bounds")
    weight_grad = weight_grad.reshape(heads * columns, features)

    projected = jnp.dot(everywhere, weight_rows, preferred_element_type=f32).astype(bf16)
    key_grad, value_grad = call(
        finish_kernel,
        (shape((tokens, columns), bf16), shape((tokens, columns), bf16)),
        [vmem] * 5,
        [pltpu.VMEM((tokens, columns), f32)] * 2,
        moved=2 << 20,
    )(key_part, value_part, from_left, from_right, others)
    return projected, query_grad, key_grad, value_grad, weight_grad


def solution(mesh):
    seq_count, head_count = mesh.devices.shape
    fine = Mesh(
        mesh.devices.reshape(seq_count // LANES, LANES, head_count), ("slab", "lane", "head")
    )
    seq = ("slab", "lane")
    placed = (
        P(seq, "head"),
        P(seq, "head"),
        P(seq, "head"),
        P(None, "head"),
        P(seq, "head"),
        P(seq, None),
        P(),
    )
    return jax.shard_map(
        shards,
        mesh=fine,
        in_specs=placed,
        out_specs=(
            P(seq, "head"),
            P(seq, "head"),
            P(seq, "head"),
            P(seq, "head"),
            P(None, "head"),
        ),
        check_vma=False,
    )
```

time: 357 us -> 331 us (0.927)
  the two profiles are of different devices: /device:TPU:1 before, /device:TPU:10 now
where the time goes in v4:
time: 331 us; the launch traced here: 330 us
  waiting for transfers between devices  104 us (31%)
  blocking collectives  85.5 us (26%)
  starting transfers between devices  64.1 us (19%)
  Pallas kernels  30 us (9%)
  local copies, waits for them, and re-layouts  18.6 us (6%)
  between operations  15.5 us (5%)
  other arithmetic  6.93 us (2%)
  matrix products  4.96 us (1%)
    all_to_all x4, blocking collectives, exchange(): return lax.all_to_all(array, axis, split_axis=0, concat_axis=0, tiled=True)  85.5 us
    all_to_all x4, starting transfers between devices, exchange(): return lax.all_to_all(array, axis, split_axis=0, concat_axis=0, tiled=True)  35.1 us
    all_gather x1, waiting for transfers between devices, shards(): lane_blocks = lax.all_gather(own, 'slab', axis=0, tiled=True)  27 us
    reduce_scatter x1, waiting for transfers between devices, shards(): lax.psum_scatter(lane_grads, 'slab', scatter_dimension=0, tiled=True)  24.9 us
    all_to_all x4, waiting for transfers between devices, exchange(): return lax.all_to_all(array, axis, split_axis=0, concat_axis=0, tiled=True)  23.8 us
    ppermute x3, waiting for transfers between devices, middle(): other = lax.ppermute(other, 'lane', [(i, i ^ step) for i in range(LANES)])  23.1 us
    pallas_call x1, Pallas kernels, middle(): call(collect_kernel, shape((slabs * blocks, PAIR, columns), bf16), [smem,...  10.7 us
    ppermute x3, starting transfers between devices, middle(): lax.ppermute(attended, 'head', [(i, (i + k) % heads) for i in range(heads)])  10.1 us
  transfers between devices with their start and end apart: 16, of which 9 were waited for; matrix products, arithmetic and copies ran while one was open for 7% of the time, Pallas kernels for 0%

profile of v4, /device:TPU:10, one launch (start us, length us, event | category | flops | bytes accessed | tf_op | source)
XLA Modules:
  0.0 330.0 jit_solution(11941221482784441802)
XLA Ops:
  7.3 1.8 pad_maximum_fusion
  9.1 0.8 copy.20
  9.9 0.1 reshape.222
  10.0 0.2 convert_reduce_fusion
  10.2 0.6 fusion.8
  10.8 0.1 select_reduce_fusion
  11.7 8.5 %all_to_all.56 = s32[8,1,17]{2,1,0:T(1,128)S(1)} all-to-all(s32[8,1,17]{2,1,0:T(1,128)S(1)} %bitcast.81), channel_id=1, replica_groups=mesh['slab'=16,'lane'=8,'head'=4] {'lane'}, dimensions={0} | all-to-all | bytes 1088 | tf_op jit(solution)/shard_map/all_to_all | solution.py:277
  20.2 0.7 slice_reduce_fusion
  20.9 1.2 broadcast_in_dim.20
  22.1 15.2 %all-to-all-start.5 = ((s32[16,1,1]{2,1,0:T(1,128)}), s32[16,1,1]{2,1,0:T(1,128)S(1)}, u32[]{:S(2)}, u32[]{:S(2)}) async-start(s32[16,1,1]{2,1,0:T(1,128)} %broadcast_in_dim.20), calls=%async_computation.5 | async-start | bytes 16384 | tf_op jit(solution)/shard_map/all_to_all | solution.py:277
  37.4 1.3 convolution_bitcast_fusion
  38.7 1.1 copy.27
  39.8 10.0 %all-to-all-done.5 = s32[16,1,1]{2,1,0:T(1,128)S(1)} async-done(((s32[16,1,1]{2,1,0:T(1,128)}), s32[16,1,1]{2,1,0:T(1,128)S(1)}, u32[]{:S(2)}, u32[]{:S(2)}) %all-to-all-start.5) | async-done | bytes 96 | tf_op jit(solution)/shard_map/all_to_all | solution.py:277
  49.8 4.9 %all-to-all-start.6 = ((f32[4,576,128]{2,1,0:T(8,128)}), f32[4,576,128]{2,1,0:T(8,128)S(1)}, u32[]{:S(2)}, u32[]{:S(2)}) async-start(f32[4,576,128]{2,1,0:T(8,128)} %bitcast.61), calls=%async_computation.6 | async-start | bytes 2359296 | tf_op jit(solution)/shard_map/all_to_all | solution.py:277
  54.7 1.9 collective-permute-start.17
  56.6 2.4 collective-permute-start.16
  59.2 1.3 gather_fusion
  60.5 0.7 reduce_max.39
  61.2 7.0 %all-to-all-done.6 = f32[4,576,128]{2,1,0:T(8,128)S(1)} async-done(((f32[4,576,128]{2,1,0:T(8,128)}), f32[4,576,128]{2,1,0:T(8,128)S(1)}, u32[]{:S(2)}, u32[]{:S(2)}) %all-to-all-start.6) | async-done | bytes 1179680 | tf_op jit(solution)/shard_map/all_to_all | solution.py:277
  68.3 27.0 %all-gather.2.cloned.1.call-done = bf16[144,128,128]{2,1,0:T(8,128)(2,1)} async-done(((bf16[9,128,128]{2,1,0:T(8,128)(2,1)}), bf16[144,128,128]{2,1,0:T(8,128)(2,1)}) %all-gather.2.cloned.1.call-update) | async-done | bytes 4718608 | tf_op jit(solution)/shard_map/all_gather | solution.py:298
  96.0 142.2 %conditional.1 = (bf16[576,512]{1,0:T(8,128)(2,1)}, bf16[576,128]{1,0:T(8,128)(2,1)}, f32[704,128]{1,0:T(8,128)}, f32[704,128]{1,0:T(8,128)}, bf16[128,128]{1,0:...) conditional(s32[]{:T(128)} %convert_element_type.14, ...), branch_computations={%region_6.7_spmd, %region_7.8_spmd} | conditional | flops 1224982528 | bytes 82805920 | solution.py:413
  96.0 8.2 %branch_1_fun.3 = bf16[8,12,128,128]{3,2,1,0:T(8,128)(2,1)S(1)} custom-call(s32[2]{0:T(128)S(1)} %get-tuple-element.94.where, s32[128]{0:T(128)S(1)} %get-tuple-element.95.asked, s32[128]{0:T(128)S(1)} %get-tuple-element.96.global_pos, bf16[144,128,128]{2,1,0:T(8,128)(2,1)} %get-tuple-element.97.lane_blocks), custom_call_target="tpu_custom_call" | custom-call | bytes 8388608 | tf_op jit(solution)/shard_map/cond/branch_1_fun/pallas_call | solution.py:337
  104.2 42.0 %all_to_all.55.arrived = bf16[8,12,128,128]{3,2,1,0:T(8,128)(2,1)S(1)} all-to-all(bf16[8,12,128,128]{3,2,1,0:T(8,128)(2,1)S(1)} %branch_1_fun.3), channel_id=1, replica_groups=mesh['slab'=16,'lane'=8,'head'=4] {'lane'}, dimensions={0} | all-to-all | bytes 6291456 | tf_op jit(solution)/shard_map/cond/branch_1_fun/all_to_all | solution.py:277
  146.2 9.2 %branch_1_fun.4 = (bf16[576,128]{1,0:T(8,128)(2,1)S(1)}, bf16[576,128]{1,0:T(8,128)(2,1)}, f32[704,128]{1,0:T(8,128)}, f32[704,128]{1,0:T(8,128)}, bf16[2,128,12...) custom-call(s32[2]{0:T(128)S(1)} %get-tuple-element.85.place, s32[27]{0:T(128)S(1)} %get-tuple-element.86.names, ...), custom_call_target="tpu_custom_call" | custom-call | flops 1073741824 | bytes 12582912 | tf_op jit(solution)/shard_map/cond/branch_1_fun/pallas_call | solution.py:345
  155.5 1.7 copy-done.2
  157.1 0.6 copy-done.4
  157.7 5.0 %all-to-all-start.3 = ((bf16[8,12,128,128]{3,2,1,0:T(8,128)(2,1)}), bf16[8,12,128,128]{3,2,1,0:T(8,128)(2,1)S(1)}, u32[]{:S(2)}, u32[]{:S(2)}) async-start(bf16[8,12,128,128]{3,2,1,0:T(8,128)(2,1)} %copy-done.2), calls=%async_computation.3 | async-start | bytes 6291456 | tf_op jit(solution)/shard_map/cond/branch_1_fun/all_to_all | solution.py:277
  162.8 3.3 %collective-permute-start.8 = (bf16[576,128]{1,0:T(8,128)(2,1)S(1)}, bf16[576,128]{1,0:T(8,128)(2,1)}, u32[]{:S(2)}, u32[]{:S(2)}) collective-permute-start(bf16[576,128]{1,0:T(8,128)(2,1)S(1)} %get-tuple-element.98), channel_id=1, source_target_pairs={{0,1},{1,2},{2,3},{3,0},{4,5},{5,6},{6,7},{7,4},{8,9},{9,10},{10,1... | collective-permute-start | bytes 442376 | tf_op jit(solution)/shard_map/cond/branch_1_fun/ppermute | solution.py:367
  166.2 2.5 collective-permute-start.10
  168.7 4.2 %collective-permute-start.9 = (bf16[576,128]{1,0:T(8,128)(2,1)S(1)}, bf16[576,128]{1,0:T(8,128)(2,1)S(1)}, u32[]{:S(2)}, u32[]{:S(2)}) collective-permute-start(bf16[576,128]{1,0:T(8,128)(2,1)S(1)} %get-tuple-element.98), channel_id=1, source_target_pairs={{0,2},{1,3},{2,0},{3,1},{4,6},{5,7},{6,4},{7,5},{8,10},{9,11},{10,... | collective-permute-start | bytes 442376 | tf_op jit(solution)/shard_map/cond/branch_1_fun/ppermute | solution.py:367
  172.9 0.7 constant_dynamic-update-slice_fusion.7
  173.6 1.6 constant_dynamic-update-slice_fusion.6
  175.2 2.5 collective-permute-done.9
  177.7 0.7 constant_dynamic-update-slice_fusion.5
  178.4 0.7 constant_dynamic-update-slice_fusion.4
  179.1 1.5 convolution_multiply_fusion.1
  180.6 0.8 copy-done.9
  181.4 0.7 dynamic-slice_bitcast_fusion.2
  182.2 4.0 %collective-permute-start.13 = (f32[4,64,256]{2,1,0:T(8,128)}, f32[4,64,256]{2,1,0:T(8,128)}, u32[]{:S(2)}, u32[]{:S(2)}) collective-permute-start(f32[4,64,256]{2,1,0:T(8,128)} %dynamic-slice_bitcast_fusion.2), channel_id=1, source_target_pairs={{0,16},{4,20},{8,24},{12,28},{16,0},{20,4},{24,8},{28,12},{1,17},{... | collective-permute-start | bytes 786440 | tf_op jit(solution)/shard_map/cond/branch_1_fun/ppermute | solution.py:383
  186.2 19.3 %collective-permute-done.13 = f32[4,64,256]{2,1,0:T(8,128)} collective-permute-done((f32[4,64,256]{2,1,0:T(8,128)}, f32[4,64,256]{2,1,0:T(8,128)}, u32[]{:S(2)}, u32[]{:S(2)}) %collective-permute-start.13) | collective-permute-done | bytes 262176 | tf_op jit(solution)/shard_map/cond/branch_1_fun/ppermute | solution.py:383
  205.5 1.1 bitcast_add_fusion.2
  206.6 0.7 copy-done.8
  207.3 0.7 dynamic-slice_bitcast_fusion.3
  208.0 3.3 %collective-permute-start.14 = (f32[2,64,256]{2,1,0:T(8,128)}, f32[2,64,256]{2,1,0:T(8,128)S(1)}, u32[]{:S(2)}, u32[]{:S(2)}) collective-permute-start(f32[2,64,256]{2,1,0:T(8,128)} %dynamic-slice_bitcast_fusion.3), channel_id=1, source_target_pairs={{0,8},{4,12},{8,0},{12,4},{16,24},{20,28},{24,16},{28,20},{1,9},{5... | collective-permute-start | bytes 393224 | tf_op jit(solution)/shard_map/cond/branch_1_fun/ppermute | solution.py:383
  211.3 3.8 %collective-permute-done.14 = f32[2,64,256]{2,1,0:T(8,128)S(1)} collective-permute-done((f32[2,64,256]{2,1,0:T(8,128)}, f32[2,64,256]{2,1,0:T(8,128)S(1)}, u32[]{:S(2)}, u32[]{:S(2)}) %collective-permute-start.14) | collective-permute-done | bytes 131104 | tf_op jit(solution)/shard_map/cond/branch_1_fun/ppermute | solution.py:383
  215.1 0.9 bitcast_add_fusion.3
  216.0 1.9 collective-permute-start.15
  218.0 0.8 slice_bitcast_fusion.2
  218.7 3.4 %collective-permute-start.12 = (bf16[128,128]{1,0:T(8,128)(2,1)S(1)}, bf16[128,128]{1,0:T(8,128)(2,1)}, u32[]{:S(2)}, u32[]{:S(2)}) collective-permute-start(bf16[128,128]{1,0:T(8,128)(2,1)S(1)} %get-tuple-element.153), channel_id=1, source_target_pairs={{4,0},{8,4},{12,8},{16,12},{20,16},{24,20},{28,24},{32,28},{36,32}... | collective-permute-start | bytes 98312 | tf_op jit(solution)/shard_map/cond/branch_1_fun/ppermute | solution.py:371
  222.2 1.9 collective-permute-start.11
  224.1 0.6 dynamic-slice_add_fusion.1
  224.8 2.8 collective-permute-done.11
  227.5 10.7 %branch_1_fun.5 = bf16[144,128,128]{2,1,0:T(8,128)(2,1)} custom-call(s32[2]{0:T(128)} %copy-done.14, s32[128]{0:T(128)} %copy-done.13, s32[128]{0:T(128)} %copy-done.16, bf16[8,12,128,128]{3,2,1,0:T(8,128)(2,1)S(1)} %all-to-all-done.3.returned), custom_call_target="tpu_custom_call" | custom-call | bytes 10485760 | tf_op jit(solution)/shard_map/cond/branch_1_fun/pallas_call | solution.py:389
  238.2 0.9 reshape.228
  239.1 19.7 %all_to_all.57 = f32[16,4,256]{2,1,0:T(4,128)S(1)} all-to-all(f32[16,4,256]{2,1,0:T(4,128)S(1)} %reshape.228), channel_id=1, replica_groups=mesh['slab'=16,'lane'=8,'head'=4] {'slab'}, dimensions={0} | all-to-all | bytes 131072 | tf_op jit(solution)/shard_map/all_to_all | solution.py:277
  258.8 15.4 %all_to_all.58 = f32[16,4,256]{2,1,0:T(4,128)S(1)} all-to-all(f32[16,4,256]{2,1,0:T(4,128)S(1)} %broadcast_in_dim.34), channel_id=1, replica_groups=mesh['slab'=16,'lane'=8,'head'=4] {'slab'}, dimensions={0} | all-to-all | bytes 131072 | tf_op jit(solution)/shard_map/all_to_all | solution.py:277
  274.3 0.8 broadcast_in_dim.35
  275.1 9.9 %all-to-all-start.9 = ((f32[8,64,256]{2,1,0:T(8,128)}), f32[8,64,256]{2,1,0:T(8,128)S(1)}, u32[]{:S(2)}, u32[]{:S(2)}) async-start(f32[8,64,256]{2,1,0:T(8,128)} %broadcast_in_dim.35), calls=%async_computation.10 | async-start | bytes 1048576 | tf_op jit(solution)/shard_map/all_to_all | solution.py:277
  285.0 2.1 convolution_convert_fusion
  287.1 6.8 %all-to-all-done.9 = f32[8,64,256]{2,1,0:T(8,128)S(1)} async-done(((f32[8,64,256]{2,1,0:T(8,128)}), f32[8,64,256]{2,1,0:T(8,128)S(1)}, u32[]{:S(2)}, u32[]{:S(2)}) %all-to-all-start.9) | async-done | bytes 524320 | tf_op jit(solution)/shard_map/all_to_all | solution.py:277
  293.9 1.5 gather_fusion.1
  295.4 24.9 %reduce-scatter.2.cloned.1.call-done.others = bf16[9,128,128]{2,1,0:T(8,128)(2,1)} async-done(((bf16[144,128,128]{2,1,0:T(8,128)(2,1)}), bf16[9,128,128]{2,1,0:T(8,128)(2,1)}) %reduce-scatter.2.cloned.1.call-update) | async-done | bytes 294928 | tf_op jit(solution)/shard_map/reduce_scatter | solution.py:415
  320.3 1.0 copy-done.3
  321.3 1.9 shard_map.110
  (53 shorter events, 0.6 us)
Async XLA Ops:
  7.2 30.2 %copy-start = (bf16[512,256]{1,0:T(8,128)(2,1)S(1)}, bf16[512,256]{1,0:T(8,128)(2,1)}, u32[]{:S(2)}) copy-start(bf16[512,256]{1,0:T(8,128)(2,1)} %param.12) | copy-start | bytes 786436
  7.2 47.5 %copy-start.5 = (bf16[576,128]{1,0:T(8,128)(2,1)S(1)}, bf16[576,128]{1,0:T(8,128)(2,1)}, u32[]{:S(2)}) copy-start(bf16[576,128]{1,0:T(8,128)(2,1)} %param.11) | copy-start | bytes 442372
  7.2 47.5 %copy-start.6 = (bf16[576,128]{1,0:T(8,128)(2,1)S(1)}, bf16[576,128]{1,0:T(8,128)(2,1)}, u32[]{:S(2)}) copy-start(bf16[576,128]{1,0:T(8,128)(2,1)} %param.10) | copy-start | bytes 442372
  7.2 88.1 %all-gather.2.cloned.1.call-start = ((), (), s32[]{:S(2)}) async-start(), calls=%async_computation.11 | async-start | bytes 5013504 | tf_op jit(solution)/shard_map/all_gather | solution.py:298
  7.2 88.7 %copy-start.10 = (bf16[576,256]{1,0:T(8,128)(2,1)S(1)}, bf16[576,256]{1,0:T(8,128)(2,1)}, u32[]{:S(2)}) copy-start(bf16[576,256]{1,0:T(8,128)(2,1)} %param.13) | copy-start | bytes 884740
  7.3 88.7 %copy-start.12 = (bf16[576,128]{1,0:T(8,128)(2,1)S(1)}, bf16[576,128]{1,0:T(8,128)(2,1)}, u32[]{:S(2)}) copy-start(bf16[576,128]{1,0:T(8,128)(2,1)} %param.9) | copy-start | bytes 442372
  7.3 88.7 %copy-start.15 = (s32[128]{0:T(128)S(1)}, s32[128]{0:T(128)}, u32[]{:S(2)}) copy-start(s32[128]{0:T(128)} %param.15) | copy-start | bytes 1540
  22.1 27.6 %all-to-all-start.5 = ((s32[16,1,1]{2,1,0:T(1,128)}), s32[16,1,1]{2,1,0:T(1,128)S(1)}, u32[]{:S(2)}, u32[]{:S(2)}) async-start(s32[16,1,1]{2,1,0:T(1,128)} %broadcast_in_dim.20), calls=%async_computation.5 | async-start | bytes 16384 | tf_op jit(solution)/shard_map/all_to_all | solution.py:277
  49.8 18.4 %all-to-all-start.6 = ((f32[4,576,128]{2,1,0:T(8,128)}), f32[4,576,128]{2,1,0:T(8,128)S(1)}, u32[]{:S(2)}, u32[]{:S(2)}) async-start(f32[4,576,128]{2,1,0:T(8,128)} %bitcast.61), calls=%async_computation.6 | async-start | bytes 2359296 | tf_op jit(solution)/shard_map/all_to_all | solution.py:277
  54.7 265.6 %reduce-scatter.2.cloned.1.call-start = ((), (), s32[]{:S(2)}) async-start(), calls=%async_computation.12 | async-start | bytes 5013504 | tf_op jit(solution)/shard_map/reduce_scatter | solution.py:415
  54.7 13.5 %collective-permute-start.17 = (bf16[128,128]{1,0:T(8,128)(2,1)S(1)}, bf16[128,128]{1,0:T(8,128)(2,1)S(1)}, u32[]{:S(2)}, u32[]{:S(2)}) collective-permute-start(bf16[128,128]{1,0:T(8,128)(2,1)S(1)} %get-tuple-element.155), channel_id=1, source_target_pairs={{4,0},{8,4},{12,8},{16,12},{20,16},{24,20},{28,24},{32,28},{36,32}... | collective-permute-start | bytes 98312 | tf_op jit(solution)/shard_map/ppermute | solution.py:324
  56.6 11.6 %collective-permute-start.16 = (bf16[128,128]{1,0:T(8,128)(2,1)S(1)}, bf16[128,128]{1,0:T(8,128)(2,1)S(1)}, u32[]{:S(2)}, u32[]{:S(2)}) collective-permute-start(bf16[128,128]{1,0:T(8,128)(2,1)S(1)} %get-tuple-element.156), channel_id=1, source_target_pairs={{0,4},{4,8},{8,12},{12,16},{16,20},{20,24},{24,28},{28,32},{32,36}... | collective-permute-start | bytes 98312 | tf_op jit(solution)/shard_map/ppermute | solution.py:323
  59.1 1.3 copy-start.17
  96.0 50.2 %copy-start.11 = (bf16[576,256]{1,0:T(8,128)(2,1)}, bf16[576,256]{1,0:T(8,128)(2,1)S(1)}, u32[]{:S(2)}) copy-start(bf16[576,256]{1,0:T(8,128)(2,1)S(1)} %get-tuple-element.104) | copy-start | bytes 884740 | tf_op jit(solution)/shard_map/cond
  96.0 50.2 %copy-start.13 = (s32[128]{0:T(128)}, s32[128]{0:T(128)S(1)}, u32[]{:S(2)}) copy-start(s32[128]{0:T(128)S(1)} %get-tuple-element.95.asked) | copy-start | bytes 1540 | tf_op jit(solution)/shard_map/cond
  96.0 50.2 %copy-start.14 = (s32[2]{0:T(128)}, s32[2]{0:T(128)S(1)}, u32[]{:S(2)}) copy-start(s32[2]{0:T(128)S(1)} %get-tuple-element.94.where) | copy-start | bytes 28 | tf_op jit(solution)/shard_map/cond
  96.0 50.2 %copy-start.16 = (s32[128]{0:T(128)}, s32[128]{0:T(128)S(1)}, u32[]{:S(2)}) copy-start(s32[128]{0:T(128)S(1)} %get-tuple-element.96.global_pos) | copy-start | bytes 1540 | tf_op jit(solution)/shard_map/cond
  155.5 1.7 copy-start.2
  157.1 0.6 copy-start.4
  157.7 69.8 %all-to-all-start.3 = ((bf16[8,12,128,128]{3,2,1,0:T(8,128)(2,1)}), bf16[8,12,128,128]{3,2,1,0:T(8,128)(2,1)S(1)}, u32[]{:S(2)}, u32[]{:S(2)}) async-start(bf16[8,12,128,128]{3,2,1,0:T(8,128)(2,1)} %copy-done.2), calls=%async_computation.3 | async-start | bytes 6291456 | tf_op jit(solution)/shard_map/cond/branch_1_fun/all_to_all | solution.py:277
  162.8 10.8 %collective-permute-start.8 = (bf16[576,128]{1,0:T(8,128)(2,1)S(1)}, bf16[576,128]{1,0:T(8,128)(2,1)}, u32[]{:S(2)}, u32[]{:S(2)}) collective-permute-start(bf16[576,128]{1,0:T(8,128)(2,1)S(1)} %get-tuple-element.98), channel_id=1, source_target_pairs={{0,1},{1,2},{2,3},{3,0},{4,5},{5,6},{6,7},{7,4},{8,9},{9,10},{10,1... | collective-permute-start | bytes 442376 | tf_op jit(solution)/shard_map/cond/branch_1_fun/ppermute | solution.py:367
  166.2 12.2 %collective-permute-start.10 = (bf16[576,128]{1,0:T(8,128)(2,1)S(1)}, bf16[576,128]{1,0:T(8,128)(2,1)S(1)}, u32[]{:S(2)}, u32[]{:S(2)}) collective-permute-start(bf16[576,128]{1,0:T(8,128)(2,1)S(1)} %get-tuple-element.98), channel_id=1, source_target_pairs={{0,3},{1,0},{2,1},{3,2},{4,7},{5,4},{6,5},{7,6},{8,11},{9,8},{10,9... | collective-permute-start | bytes 442376 | tf_op jit(solution)/shard_map/cond/branch_1_fun/ppermute | solution.py:367
  168.7 9.0 %collective-permute-start.9 = (bf16[576,128]{1,0:T(8,128)(2,1)S(1)}, bf16[576,128]{1,0:T(8,128)(2,1)S(1)}, u32[]{:S(2)}, u32[]{:S(2)}) collective-permute-start(bf16[576,128]{1,0:T(8,128)(2,1)S(1)} %get-tuple-element.98), channel_id=1, source_target_pairs={{0,2},{1,3},{2,0},{3,1},{4,6},{5,7},{6,4},{7,5},{8,10},{9,11},{10,... | collective-permute-start | bytes 442376 | tf_op jit(solution)/shard_map/cond/branch_1_fun/ppermute | solution.py:367
  180.6 0.8 copy-start.9
  182.2 23.4 %collective-permute-start.13 = (f32[4,64,256]{2,1,0:T(8,128)}, f32[4,64,256]{2,1,0:T(8,128)}, u32[]{:S(2)}, u32[]{:S(2)}) collective-permute-start(f32[4,64,256]{2,1,0:T(8,128)} %dynamic-slice_bitcast_fusion.2), channel_id=1, source_target_pairs={{0,16},{4,20},{8,24},{12,28},{16,0},{20,4},{24,8},{28,12},{1,17},{... | collective-permute-start | bytes 786440 | tf_op jit(solution)/shard_map/cond/branch_1_fun/ppermute | solution.py:383
  206.6 0.7 copy-start.8
  208.0 7.1 %collective-permute-start.14 = (f32[2,64,256]{2,1,0:T(8,128)}, f32[2,64,256]{2,1,0:T(8,128)S(1)}, u32[]{:S(2)}, u32[]{:S(2)}) collective-permute-start(f32[2,64,256]{2,1,0:T(8,128)} %dynamic-slice_bitcast_fusion.3), channel_id=1, source_target_pairs={{0,8},{4,12},{8,0},{12,4},{16,24},{20,28},{24,16},{28,20},{1,9},{5... | collective-permute-start | bytes 393224 | tf_op jit(solution)/shard_map/cond/branch_1_fun/ppermute | solution.py:383
  216.0 8.1 %collective-permute-start.15 = (f32[1,64,256]{2,1,0:T(8,128)S(1)}, f32[1,64,256]{2,1,0:T(8,128)S(1)}, u32[]{:S(2)}, u32[]{:S(2)}) collective-permute-start(f32[1,64,256]{2,1,0:T(8,128)S(1)} %constant_dynamic-slice_fusion.1), channel_id=1, source_target_pairs={{0,4},{4,0},{8,12},{12,8},{16,20},{20,16},{24,28},{28,24},{1,5},{5... | collective-permute-start | bytes 196616 | tf_op jit(solution)/shard_map/cond/branch_1_fun/ppermute | solution.py:383
  218.7 6.0 %collective-permute-start.12 = (bf16[128,128]{1,0:T(8,128)(2,1)S(1)}, bf16[128,128]{1,0:T(8,128)(2,1)}, u32[]{:S(2)}, u32[]{:S(2)}) collective-permute-start(bf16[128,128]{1,0:T(8,128)(2,1)S(1)} %get-tuple-element.153), channel_id=1, source_target_pairs={{4,0},{8,4},{12,8},{16,12},{20,16},{24,20},{28,24},{32,28},{36,32}... | collective-permute-start | bytes 98312 | tf_op jit(solution)/shard_map/cond/branch_1_fun/ppermute | solution.py:371
  222.2 5.3 %collective-permute-start.11 = (bf16[128,128]{1,0:T(8,128)(2,1)S(1)}, bf16[128,128]{1,0:T(8,128)(2,1)}, u32[]{:S(2)}, u32[]{:S(2)}) collective-permute-start(bf16[128,128]{1,0:T(8,128)(2,1)S(1)} %get-tuple-element.154), channel_id=1, source_target_pairs={{0,4},{4,8},{8,12},{12,16},{16,20},{20,24},{24,28},{28,32},{32,36}... | collective-permute-start | bytes 98312 | tf_op jit(solution)/shard_map/cond/branch_1_fun/ppermute | solution.py:370
  238.2 46.8 %copy-start.7 = (bf16[4,128,256]{2,1,0:T(8,128)(2,1)S(1)}, bf16[4,128,256]{2,1,0:T(8,128)(2,1)}, u32[]{:S(2)}) copy-start(bf16[4,128,256]{2,1,0:T(8,128)(2,1)} %gather_fusion) | copy-start | bytes 786436
  275.1 18.8 %all-to-all-start.9 = ((f32[8,64,256]{2,1,0:T(8,128)}), f32[8,64,256]{2,1,0:T(8,128)S(1)}, u32[]{:S(2)}, u32[]{:S(2)}) async-start(f32[8,64,256]{2,1,0:T(8,128)} %broadcast_in_dim.35), calls=%async_computation.10 | async-start | bytes 1048576 | tf_op jit(solution)/shard_map/all_to_all | solution.py:277
  320.3 1.0 copy-start.3
Sparse Core Ops, SparseCore 0:
  10.7 84.5 all-gather.1
  238.3 81.9 reduce-scatter.1

commit v5 on v4

--- a/solution.py
+++ b/solution.py
@@ -13,8 +13,8 @@
 PAIR = 2 * BLOCK
 LANES = 8
 TILE = 16
-PANEL = 2
 FEW = 10
+FEW_ROWS = 32
 R = 3
 GLOBALS = 128
 VMEM_LIMIT = 40 * 1024 * 1024
@@ -40,16 +40,18 @@
     )
 
 
-def serve_kernel(where, asked, global_pos, lane_blocks, send, panel):
+def serve_kernel(where, asked, global_pos, global_rank, lane_blocks, send, panel):
     me, blocks = where[0], where[1]
     tokens = blocks * BLOCK
     most = asked.shape[0] // LANES
-    slots = send.shape[1] - PANEL
+    room = panel.shape[0] // 2
+    slots = send.shape[1] // PAIR if room < GLOBALS else most
 
     def serve(number, carry):
         to = number // slots
         rank = number % slots
-        send[to, rank] = lane_blocks[jnp.maximum(asked[to * most + rank], 0)]
+        rows = pl.ds(pl.multiple_of(rank * PAIR, PAIR), PAIR)
+        send[to, rows, :] = lane_blocks[jnp.maximum(asked[to * most + rank], 0)]
         return carry
 
     lax.fori_loop(0, LANES * slots, serve, 0)
@@ -70,16 +72,16 @@
             hit = row_number == inside % TILE
             for half in range(2):
                 rows = lane_blocks[source, pl.ds(first + half * BLOCK, TILE), :]
-                panel[pl.ds(number + half * GLOBALS, 1), :] = jnp.sum(
+                panel[pl.ds(global_rank[number] + half * room, 1), :] = jnp.sum(
                     jnp.where(hit, rows.astype(jnp.float32), 0.0), axis=0, keepdims=True
                 )
 
         return carry
 
     lax.fori_loop(0, GLOBALS, pick, 0)
-    panel_rows = panel[...].astype(send.dtype).reshape(PANEL, PAIR, panel.shape[1])
+    panel_rows = panel[...].astype(send.dtype)
     for to in range(LANES):
-        send[to, slots:] = panel_rows
+        send[to, slots * PAIR :, :] = panel_rows
 
 
 def attention_kernel(
@@ -92,6 +94,7 @@
     value,
     left,
     right,
+    global_place,
     arrived,
     attended,
     query_grad,
@@ -114,11 +117,6 @@
     value_pad[BLOCK : BLOCK + tokens, :] = value[...]
     key_pad[BLOCK + tokens :, :] = right[:BLOCK, :]
     value_pad[BLOCK + tokens :, :] = right[BLOCK:, :]
-    slots = arrived.shape[1] - PANEL
-    panel_sum = jnp.zeros((PANEL, PAIR, columns), f32)
-    for lane in range(LANES):
-        panel_sum += arrived[lane, slots:].astype(f32)
-    panel[...] = panel_sum.reshape(panel.shape).astype(bf16)
     key_grad[...] = jnp.zeros_like(key_grad)
     value_grad[...] = jnp.zeros_like(value_grad)
     panel_grad[...] = jnp.zeros_like(panel_grad)
@@ -140,17 +138,30 @@
     def dot(a, b, dims):
         return lax.dot_general(a, b, (dims, ((), ())), preferred_element_type=f32)
 
+    room = GLOBALS if arrived.shape[1] % PAIR == 0 else arrived.shape[1] % PAIR // 2
+    first_row = arrived.shape[1] - 2 * room
+    packed = lax.broadcasted_iota(jnp.int32, (GLOBALS, LANES * room), 1)
+    chosen = jnp.where(packed == global_place[...], 1.0, 0.0).astype(bf16)
+    for half in range(2):
+        begin = first_row + half * room
+        rows = [arrived[lane, begin : begin + room, :] for lane in range(LANES)]
+        panel[half * GLOBALS : (half + 1) * GLOBALS, :] = dot(
+            chosen, jnp.concatenate(rows, axis=0), ((1,), (0,))
+        ).astype(bf16)
+
     def one(block, carry):
         row = pl.multiple_of(block * BLOCK, BLOCK)
         here = pl.ds(row, BLOCK)
         around = pl.ds(row, window)
         named = [block * R + j for j in range(R)]
-        places = [(names[n] // blocks % LANES, ranks[n]) for n in named]
+        places = [
+            (names[n] // blocks % LANES, pl.multiple_of(ranks[n] * PAIR, PAIR)) for n in named
+        ]
         kk = jnp.concatenate(
-            [key_pad[around, :], panel[:GLOBALS, :]] + [arrived[a, b, :BLOCK, :] for a, b in places], axis=0
+            [key_pad[around, :], panel[:GLOBALS, :]] + [arrived[a, pl.ds(b, BLOCK), :] for a, b in places], axis=0
         )
         vv = jnp.concatenate(
-            [value_pad[around, :], panel[GLOBALS:, :]] + [arrived[a, b, BLOCK:, :] for a, b in places], axis=0
+            [value_pad[around, :], panel[GLOBALS:, :]] + [arrived[a, pl.ds(b + BLOCK, BLOCK), :] for a, b in places], axis=0
         )
         q2 = by_head(q[here, :])
         g2 = by_head(g[here, :])
@@ -180,24 +191,28 @@
         panel_grad[GLOBALS:, :] += dv[window : window + GLOBALS]
         for j, (a, b) in enumerate(places):
             first = window + GLOBALS + j * BLOCK
-            send[a, b, :BLOCK, :] = dk[first : first + BLOCK].astype(bf16)
-            send[a, b, BLOCK:, :] = dv[first : first + BLOCK].astype(bf16)
+            send[a, pl.ds(b, BLOCK), :] = dk[first : first + BLOCK].astype(bf16)
+            send[a, pl.ds(b + BLOCK, BLOCK), :] = dv[first : first + BLOCK].astype(bf16)
         return carry
 
     lax.fori_loop(0, blocks, one, 0)
     for side, rows in enumerate((pl.ds(0, BLOCK), pl.ds(BLOCK + tokens, BLOCK))):
         rims[side, :BLOCK, :] = key_grad[rows, :].astype(bf16)
         rims[side, BLOCK:, :] = value_grad[rows, :].astype(bf16)
-    panel_rows = panel_grad[...].astype(bf16).reshape(PANEL, PAIR, columns)
-    for lane in range(LANES):
-        send[lane, slots:] = panel_rows
-
-
-def collect_kernel(where, asked, global_pos, returned, lane_grads, sums, panel):
+    for half in range(2):
+        begin = first_row + half * room
+        rows = panel_grad[half * GLOBALS : (half + 1) * GLOBALS, :].astype(bf16)
+        rows = dot(chosen, rows, ((0,), (0,))).astype(bf16)
+        for lane in range(LANES):
+            send[lane, begin : begin + room, :] = rows[lane * room : (lane + 1) * room]
+
+
+def collect_kernel(where, asked, global_pos, global_rank, returned, lane_grads, sums, panel):
     me, blocks = where[0], where[1]
     tokens = blocks * BLOCK
     most = asked.shape[0] // LANES
-    slots = returned.shape[1] - PANEL
+    room = panel.shape[0] // 2
+    slots = returned.shape[1] // PAIR if room < GLOBALS else most
     f32 = jnp.float32
     sums[...] = jnp.zeros_like(sums)
 
@@ -208,15 +223,16 @@
 
         @pl.when(wanted >= 0)
         def _():
-            sums[wanted] += returned[source, rank].astype(f32)
+            rows = pl.ds(pl.multiple_of(rank * PAIR, PAIR), PAIR)
+            sums[wanted] += returned[source, rows, :].astype(f32)
 
         return carry
 
     lax.fori_loop(0, LANES * slots, add, 0)
-    total_rows = jnp.zeros((PANEL, PAIR, panel.shape[1]), f32)
+    total_rows = jnp.zeros(panel.shape, f32)
     for lane in range(LANES):
-        total_rows += returned[lane, slots:].astype(f32)
-    panel[...] = total_rows.reshape(panel.shape)
+        total_rows += returned[lane, slots * PAIR :, :].astype(f32)
+    panel[...] = total_rows
 
     def spread(number, carry):
         position = global_pos[number]
@@ -228,7 +244,7 @@
             to = owner // LANES * blocks + row // BLOCK
             for half in range(2):
                 sums[to, pl.ds(row % BLOCK + half * BLOCK, 1), :] += panel[
-                    pl.ds(number + half * GLOBALS, 1), :
+                    pl.ds(global_rank[number] + half * room, 1), :
                 ]
 
         return carry
@@ -307,9 +323,14 @@
     hit = (lane * slabs + ranks)[None, :] == index[:, None]
     wanted = jnp.max(jnp.where(hit, code[None, :], -1), axis=1).reshape(LANES, slabs)
     load = jnp.broadcast_to(jnp.max(ranks) + 1, (LANES, 1))
+    global_lane = global_pos // tokens % LANES
+    number = jnp.arange(GLOBALS)
+    same = (global_lane[:, None] == global_lane[None, :]) & (number[None, :] < number[:, None])
+    global_rank = jnp.sum(same.astype(jnp.int32), axis=1)
     heard = exchange(jnp.concatenate([wanted, load], axis=1), "lane")
     asked = heard[:, :slabs].reshape(-1)
     load = jnp.max(spread(jnp.max(heard[:, slabs:]).reshape(1), "slab"))
+    fits = (load <= FEW) & (jnp.max(global_rank) < FEW_ROWS)
 
     partial_grad = lax.dot_general(
         output_grad, out_weight, (((1,), (1,)), ((), ())), preferred_element_type=f32
@@ -326,21 +347,22 @@
     order = (head - jnp.arange(heads)) % heads
     weight_rows = out_weight.reshape(heads, columns, -1).at[order].get(mode="promise_in_bounds")
     weight_rows = weight_rows.reshape(out_weight.shape)
-    lane_blocks, asked, load, grad_att, left, right, weight_rows = lax.optimization_barrier(
-        (lane_blocks, asked, load, grad_att, left, right, weight_rows)
+    lane_blocks, asked, fits, grad_att, left, right, weight_rows = lax.optimization_barrier(
+        (lane_blocks, asked, fits, grad_att, left, right, weight_rows)
     )
     place = jnp.stack([position * blocks, seq_count * blocks - 1]).astype(jnp.int32)
     padded = tokens + PAIR
 
-    def middle(slots):
-        slots += PANEL
+    def middle(slots, room):
+        sent_rows = slots * PAIR + 2 * room
+        global_place = (global_lane * room + global_rank).reshape(GLOBALS, 1)
         served = call(
             serve_kernel,
-            shape((LANES, slots, PAIR, columns), bf16),
-            [smem, smem, smem, vmem],
-            [pltpu.VMEM((2 * GLOBALS, columns), f32)],
+            shape((LANES, sent_rows, columns), bf16),
+            [smem, smem, smem, smem, vmem],
+            [pltpu.VMEM((2 * room, columns), f32)],
             moved=8 << 20,
-        )(where, asked, global_pos, lane_blocks)
+        )(where, asked, global_pos, global_rank, lane_blocks)
         arrived = exchange(served, "lane")
         attended, query_grad, key_part, value_part, rims, sent = call(
             attention_kernel,
@@ -350,9 +372,9 @@
                 shape((padded, columns), f32),
                 shape((padded, columns), f32),
                 shape((2, PAIR, columns), bf16),
-                shape((LANES, slots, PAIR, columns), bf16),
+                shape((LANES, sent_rows, columns), bf16),
             ),
-            [smem, smem, smem] + [vmem] * 7,
+            [smem, smem, smem] + [vmem] * 8,
             [pltpu.VMEM((padded, columns), bf16)] * 2
             + [
                 pltpu.VMEM((2 * GLOBALS, columns), bf16),
@@ -360,7 +382,19 @@
             ],
             flops=1 << 30,
             moved=12 << 20,
-        )(place, names, ranks, queries, grad_att, key_states, value_states, left, right, arrived)
+        )(
+            place,
+            names,
+            ranks,
+            queries,
+            grad_att,
+            key_states,
+            value_states,
+            left,
+            right,
+            global_place,
+            arrived,
+        )
         returned = exchange(sent, "lane")
 
         pieces = [attended] + [
@@ -373,29 +407,19 @@
         weight_part = lax.dot_general(
             everywhere, output_grad, (((0,), (0,)), ((), ())), preferred_element_type=f32
         ) * (1.0 / math.sqrt(tokens * seq_count))
-        weight_part = weight_part.reshape(LANES, -1, weight_part.shape[1])
-        step = LANES // 2
-        while step:
-            pair = weight_part.reshape((2, step) + weight_part.shape[1:])
-            mine = me // step % 2
-            kept = lax.dynamic_index_in_dim(pair, mine, 0, keepdims=False)
-            other = lax.dynamic_index_in_dim(pair, 1 - mine, 0, keepdims=False)
-            other = lax.ppermute(other, "lane", [(i, i ^ step) for i in range(LANES)])
-            weight_part = kept + other
-            step //= 2
         returned, from_left, from_right, weight_part = lax.optimization_barrier(
             (returned, from_left, from_right, weight_part)
         )
         lane_grads = call(
             collect_kernel,
             shape((slabs * blocks, PAIR, columns), bf16),
-            [smem, smem, smem, vmem],
+            [smem, smem, smem, smem, vmem],
             [
                 pltpu.VMEM((slabs * blocks, PAIR, columns), f32),
-                pltpu.VMEM((2 * GLOBALS, columns), f32),
+                pltpu.VMEM((2 * room, columns), f32),
             ],
             moved=10 << 20,
-        )(where, asked, global_pos, returned)
+        )(where, asked, global_pos, global_rank, returned)
         return (
             everywhere,
             query_grad,
@@ -407,13 +431,23 @@
             lane_grads,
         )
 
-    few = lambda: middle(FEW)
-    all_slots = lambda: middle(slabs)
+    few = lambda: middle(FEW, FEW_ROWS)
+    all_slots = lambda: middle(slabs, GLOBALS)
     everywhere, query_grad, key_part, value_part, from_left, from_right, weight_part, lane_grads = (
-        lax.cond(load <= FEW, few, all_slots) if FEW < slabs else all_slots()
+        lax.cond(fits, few, all_slots) if FEW < slabs else all_slots()
     )
     others = lax.psum_scatter(lane_grads, "slab", scatter_dimension=0, tiled=True)
 
+    weight_part = weight_part.reshape(LANES, -1, weight_part.shape[1])
+    step = LANES // 2
+    while step:
+        pair = weight_part.reshape((2, step) + weight_part.shape[1:])
+        mine = me // step % 2
+        kept = lax.dynamic_index_in_dim(pair, mine, 0, keepdims=False)
+        other = lax.dynamic_index_in_dim(pair, 1 - mine, 0, keepdims=False)
+        other = lax.ppermute(other, "lane", [(i, i ^ step) for i in range(LANES)])
+        weight_part = kept + other
+        step //= 2
     features = weight_part.shape[-1]
     share = jnp.sum(exchange(weight_part.reshape(slabs, -1, features), "slab"), axis=0)
     share = spread(share, "slab").reshape(-1, features)

time: 331 us -> 295 us (0.89)
  the two profiles are of different devices: /device:TPU:10 before, /device:TPU:1 now
where the time goes in v5:
time: 295 us; the launch traced here: 291 us
  waiting for transfers between devices  95.2 us (32%)
  starting transfers between devices  72.8 us (25%)
  blocking collectives  48.6 us (16%)
  Pallas kernels  32.3 us (11%)
  between operations  16.3 us (6%)
  local copies, waits for them, and re-layouts  13.6 us (5%)
  other arithmetic  6.12 us (2%)
  matrix products  5.68 us (2%)
    all_to_all x5, waiting for transfers between devices, exchange(): return lax.all_to_all(array, axis, split_axis=0, concat_axis=0, tiled=True)  53.3 us
    all_to_all x3, blocking collectives, exchange(): return lax.all_to_all(array, axis, split_axis=0, concat_axis=0, tiled=True)  48.6 us
    all_to_all x5, starting transfers between devices, exchange(): return lax.all_to_all(array, axis, split_axis=0, concat_axis=0, tiled=True)  38.4 us
    all_gather x1, waiting for transfers between devices, shards(): lane_blocks = lax.all_gather(own, 'slab', axis=0, tiled=True)  20.5 us
    ppermute x3, starting transfers between devices, shards(): other = lax.ppermute(other, 'lane', [(i, i ^ step) for i in range(LANES)])  10.9 us
    ppermute x3, waiting for transfers between devices, shards(): other = lax.ppermute(other, 'lane', [(i, i ^ step) for i in range(LANES)])  10.7 us
    ppermute x3, starting transfers between devices, middle(): lax.ppermute(attended, 'head', [(i, (i + k) % heads) for i in range(heads)])  10.7 us
    pallas_call x1, Pallas kernels, middle(): call(collect_kernel, shape((slabs * blocks, PAIR, columns), bf16), [smem,...  10.6 us
  transfers between devices with their start and end apart: 17, of which 11 were waited for; matrix products, arithmetic and copies ran while one was open for 7% of the time, Pallas kernels for 0%

profile of v5, /device:TPU:1, one launch (start us, length us, event | category | flops | bytes accessed | tf_op | source)
XLA Modules:
  0.0 291.0 jit_solution(4459678799261745216)
XLA Ops:
  7.3 1.8 pad_maximum_fusion
  9.1 0.8 copy.30
  9.9 0.1 reshape.216
  10.0 0.2 convert_reduce_fusion.1
  10.2 0.6 fusion.10
  10.8 0.1 select_reduce_fusion
  10.9 0.1 reshape.217
  11.7 13.8 %all_to_all.54 = s32[8,1,17]{2,1,0:T(1,128)S(1)} all-to-all(s32[8,1,17]{2,1,0:T(1,128)S(1)} %bitcast.69), channel_id=1, replica_groups=mesh['slab'=16,'lane'=8,'head'=4] {'lane'}, dimensions={0} | all-to-all | bytes 1088 | tf_op jit(solution)/shard_map/all_to_all | solution.py:293
  25.5 0.7 slice_reduce_fusion
  26.2 1.2 broadcast_in_dim.20
  27.4 11.5 %all-to-all-start.5 = ((s32[16,1,1]{2,1,0:T(1,128)}), s32[16,1,1]{2,1,0:T(1,128)S(1)}, u32[]{:S(2)}, u32[]{:S(2)}) async-start(s32[16,1,1]{2,1,0:T(1,128)} %broadcast_in_dim.20), calls=%async_computation.5 | async-start | bytes 16384 | tf_op jit(solution)/shard_map/all_to_all | solution.py:293
  38.9 1.3 convolution_bitcast_fusion
  40.2 1.1 copy.37
  41.3 8.8 %all-to-all-done.5 = s32[16,1,1]{2,1,0:T(1,128)S(1)} async-done(((s32[16,1,1]{2,1,0:T(1,128)}), s32[16,1,1]{2,1,0:T(1,128)S(1)}, u32[]{:S(2)}, u32[]{:S(2)}) %all-to-all-start.5) | async-done | bytes 96 | tf_op jit(solution)/shard_map/all_to_all | solution.py:293
  50.2 4.0 %all-to-all-start.6 = ((f32[4,576,128]{2,1,0:T(8,128)}), f32[4,576,128]{2,1,0:T(8,128)S(1)}, u32[]{:S(2)}, u32[]{:S(2)}) async-start(f32[4,576,128]{2,1,0:T(8,128)} %bitcast.55), calls=%async_computation.6 | async-start | bytes 2359296 | tf_op jit(solution)/shard_map/all_to_all | solution.py:293
  54.2 4.6 %collective-permute-start.10 = (bf16[128,128]{1,0:T(8,128)(2,1)S(1)}, bf16[128,128]{1,0:T(8,128)(2,1)S(1)}, u32[]{:S(2)}, u32[]{:S(2)}) collective-permute-start(bf16[128,128]{1,0:T(8,128)(2,1)S(1)} %get-tuple-element.162), channel_id=1, source_target_pairs={{0,4},{4,8},{8,12},{12,16},{16,20},{20,24},{24,28},{28,32},{32,36}... | collective-permute-start | bytes 98312 | tf_op jit(solution)/shard_map/ppermute | solution.py:344
  58.8 1.9 collective-permute-start.11
  60.8 0.2 convert_reduce_fusion
  61.0 0.1 pad_add_fusion
  61.1 0.6 reduce_max.49
  62.3 1.3 gather_fusion
  63.6 0.1 reshape.218
  63.7 0.7 reduce_max.48
  65.0 3.2 %all-to-all-done.6 = f32[4,576,128]{2,1,0:T(8,128)S(1)} async-done(((f32[4,576,128]{2,1,0:T(8,128)}), f32[4,576,128]{2,1,0:T(8,128)S(1)}, u32[]{:S(2)}, u32[]{:S(2)}) %all-to-all-start.6) | async-done | bytes 1179680 | tf_op jit(solution)/shard_map/all_to_all | solution.py:293
  68.3 20.5 %all-gather.2.cloned.1.call-done = bf16[144,128,128]{2,1,0:T(8,128)(2,1)} async-done(((bf16[9,128,128]{2,1,0:T(8,128)(2,1)}), bf16[144,128,128]{2,1,0:T(8,128)(2,1)}) %all-gather.2.cloned.1.call-update) | async-done | bytes 4718608 | tf_op jit(solution)/shard_map/all_gather | solution.py:314
  88.8 115.6 %conditional.1 = (bf16[576,512]{1,0:T(8,128)(2,1)}, bf16[576,128]{1,0:T(8,128)(2,1)}, f32[704,128]{1,0:T(8,128)}, f32[704,128]{1,0:T(8,128)}, bf16[128,128]{1,0:...) conditional(s32[]{:T(128)} %convert_element_type.18, ...), branch_computations={%region_8.9_spmd, %region_9.10_spmd} | conditional | flops 1224868096 | bytes 102271872 | solution.py:437
  88.9 9.9 %branch_1_fun.3 = bf16[8,1344,128]{2,1,0:T(8,128)(2,1)} custom-call(s32[2]{0:T(128)S(1)} %get-tuple-element.101.where, s32[128]{0:T(128)S(1)} %get-tuple-element.102.asked, s32[128]{0:T(128)S(1)} %get-tuple-element.103.global_pos, s32[128]{0:T(128)S(1)} %get-tuple-element.100.global_rank, bf16[144,128,128]{2,1,0:T(8,128)(2,1)} %get-tuple-element.104.lane_blocks), custom_call_target="tpu_custom_call" | custom-call | bytes 8388608 | tf_op jit(solution)/shard_map/cond/branch_1_fun/pallas_call | solution.py:359
  98.9 12.2 %all-to-all-start.2 = ((bf16[8,1344,128]{2,1,0:T(8,128)(2,1)}), bf16[8,1344,128]{2,1,0:T(8,128)(2,1)S(1)}, u32[]{:S(2)}, u32[]{:S(2)}) async-start(bf16[8,1344,128]{2,1,0:T(8,128)(2,1)} %branch_1_fun.3), calls=%async_computation.2 | async-start | bytes 5505024 | tf_op jit(solution)/shard_map/cond/branch_1_fun/all_to_all | solution.py:293
  111.1 0.1 copy.29.global_place
  111.2 33.2 %all-to-all-done.2.arrived = bf16[8,1344,128]{2,1,0:T(8,128)(2,1)S(1)} async-done(((bf16[8,1344,128]{2,1,0:T(8,128)(2,1)}), bf16[8,1344,128]{2,1,0:T(8,128)(2,1)S(1)}, u32[]{:S(2)}, u32[]{:S(2)}) %all-to-all-start.2) | async-done | bytes 2752544 | tf_op jit(solution)/shard_map/cond/branch_1_fun/all_to_all | solution.py:293
  144.5 9.9 %branch_1_fun.4 = (bf16[576,128]{1,0:T(8,128)(2,1)S(1)}, bf16[576,128]{1,0:T(8,128)(2,1)}, f32[704,128]{1,0:T(8,128)}, f32[704,128]{1,0:T(8,128)}, bf16[2,128,12...) custom-call(s32[2]{0:T(128)} %copy-done.27, s32[27]{0:T(128)} %copy-done.25, s32[27]{0:T(128)} %copy-done.26, ...), custom_call_target="tpu_custom_call" | custom-call | flops 1073741824 | bytes 12582912 | tf_op jit(solution)/shard_map/cond/branch_1_fun/pallas_call | solution.py:367
  154.4 1.5 copy-done.3
  155.9 4.6 %all-to-all-start.3 = ((bf16[8,1344,128]{2,1,0:T(8,128)(2,1)}), bf16[8,1344,128]{2,1,0:T(8,128)(2,1)S(1)}, u32[]{:S(2)}, u32[]{:S(2)}) async-start(bf16[8,1344,128]{2,1,0:T(8,128)(2,1)} %copy-done.3), calls=%async_computation.3 | async-start | bytes 5505024 | tf_op jit(solution)/shard_map/cond/branch_1_fun/all_to_all | solution.py:293
  160.5 3.3 %collective-permute-start.5 = (bf16[576,128]{1,0:T(8,128)(2,1)S(1)}, bf16[576,128]{1,0:T(8,128)(2,1)S(1)}, u32[]{:S(2)}, u32[]{:S(2)}) collective-permute-start(bf16[576,128]{1,0:T(8,128)(2,1)S(1)} %get-tuple-element.105), channel_id=1, source_target_pairs={{0,1},{1,2},{2,3},{3,0},{4,5},{5,6},{6,7},{7,4},{8,9},{9,10},{10,1... | collective-permute-start | bytes 442376 | tf_op jit(solution)/shard_map/cond/branch_1_fun/ppermute | solution.py:401
  163.8 4.3 %collective-permute-start.6 = (bf16[576,128]{1,0:T(8,128)(2,1)S(1)}, bf16[576,128]{1,0:T(8,128)(2,1)S(1)}, u32[]{:S(2)}, u32[]{:S(2)}) collective-permute-start(bf16[576,128]{1,0:T(8,128)(2,1)S(1)} %get-tuple-element.105), channel_id=1, source_target_pairs={{0,2},{1,3},{2,0},{3,1},{4,6},{5,7},{6,4},{7,5},{8,10},{9,11},{10,... | collective-permute-start | bytes 442376 | tf_op jit(solution)/shard_map/cond/branch_1_fun/ppermute | solution.py:401
  168.1 3.1 %collective-permute-start.7 = (bf16[576,128]{1,0:T(8,128)(2,1)S(1)}, bf16[576,128]{1,0:T(8,128)(2,1)S(1)}, u32[]{:S(2)}, u32[]{:S(2)}) collective-permute-start(bf16[576,128]{1,0:T(8,128)(2,1)S(1)} %get-tuple-element.105), channel_id=1, source_target_pairs={{0,3},{1,0},{2,1},{3,2},{4,7},{5,4},{6,5},{7,6},{8,11},{9,8},{10,9... | collective-permute-start | bytes 442376 | tf_op jit(solution)/shard_map/cond/branch_1_fun/ppermute | solution.py:401
  171.2 0.7 constant_dynamic-update-slice_fusion.7
  171.9 4.4 %collective-permute-start.8 = (bf16[128,128]{1,0:T(8,128)(2,1)S(1)}, bf16[128,128]{1,0:T(8,128)(2,1)}, u32[]{:S(2)}, u32[]{:S(2)}) collective-permute-start(bf16[128,128]{1,0:T(8,128)(2,1)S(1)} %get-tuple-element.160), channel_id=1, source_target_pairs={{0,4},{4,8},{8,12},{12,16},{16,20},{20,24},{24,28},{28,32},{32,36}... | collective-permute-start | bytes 98312 | tf_op jit(solution)/shard_map/cond/branch_1_fun/ppermute | solution.py:404
  176.3 1.9 collective-permute-start.9
  178.2 0.7 constant_dynamic-update-slice_fusion.6
  178.9 0.7 constant_dynamic-update-slice_fusion.5
  179.6 0.7 constant_dynamic-update-slice_fusion.4
  180.3 2.3 convolution_multiply_fusion.1
  182.6 8.6 %collective-permute-done.8 = bf16[128,128]{1,0:T(8,128)(2,1)} collective-permute-done((bf16[128,128]{1,0:T(8,128)(2,1)S(1)}, bf16[128,128]{1,0:T(8,128)(2,1)}, u32[]{:S(2)}, u32[]{:S(2)}) %collective-permute-start.8) | collective-permute-done | bytes 32800 | tf_op jit(solution)/shard_map/cond/branch_1_fun/ppermute | solution.py:404
  191.1 2.0 collective-permute-done.9
  193.2 0.7 all-to-all-done.3.returned
  193.9 10.6 %branch_1_fun.5 = bf16[144,128,128]{2,1,0:T(8,128)(2,1)} custom-call(s32[2]{0:T(128)S(1)} %copy-done.18, s32[128]{0:T(128)S(1)} %copy-done.16, s32[128]{0:T(128)S(1)} %copy-done.21, s32[128]{0:T(128)S(1)} %copy-done.23, bf16[8,1344,128]{2,1,0:T(8,128)(2,1)S(1)} %all-to-all-done.3.returned), custom_call_target="tpu_custom_call" | custom-call | bytes 10485760 | tf_op jit(solution)/shard_map/cond/branch_1_fun/pallas_call | solution.py:413
  204.5 1.0 dynamic-slice_bitcast_fusion
  205.5 3.4 %collective-permute-start.12 = (f32[4,64,256]{2,1,0:T(8,128)S(1)}, f32[4,64,256]{2,1,0:T(8,128)S(1)}, u32[]{:S(2)}, u32[]{:S(2)}) collective-permute-start(f32[4,64,256]{2,1,0:T(8,128)S(1)} %dynamic-slice_bitcast_fusion), channel_id=1, source_target_pairs={{0,16},{4,20},{8,24},{12,28},{16,0},{20,4},{24,8},{28,12},{1,17},{... | collective-permute-start | bytes 786440 | tf_op jit(solution)/shard_map/ppermute | solution.py:448
  208.9 6.6 %collective-permute-done.12 = f32[4,64,256]{2,1,0:T(8,128)S(1)} collective-permute-done((f32[4,64,256]{2,1,0:T(8,128)S(1)}, f32[4,64,256]{2,1,0:T(8,128)S(1)}, u32[]{:S(2)}, u32[]{:S(2)}) %collective-permute-start.12) | collective-permute-done | bytes 262176 | tf_op jit(solution)/shard_map/ppermute | solution.py:448
  215.5 1.0 bitcast_add_fusion
  216.5 2.8 collective-permute-start.13
  219.3 3.3 %collective-permute-done.13 = f32[2,64,256]{2,1,0:T(8,128)S(1)} collective-permute-done((f32[2,64,256]{2,1,0:T(8,128)S(1)}, f32[2,64,256]{2,1,0:T(8,128)S(1)}, u32[]{:S(2)}, u32[]{:S(2)}) %collective-permute-start.13) | collective-permute-done | bytes 131104 | tf_op jit(solution)/shard_map/ppermute | solution.py:448
  222.6 4.8 %collective-permute-start.14 = (f32[1,64,256]{2,1,0:T(8,128)S(1)}, f32[1,64,256]{2,1,0:T(8,128)S(1)}, u32[]{:S(2)}, u32[]{:S(2)}) collective-permute-start(f32[1,64,256]{2,1,0:T(8,128)S(1)} %constant_dynamic-slice_fusion), channel_id=1, source_target_pairs={{0,4},{4,0},{8,12},{12,8},{16,20},{20,16},{24,28},{28,24},{1,5},{5... | collective-permute-start | bytes 196616 | tf_op jit(solution)/shard_map/ppermute | solution.py:448
  227.5 0.9 collective-permute-done.14
  228.4 18.4 %all_to_all.55 = f32[16,4,256]{2,1,0:T(4,128)S(1)} all-to-all(f32[16,4,256]{2,1,0:T(4,128)S(1)} %reshape.223), channel_id=1, replica_groups=mesh['slab'=16,'lane'=8,'head'=4] {'slab'}, dimensions={0} | all-to-all | bytes 131072 | tf_op jit(solution)/shard_map/all_to_all | solution.py:293
  246.9 16.4 %all_to_all.56 = f32[16,4,256]{2,1,0:T(4,128)S(1)} all-to-all(f32[16,4,256]{2,1,0:T(4,128)S(1)} %broadcast_in_dim.21), channel_id=1, replica_groups=mesh['slab'=16,'lane'=8,'head'=4] {'slab'}, dimensions={0} | all-to-all | bytes 131072 | tf_op jit(solution)/shard_map/all_to_all | solution.py:293
  263.3 0.8 broadcast_in_dim.22
  264.1 6.1 %all-to-all-start.9 = ((f32[8,64,256]{2,1,0:T(8,128)}), f32[8,64,256]{2,1,0:T(8,128)S(1)}, u32[]{:S(2)}, u32[]{:S(2)}) async-start(f32[8,64,256]{2,1,0:T(8,128)} %broadcast_in_dim.22), calls=%async_computation.10 | async-start | bytes 1048576 | tf_op jit(solution)/shard_map/all_to_all | solution.py:293
  270.3 2.1 convolution_convert_fusion
  272.4 7.4 %all-to-all-done.9 = f32[8,64,256]{2,1,0:T(8,128)S(1)} async-done(((f32[8,64,256]{2,1,0:T(8,128)}), f32[8,64,256]{2,1,0:T(8,128)S(1)}, u32[]{:S(2)}, u32[]{:S(2)}) %all-to-all-start.9) | async-done | bytes 524320 | tf_op jit(solution)/shard_map/all_to_all | solution.py:293
  279.8 1.5 gather_fusion.1
  281.3 1.0 copy-done.4
  282.2 1.9 shard_map.110
  (77 shorter events, 0.5 us)
Async XLA Ops:
  7.2 31.7 %copy-start = (bf16[512,256]{1,0:T(8,128)(2,1)S(1)}, bf16[512,256]{1,0:T(8,128)(2,1)}, u32[]{:S(2)}) copy-start(bf16[512,256]{1,0:T(8,128)(2,1)} %param.12) | copy-start | bytes 786436
  7.2 47.0 %copy-start.6 = (bf16[576,128]{1,0:T(8,128)(2,1)S(1)}, bf16[576,128]{1,0:T(8,128)(2,1)}, u32[]{:S(2)}) copy-start(bf16[576,128]{1,0:T(8,128)(2,1)} %param.10) | copy-start | bytes 442372
  7.2 47.0 %copy-start.5 = (bf16[576,128]{1,0:T(8,128)(2,1)S(1)}, bf16[576,128]{1,0:T(8,128)(2,1)}, u32[]{:S(2)}) copy-start(bf16[576,128]{1,0:T(8,128)(2,1)} %param.11) | copy-start | bytes 442372
  7.2 53.6 %copy-start.19 = (s32[128]{0:T(128)S(1)}, s32[128]{0:T(128)}, u32[]{:S(2)}) copy-start(s32[128]{0:T(128)} %param.15) | copy-start | bytes 1540
  7.2 81.6 %all-gather.2.cloned.1.call-start = ((), (), s32[]{:S(2)}) async-start(), calls=%async_computation.11 | async-start | bytes 5013504 | tf_op jit(solution)/shard_map/all_gather | solution.py:314
  9.1 79.8 %copy-start.10 = (bf16[576,256]{1,0:T(8,128)(2,1)S(1)}, bf16[576,256]{1,0:T(8,128)(2,1)}, u32[]{:S(2)}) copy-start(bf16[576,256]{1,0:T(8,128)(2,1)} %param.13) | copy-start | bytes 884740
  9.1 79.8 %copy-start.13 = (bf16[576,128]{1,0:T(8,128)(2,1)S(1)}, bf16[576,128]{1,0:T(8,128)(2,1)}, u32[]{:S(2)}) copy-start(bf16[576,128]{1,0:T(8,128)(2,1)} %param.9) | copy-start | bytes 442372
  27.4 22.7 %all-to-all-start.5 = ((s32[16,1,1]{2,1,0:T(1,128)}), s32[16,1,1]{2,1,0:T(1,128)S(1)}, u32[]{:S(2)}, u32[]{:S(2)}) async-start(s32[16,1,1]{2,1,0:T(1,128)} %broadcast_in_dim.20), calls=%async_computation.5 | async-start | bytes 16384 | tf_op jit(solution)/shard_map/all_to_all | solution.py:293
  50.2 18.0 %all-to-all-start.6 = ((f32[4,576,128]{2,1,0:T(8,128)}), f32[4,576,128]{2,1,0:T(8,128)S(1)}, u32[]{:S(2)}, u32[]{:S(2)}) async-start(f32[4,576,128]{2,1,0:T(8,128)} %bitcast.55), calls=%async_computation.6 | async-start | bytes 2359296 | tf_op jit(solution)/shard_map/all_to_all | solution.py:293
  54.2 227.1 %reduce-scatter.2.cloned.1.call-start = ((), (), s32[]{:S(2)}) async-start(), calls=%async_computation.12 | async-start | bytes 5013504 | tf_op jit(solution)/shard_map/reduce_scatter | solution.py:439
  54.2 14.1 %collective-permute-start.10 = (bf16[128,128]{1,0:T(8,128)(2,1)S(1)}, bf16[128,128]{1,0:T(8,128)(2,1)S(1)}, u32[]{:S(2)}, u32[]{:S(2)}) collective-permute-start(bf16[128,128]{1,0:T(8,128)(2,1)S(1)} %get-tuple-element.162), channel_id=1, source_target_pairs={{0,4},{4,8},{8,12},{12,16},{16,20},{20,24},{24,28},{28,32},{32,36}... | collective-permute-start | bytes 98312 | tf_op jit(solution)/shard_map/ppermute | solution.py:344
  58.8 9.5 %collective-permute-start.11 = (bf16[128,128]{1,0:T(8,128)(2,1)S(1)}, bf16[128,128]{1,0:T(8,128)(2,1)S(1)}, u32[]{:S(2)}, u32[]{:S(2)}) collective-permute-start(bf16[128,128]{1,0:T(8,128)(2,1)S(1)} %get-tuple-element.161), channel_id=1, source_target_pairs={{4,0},{8,4},{12,8},{16,12},{20,16},{24,20},{28,24},{32,28},{36,32}... | collective-permute-start | bytes 98312 | tf_op jit(solution)/shard_map/ppermute | solution.py:345
  60.8 2.9 copy-start.24
  88.8 10.0 %copy-start.7 = (bf16[576,128]{1,0:T(8,128)(2,1)}, bf16[576,128]{1,0:T(8,128)(2,1)S(1)}, u32[]{:S(2)}) copy-start(bf16[576,128]{1,0:T(8,128)(2,1)S(1)} %get-tuple-element.95.key) | copy-start | bytes 442372 | tf_op jit(solution)/shard_map/cond
  88.8 10.0 %copy-start.9 = (bf16[576,128]{1,0:T(8,128)(2,1)}, bf16[576,128]{1,0:T(8,128)(2,1)S(1)}, u32[]{:S(2)}) copy-start(bf16[576,128]{1,0:T(8,128)(2,1)S(1)} %get-tuple-element.94.g) | copy-start | bytes 442372 | tf_op jit(solution)/shard_map/cond
  88.8 10.0 %copy-start.11 = (bf16[576,256]{1,0:T(8,128)(2,1)}, bf16[576,256]{1,0:T(8,128)(2,1)S(1)}, u32[]{:S(2)}) copy-start(bf16[576,256]{1,0:T(8,128)(2,1)S(1)} %get-tuple-element.111) | copy-start | bytes 884740 | tf_op jit(solution)/shard_map/cond
  88.8 10.0 %copy-start.14 = (bf16[576,128]{1,0:T(8,128)(2,1)}, bf16[576,128]{1,0:T(8,128)(2,1)S(1)}, u32[]{:S(2)}) copy-start(bf16[576,128]{1,0:T(8,128)(2,1)S(1)} %get-tuple-element.93.q) | copy-start | bytes 442372 | tf_op jit(solution)/shard_map/cond
  88.9 10.0 %copy-start.20 = (s32[128]{0:T(128)}, s32[128]{0:T(128)S(1)}, u32[]{:S(2)}) copy-start(s32[128]{0:T(128)S(1)} %get-tuple-element.103.global_pos) | copy-start | bytes 1540 | tf_op jit(solution)/shard_map/cond
  88.9 10.0 %copy-start.15 = (s32[128]{0:T(128)}, s32[128]{0:T(128)S(1)}, u32[]{:S(2)}) copy-start(s32[128]{0:T(128)S(1)} %get-tuple-element.102.asked) | copy-start | bytes 1540 | tf_op jit(solution)/shard_map/cond
  88.9 10.0 %copy-start.17 = (s32[2]{0:T(128)}, s32[2]{0:T(128)S(1)}, u32[]{:S(2)}) copy-start(s32[2]{0:T(128)S(1)} %get-tuple-element.101.where) | copy-start | bytes 28 | tf_op jit(solution)/shard_map/cond
  88.9 10.0 %copy-start.25 = (s32[27]{0:T(128)}, s32[27]{0:T(128)S(1)}, u32[]{:S(2)}) copy-start(s32[27]{0:T(128)S(1)} %get-tuple-element.91.names) | copy-start | bytes 328 | tf_op jit(solution)/shard_map/cond
  88.9 10.0 %copy-start.26 = (s32[27]{0:T(128)}, s32[27]{0:T(128)S(1)}, u32[]{:S(2)}) copy-start(s32[27]{0:T(128)S(1)} %get-tuple-element.92.ranks) | copy-start | bytes 328 | tf_op jit(solution)/shard_map/cond
  88.9 10.0 %copy-start.27 = (s32[2]{0:T(128)}, s32[2]{0:T(128)S(1)}, u32[]{:S(2)}) copy-start(s32[2]{0:T(128)S(1)} %get-tuple-element.90.place) | copy-start | bytes 28 | tf_op jit(solution)/shard_map/cond
  88.9 22.2 %copy-start.22 = (s32[128]{0:T(128)}, s32[128]{0:T(128)S(1)}, u32[]{:S(2)}) copy-start(s32[128]{0:T(128)S(1)} %get-tuple-element.100.global_rank) | copy-start | bytes 1540 | tf_op jit(solution)/shard_map/cond
  98.9 45.6 %all-to-all-start.2 = ((bf16[8,1344,128]{2,1,0:T(8,128)(2,1)}), bf16[8,1344,128]{2,1,0:T(8,128)(2,1)S(1)}, u32[]{:S(2)}, u32[]{:S(2)}) async-start(bf16[8,1344,128]{2,1,0:T(8,128)(2,1)} %branch_1_fun.3), calls=%async_computation.2 | async-start | bytes 5505024 | tf_op jit(solution)/shard_map/cond/branch_1_fun/all_to_all | solution.py:293
  154.4 1.5 copy-start.3
  155.9 24.4 %copy-start.12 = (bf16[576,256]{1,0:T(8,128)(2,1)S(1)}, bf16[576,256]{1,0:T(8,128)(2,1)}, u32[]{:S(2)}) copy-start(bf16[576,256]{1,0:T(8,128)(2,1)} %copy-done.11) | copy-start | bytes 884740 | tf_op jit(solution)/shard_map/cond
  155.9 38.0 %copy-start.16 = (s32[128]{0:T(128)S(1)}, s32[128]{0:T(128)}, u32[]{:S(2)}) copy-start(s32[128]{0:T(128)} %copy-done.15) | copy-start | bytes 1540 | tf_op jit(solution)/shard_map/cond
  155.9 38.0 %copy-start.18 = (s32[2]{0:T(128)S(1)}, s32[2]{0:T(128)}, u32[]{:S(2)}) copy-start(s32[2]{0:T(128)} %copy-done.17) | copy-start | bytes 28 | tf_op jit(solution)/shard_map/cond
  155.9 38.0 %copy-start.21 = (s32[128]{0:T(128)S(1)}, s32[128]{0:T(128)}, u32[]{:S(2)}) copy-start(s32[128]{0:T(128)} %copy-done.20) | copy-start | bytes 1540 | tf_op jit(solution)/shard_map/cond
  155.9 38.0 %copy-start.23 = (s32[128]{0:T(128)S(1)}, s32[128]{0:T(128)}, u32[]{:S(2)}) copy-start(s32[128]{0:T(128)} %copy-done.22) | copy-start | bytes 1540 | tf_op jit(solution)/shard_map/cond
  155.9 37.9 %all-to-all-start.3 = ((bf16[8,1344,128]{2,1,0:T(8,128)(2,1)}), bf16[8,1344,128]{2,1,0:T(8,128)(2,1)S(1)}, u32[]{:S(2)}, u32[]{:S(2)}) async-start(bf16[8,1344,128]{2,1,0:T(8,128)(2,1)} %copy-done.3), calls=%async_computation.3 | async-start | bytes 5505024 | tf_op jit(solution)/shard_map/cond/branch_1_fun/all_to_all | solution.py:293
  160.5 17.7 %collective-permute-start.5 = (bf16[576,128]{1,0:T(8,128)(2,1)S(1)}, bf16[576,128]{1,0:T(8,128)(2,1)S(1)}, u32[]{:S(2)}, u32[]{:S(2)}) collective-permute-start(bf16[576,128]{1,0:T(8,128)(2,1)S(1)} %get-tuple-element.105), channel_id=1, source_target_pairs={{0,1},{1,2},{2,3},{3,0},{4,5},{5,6},{6,7},{7,4},{8,9},{9,10},{10,1... | collective-permute-start | bytes 442376 | tf_op jit(solution)/shard_map/cond/branch_1_fun/ppermute | solution.py:401
  163.8 15.1 %collective-permute-start.6 = (bf16[576,128]{1,0:T(8,128)(2,1)S(1)}, bf16[576,128]{1,0:T(8,128)(2,1)S(1)}, u32[]{:S(2)}, u32[]{:S(2)}) collective-permute-start(bf16[576,128]{1,0:T(8,128)(2,1)S(1)} %get-tuple-element.105), channel_id=1, source_target_pairs={{0,2},{1,3},{2,0},{3,1},{4,6},{5,7},{6,4},{7,5},{8,10},{9,11},{10,... | collective-permute-start | bytes 442376 | tf_op jit(solution)/shard_map/cond/branch_1_fun/ppermute | solution.py:401
  168.1 11.5 %collective-permute-start.7 = (bf16[576,128]{1,0:T(8,128)(2,1)S(1)}, bf16[576,128]{1,0:T(8,128)(2,1)S(1)}, u32[]{:S(2)}, u32[]{:S(2)}) collective-permute-start(bf16[576,128]{1,0:T(8,128)(2,1)S(1)} %get-tuple-element.105), channel_id=1, source_target_pairs={{0,3},{1,0},{2,1},{3,2},{4,7},{5,4},{6,5},{7,6},{8,11},{9,8},{10,9... | collective-permute-start | bytes 442376 | tf_op jit(solution)/shard_map/cond/branch_1_fun/ppermute | solution.py:401
  171.9 19.3 %collective-permute-start.8 = (bf16[128,128]{1,0:T(8,128)(2,1)S(1)}, bf16[128,128]{1,0:T(8,128)(2,1)}, u32[]{:S(2)}, u32[]{:S(2)}) collective-permute-start(bf16[128,128]{1,0:T(8,128)(2,1)S(1)} %get-tuple-element.160), channel_id=1, source_target_pairs={{0,4},{4,8},{8,12},{12,16},{16,20},{20,24},{24,28},{28,32},{32,36}... | collective-permute-start | bytes 98312 | tf_op jit(solution)/shard_map/cond/branch_1_fun/ppermute | solution.py:404
  176.3 16.9 %collective-permute-start.9 = (bf16[128,128]{1,0:T(8,128)(2,1)S(1)}, bf16[128,128]{1,0:T(8,128)(2,1)}, u32[]{:S(2)}, u32[]{:S(2)}) collective-permute-start(bf16[128,128]{1,0:T(8,128)(2,1)S(1)} %get-tuple-element.159), channel_id=1, source_target_pairs={{4,0},{8,4},{12,8},{16,12},{20,16},{24,20},{28,24},{32,28},{36,32}... | collective-permute-start | bytes 98312 | tf_op jit(solution)/shard_map/cond/branch_1_fun/ppermute | solution.py:405
  204.4 65.8 %copy-start.8 = (bf16[4,128,256]{2,1,0:T(8,128)(2,1)S(1)}, bf16[4,128,256]{2,1,0:T(8,128)(2,1)}, u32[]{:S(2)}) copy-start(bf16[4,128,256]{2,1,0:T(8,128)(2,1)} %gather_fusion) | copy-start | bytes 786436
  205.5 10.0 %collective-permute-start.12 = (f32[4,64,256]{2,1,0:T(8,128)S(1)}, f32[4,64,256]{2,1,0:T(8,128)S(1)}, u32[]{:S(2)}, u32[]{:S(2)}) collective-permute-start(f32[4,64,256]{2,1,0:T(8,128)S(1)} %dynamic-slice_bitcast_fusion), channel_id=1, source_target_pairs={{0,16},{4,20},{8,24},{12,28},{16,0},{20,4},{24,8},{28,12},{1,17},{... | collective-permute-start | bytes 786440 | tf_op jit(solution)/shard_map/ppermute | solution.py:448
  216.5 6.1 %collective-permute-start.13 = (f32[2,64,256]{2,1,0:T(8,128)S(1)}, f32[2,64,256]{2,1,0:T(8,128)S(1)}, u32[]{:S(2)}, u32[]{:S(2)}) collective-permute-start(f32[2,64,256]{2,1,0:T(8,128)S(1)} %dynamic-slice_bitcast_fusion.1), channel_id=1, source_target_pairs={{0,8},{4,12},{8,0},{12,4},{16,24},{20,28},{24,16},{28,20},{1,9},{5... | collective-permute-start | bytes 393224 | tf_op jit(solution)/shard_map/ppermute | solution.py:448
  222.6 5.7 %collective-permute-start.14 = (f32[1,64,256]{2,1,0:T(8,128)S(1)}, f32[1,64,256]{2,1,0:T(8,128)S(1)}, u32[]{:S(2)}, u32[]{:S(2)}) collective-permute-start(f32[1,64,256]{2,1,0:T(8,128)S(1)} %constant_dynamic-slice_fusion), channel_id=1, source_target_pairs={{0,4},{4,0},{8,12},{12,8},{16,20},{20,16},{24,28},{28,24},{1,5},{5... | collective-permute-start | bytes 196616 | tf_op jit(solution)/shard_map/ppermute | solution.py:448
  264.1 15.6 %all-to-all-start.9 = ((f32[8,64,256]{2,1,0:T(8,128)}), f32[8,64,256]{2,1,0:T(8,128)S(1)}, u32[]{:S(2)}, u32[]{:S(2)}) async-start(f32[8,64,256]{2,1,0:T(8,128)} %broadcast_in_dim.22), calls=%async_computation.10 | async-start | bytes 1048576 | tf_op jit(solution)/shard_map/all_to_all | solution.py:293
  281.2 1.0 copy-start.4
Sparse Core Ops, SparseCore 0:
  10.7 78.0 all-gather.1
  204.6 72.1 reduce-scatter.1

commit v6 on v5

--- a/solution.py
+++ b/solution.py
@@ -40,45 +40,34 @@
     )
 
 
-def serve_kernel(where, asked, global_pos, global_rank, lane_blocks, send, panel):
-    me, blocks = where[0], where[1]
-    tokens = blocks * BLOCK
+def serve_kernel(asked, global_block, global_row, lane_blocks, send, panel):
+    room = panel.shape[0] // 2
     most = asked.shape[0] // LANES
-    room = panel.shape[0] // 2
     slots = send.shape[1] // PAIR if room < GLOBALS else most
-
-    def serve(number, carry):
-        to = number // slots
-        rank = number % slots
-        rows = pl.ds(pl.multiple_of(rank * PAIR, PAIR), PAIR)
-        send[to, rows, :] = lane_blocks[jnp.maximum(asked[to * most + rank], 0)]
-        return carry
-
-    lax.fori_loop(0, LANES * slots, serve, 0)
+    for to in range(LANES):
+        for rank in range(slots):
+            wanted = jnp.maximum(asked[to * most + rank], 0)
+            send[to, rank * PAIR : (rank + 1) * PAIR, :] = lane_blocks[wanted]
 
     panel[...] = jnp.zeros_like(panel)
     row_number = lax.broadcasted_iota(jnp.int32, (TILE, panel.shape[1]), 0)
 
     def pick(number, carry):
-        position = global_pos[number]
-        owner = position // tokens
-        row = position % tokens
-
-        @pl.when(owner % LANES == me)
+        source, inside = global_block[number], global_row[number]
+
+        @pl.when(source >= 0)
         def _():
-            source = owner // LANES * blocks + row // BLOCK
-            inside = row % BLOCK
             first = pl.multiple_of(inside // TILE * TILE, TILE)
             hit = row_number == inside % TILE
             for half in range(2):
                 rows = lane_blocks[source, pl.ds(first + half * BLOCK, TILE), :]
-                panel[pl.ds(global_rank[number] + half * room, 1), :] = jnp.sum(
+                panel[pl.ds(number + half * room, 1), :] = jnp.sum(
                     jnp.where(hit, rows.astype(jnp.float32), 0.0), axis=0, keepdims=True
                 )
 
         return carry
 
-    lax.fori_loop(0, GLOBALS, pick, 0)
+    lax.fori_loop(0, room, pick, 0)
     panel_rows = panel[...].astype(send.dtype)
     for to in range(LANES):
         send[to, slots * PAIR :, :] = panel_rows
@@ -195,7 +184,7 @@
             send[a, pl.ds(b + BLOCK, BLOCK), :] = dv[first : first + BLOCK].astype(bf16)
         return carry
 
-    lax.fori_loop(0, blocks, one, 0)
+    lax.fori_loop(0, blocks, one, 0, unroll=R)
     for side, rows in enumerate((pl.ds(0, BLOCK), pl.ds(BLOCK + tokens, BLOCK))):
         rims[side, :BLOCK, :] = key_grad[rows, :].astype(bf16)
         rims[side, BLOCK:, :] = value_grad[rows, :].astype(bf16)
@@ -207,55 +196,40 @@
             send[lane, begin : begin + room, :] = rows[lane * room : (lane + 1) * room]
 
 
-def collect_kernel(where, asked, global_pos, global_rank, returned, lane_grads, sums, panel):
-    me, blocks = where[0], where[1]
-    tokens = blocks * BLOCK
+def collect_kernel(asked, global_block, global_row, returned, lane_grads, sums, panel):
+    room = panel.shape[0] // 2
     most = asked.shape[0] // LANES
-    room = panel.shape[0] // 2
     slots = returned.shape[1] // PAIR if room < GLOBALS else most
     f32 = jnp.float32
     sums[...] = jnp.zeros_like(sums)
-
-    def add(number, carry):
-        source = number // slots
-        rank = number % slots
-        wanted = asked[source * most + rank]
-
-        @pl.when(wanted >= 0)
-        def _():
-            rows = pl.ds(pl.multiple_of(rank * PAIR, PAIR), PAIR)
-            sums[wanted] += returned[source, rows, :].astype(f32)
-
-        return carry
-
-    lax.fori_loop(0, LANES * slots, add, 0)
+    for source in range(LANES):
+        for rank in range(slots):
+            wanted = asked[source * most + rank]
+
+            @pl.when(wanted >= 0)
+            def _():
+                rows = returned[source, rank * PAIR : (rank + 1) * PAIR, :]
+                sums[wanted] += rows.astype(f32)
+
     total_rows = jnp.zeros(panel.shape, f32)
     for lane in range(LANES):
         total_rows += returned[lane, slots * PAIR :, :].astype(f32)
     panel[...] = total_rows
 
     def spread(number, carry):
-        position = global_pos[number]
-        owner = position // tokens
-        row = position % tokens
-
-        @pl.when(owner % LANES == me)
+        to = global_block[number]
+
+        @pl.when(to >= 0)
         def _():
-            to = owner // LANES * blocks + row // BLOCK
             for half in range(2):
-                sums[to, pl.ds(row % BLOCK + half * BLOCK, 1), :] += panel[
-                    pl.ds(global_rank[number] + half * room, 1), :
+                sums[to, pl.ds(global_row[number] + half * BLOCK, 1), :] += panel[
+                    pl.ds(number + half * room, 1), :
                 ]
 
         return carry
 
-    lax.fori_loop(0, GLOBALS, spread, 0)
-
-    def write(number, carry):
-        lane_grads[number] = sums[number].astype(lane_grads.dtype)
-        return carry
-
-    lax.fori_loop(0, lane_grads.shape[0], write, 0)
+    lax.fori_loop(0, room, spread, 0)
+    lane_grads[...] = sums[...].astype(lane_grads.dtype)
 
 
 def finish_kernel(
@@ -305,7 +279,6 @@
     slab, me, head = lax.axis_index("slab"), lax.axis_index("lane"), lax.axis_index("head")
     position, seq_count = slab * LANES + me, slabs * LANES
     smem, vmem = whole(pltpu.SMEM), whole()
-    where = jnp.stack([me, jnp.int32(blocks)]).astype(jnp.int32)
 
     own = jnp.concatenate(
         [key_states.reshape(blocks, BLOCK, columns), value_states.reshape(blocks, BLOCK, columns)],
@@ -327,6 +300,10 @@
     number = jnp.arange(GLOBALS)
     same = (global_lane[:, None] == global_lane[None, :]) & (number[None, :] < number[:, None])
     global_rank = jnp.sum(same.astype(jnp.int32), axis=1)
+    hit = (global_rank[None, :] == number[:, None]) & (global_lane == me)[None, :]
+    global_block = global_pos // tokens // LANES * blocks + global_pos % tokens // BLOCK
+    global_block = jnp.max(jnp.where(hit, global_block[None, :], -1), axis=1)
+    global_row = jnp.max(jnp.where(hit, (global_pos % BLOCK)[None, :], 0), axis=1)
     heard = exchange(jnp.concatenate([wanted, load], axis=1), "lane")
     asked = heard[:, :slabs].reshape(-1)
     load = jnp.max(spread(jnp.max(heard[:, slabs:]).reshape(1), "slab"))
@@ -347,9 +324,10 @@
     order = (head - jnp.arange(heads)) % heads
     weight_rows = out_weight.reshape(heads, columns, -1).at[order].get(mode="promise_in_bounds")
     weight_rows = weight_rows.reshape(out_weight.shape)
-    lane_blocks, asked, fits, grad_att, left, right, weight_rows = lax.optimization_barrier(
-        (lane_blocks, asked, fits, grad_att, left, right, weight_rows)
-    )
+    beside = (lane_blocks, asked, fits, grad_att, left, right, weight_rows)
+    beside = lax.optimization_barrier(beside + (global_lane, global_rank, global_block, global_row))
+    lane_blocks, asked, fits, grad_att, left, right, weight_rows = beside[:7]
+    global_lane, global_rank, global_block, global_row = beside[7:]
     place = jnp.stack([position * blocks, seq_count * blocks - 1]).astype(jnp.int32)
     padded = tokens + PAIR
 
@@ -359,10 +337,10 @@
         served = call(
             serve_kernel,
             shape((LANES, sent_rows, columns), bf16),
-            [smem, smem, smem, smem, vmem],
+            [smem, smem, smem, vmem],
             [pltpu.VMEM((2 * room, columns), f32)],
             moved=8 << 20,
-        )(where, asked, global_pos, global_rank, lane_blocks)
+        )(asked, global_block, global_row, lane_blocks)
         arrived = exchange(served, "lane")
         attended, query_grad, key_part, value_part, rims, sent = call(
             attention_kernel,
@@ -413,13 +391,13 @@
         lane_grads = call(
             collect_kernel,
             shape((slabs * blocks, PAIR, columns), bf16),
-            [smem, smem, smem, smem, vmem],
+            [smem, smem, smem, vmem],
             [
                 pltpu.VMEM((slabs * blocks, PAIR, columns), f32),
                 pltpu.VMEM((2 * room, columns), f32),
             ],
             moved=10 << 20,
-        )(where, asked, global_pos, global_rank, returned)
+        )(asked, global_block, global_row, returned)
         return (
             everywhere,
             query_grad,

time: 295 us -> 283 us (0.959)
  blocking collectives: 48.6 us -> 34.2 us
  Pallas kernels: 32.3 us -> 20.8 us
  starting transfers between devices: 72.8 us -> 81.1 us
  waiting for transfers between devices: 95.2 us -> 99.8 us
    all_to_all x3 -> x2, blocking collectives: 48.6 us -> 34.2 us  [exchange(): return lax.all_to_all(array, axis, split_axis=0, concat_axis=0, tiled=True)]
    all_to_all x5 -> x6, starting transfers between devices: 38.4 us -> 48.3 us  [exchange(): return lax.all_to_all(array, axis, split_axis=0, concat_axis=0, tiled=True)]
    all_to_all x5 -> x6, waiting for transfers between devices: 53.3 us -> 59.4 us  [exchange(): return lax.all_to_all(array, axis, split_axis=0, concat_axis=0, tiled=True)]
    pallas_call x1, Pallas kernels: 10.6 us -> 5.1 us  [middle(): call(collect_kernel, shape((slabs * blocks, PAIR, columns), bf16), [smem,...]
    pallas_call x1, Pallas kernels: 9.91 us -> 4.92 us  [middle(): call(serve_kernel, shape((LANES, sent_rows, columns), bf16), [smem, smem,...]
  transfers between devices with their start and end apart: 17 -> 18, of which waited for: 11 -> 11; matrix products, arithmetic and copies ran while one was open for 7% -> 8% of each run, Pallas kernels for 0% -> 0%
where the time goes in v6:
time: 283 us; the launch traced here: 279 us
  waiting for transfers between devices  99.8 us (35%)
  starting transfers between devices  81.1 us (29%)
  blocking collectives  34.2 us (12%)
  Pallas kernels  20.8 us (7%)
  between operations  16.3 us (6%)
  local copies, waits for them, and re-layouts  14.2 us (5%)
  other arithmetic  6.97 us (2%)
  matrix products  5.67 us (2%)
    all_to_all x6, waiting for transfers between devices, exchange(): return lax.all_to_all(array, axis, split_axis=0, concat_axis=0, tiled=True)  59.4 us
    all_to_all x6, starting transfers between devices, exchange(): return lax.all_to_all(array, axis, split_axis=0, concat_axis=0, tiled=True)  48.3 us
    all_to_all x2, blocking collectives, exchange(): return lax.all_to_all(array, axis, split_axis=0, concat_axis=0, tiled=True)  34.2 us
    all_gather x1, waiting for transfers between devices, shards(): lane_blocks = lax.all_gather(own, 'slab', axis=0, tiled=True)  18.4 us
    ppermute x3, starting transfers between devices, shards(): other = lax.ppermute(other, 'lane', [(i, i ^ step) for i in range(LANES)])  10.9 us
    ppermute x3, waiting for transfers between devices, shards(): other = lax.ppermute(other, 'lane', [(i, i ^ step) for i in range(LANES)])  10.8 us
    ppermute x3, starting transfers between devices, middle(): lax.ppermute(attended, 'head', [(i, (i + k) % heads) for i in range(heads)])  10.2 us
    ppermute x1, waiting for transfers between devices, middle(): from_left = lax.ppermute(rims[1], seq, forth)  9.13 us
  transfers between devices with their start and end apart: 18, of which 11 were waited for; matrix products, arithmetic and copies ran while one was open for 8% of the time, Pallas kernels for 0%

profile of v6, /device:TPU:1, one launch (start us, length us, event | category | flops | bytes accessed | tf_op | source)
XLA Modules:
  0.0 279.2 jit_solution(14593063916939616769)
XLA Ops:
  7.2 1.8 pad_maximum_fusion
  9.0 0.8 copy.30
  9.9 0.1 reshape.220
  10.0 0.2 convert_reduce_fusion.1
  10.1 0.6 fusion.12
  10.8 0.1 select_reduce_fusion.2
  11.6 0.6 concatenate.13
  12.2 10.1 %all-to-all-start.4 = ((s32[8,1,17]{2,1,0:T(1,128)}), s32[8,1,17]{2,1,0:T(1,128)S(1)}, u32[]{:S(2)}, u32[]{:S(2)}) async-start(s32[8,1,17]{2,1,0:T(1,128)} %bitcast.9), calls=%async_computation.4 | async-start | bytes 8192 | tf_op jit(solution)/shard_map/all_to_all | solution.py:267
  22.3 0.8 fusion.4
  23.1 3.5 %collective-permute-start.10 = (bf16[128,128]{1,0:T(8,128)(2,1)S(1)}, bf16[128,128]{1,0:T(8,128)(2,1)S(1)}, u32[]{:S(2)}, u32[]{:S(2)}) collective-permute-start(bf16[128,128]{1,0:T(8,128)(2,1)S(1)} %get-tuple-element.176), channel_id=1, source_target_pairs={{0,4},{4,8},{8,12},{12,16},{16,20},{20,24},{24,28},{28,32},{32,36}... | collective-permute-start | bytes 98312 | tf_op jit(solution)/shard_map/ppermute | solution.py:321
  26.6 1.9 collective-permute-start.11
  28.6 1.3 convolution_bitcast_fusion
  29.9 1.1 copy.37
  31.0 0.7 slice_reduce_fusion
  31.7 1.2 broadcast_in_dim.62
  33.0 10.8 %all-to-all-start.5 = ((s32[16,1,1]{2,1,0:T(1,128)}), s32[16,1,1]{2,1,0:T(1,128)S(1)}, u32[]{:S(2)}, u32[]{:S(2)}) async-start(s32[16,1,1]{2,1,0:T(1,128)} %broadcast_in_dim.62), calls=%async_computation.5 | async-start | bytes 16384 | tf_op jit(solution)/shard_map/all_to_all | solution.py:267
  43.8 11.3 %all-to-all-done.5 = s32[16,1,1]{2,1,0:T(1,128)S(1)} async-done(((s32[16,1,1]{2,1,0:T(1,128)}), s32[16,1,1]{2,1,0:T(1,128)S(1)}, u32[]{:S(2)}, u32[]{:S(2)}) %all-to-all-start.5) | async-done | bytes 96 | tf_op jit(solution)/shard_map/all_to_all | solution.py:267
  55.1 4.0 %all-to-all-start.6 = ((f32[4,576,128]{2,1,0:T(8,128)}), f32[4,576,128]{2,1,0:T(8,128)S(1)}, u32[]{:S(2)}, u32[]{:S(2)}) async-start(f32[4,576,128]{2,1,0:T(8,128)} %bitcast.54), calls=%async_computation.6 | async-start | bytes 2359296 | tf_op jit(solution)/shard_map/all_to_all | solution.py:267
  59.2 0.2 convert_reduce_fusion
  59.3 0.1 select_reduce_fusion
  59.5 0.6 reduce_max.67
  60.8 1.3 gather_fusion
  62.2 0.7 reduce_max.66
  63.5 6.8 %all-to-all-done.6 = f32[4,576,128]{2,1,0:T(8,128)S(1)} async-done(((f32[4,576,128]{2,1,0:T(8,128)}), f32[4,576,128]{2,1,0:T(8,128)S(1)}, u32[]{:S(2)}, u32[]{:S(2)}) %all-to-all-start.6) | async-done | bytes 1179680 | tf_op jit(solution)/shard_map/all_to_all | solution.py:267
  70.3 18.4 %all-gather.2.cloned.1.call-done = bf16[144,128,128]{2,1,0:T(8,128)(2,1)} async-done(((bf16[9,128,128]{2,1,0:T(8,128)(2,1)}), bf16[144,128,128]{2,1,0:T(8,128)(2,1)}) %all-gather.2.cloned.1.call-update) | async-done | bytes 4718608 | tf_op jit(solution)/shard_map/all_gather | solution.py:287
  88.7 104.6 %conditional.1 = (bf16[576,512]{1,0:T(8,128)(2,1)}, bf16[576,128]{1,0:T(8,128)(2,1)}, f32[704,128]{1,0:T(8,128)}, f32[704,128]{1,0:T(8,128)}, bf16[128,128]{1,0:...) conditional(s32[]{:T(128)} %convert_element_type.18, ...), branch_computations={%region_10.11_spmd, %region_11.12_spmd} | conditional | flops 1224868096 | bytes 102271872 | solution.py:415
  88.9 4.9 %branch_1_fun.3 = bf16[8,1344,128]{2,1,0:T(8,128)(2,1)} custom-call(s32[128]{0:T(128)S(1)} %get-tuple-element.101.asked, s32[128]{0:T(128)S(1)} %get-tuple-element.102.global_block, s32[128]{0:T(128)S(1)} %get-tuple-element.103.global_row, bf16[144,128,128]{2,1,0:T(8,128)(2,1)} %get-tuple-element.104.lane_blocks), custom_call_target="tpu_custom_call" | custom-call | bytes 8388608 | tf_op jit(solution)/shard_map/cond/branch_1_fun/pallas_call | solution.py:337
  93.9 12.7 %all-to-all-start.2 = ((bf16[8,1344,128]{2,1,0:T(8,128)(2,1)}), bf16[8,1344,128]{2,1,0:T(8,128)(2,1)S(1)}, u32[]{:S(2)}, u32[]{:S(2)}) async-start(bf16[8,1344,128]{2,1,0:T(8,128)(2,1)} %branch_1_fun.3), calls=%async_computation.2 | async-start | bytes 5505024 | tf_op jit(solution)/shard_map/cond/branch_1_fun/all_to_all | solution.py:267
  106.6 0.1 copy.29.global_place
  106.7 33.2 %all-to-all-done.2.arrived = bf16[8,1344,128]{2,1,0:T(8,128)(2,1)S(1)} async-done(((bf16[8,1344,128]{2,1,0:T(8,128)(2,1)}), bf16[8,1344,128]{2,1,0:T(8,128)(2,1)S(1)}, u32[]{:S(2)}, u32[]{:S(2)}) %all-to-all-start.2) | async-done | bytes 2752544 | tf_op jit(solution)/shard_map/cond/branch_1_fun/all_to_all | solution.py:267
  139.9 8.9 %branch_1_fun.4 = (bf16[576,128]{1,0:T(8,128)(2,1)S(1)}, bf16[576,128]{1,0:T(8,128)(2,1)}, f32[704,128]{1,0:T(8,128)}, f32[704,128]{1,0:T(8,128)}, bf16[2,128,12...) custom-call(s32[2]{0:T(128)} %copy-done.24, s32[27]{0:T(128)} %copy-done.22, s32[27]{0:T(128)} %copy-done.23, ...), custom_call_target="tpu_custom_call" | custom-call | flops 1073741824 | bytes 12582912 | tf_op jit(solution)/shard_map/cond/branch_1_fun/pallas_call | solution.py:345
  148.8 1.5 copy-done.3
  150.3 4.6 %all-to-all-start.3 = ((bf16[8,1344,128]{2,1,0:T(8,128)(2,1)}), bf16[8,1344,128]{2,1,0:T(8,128)(2,1)S(1)}, u32[]{:S(2)}, u32[]{:S(2)}) async-start(bf16[8,1344,128]{2,1,0:T(8,128)(2,1)} %copy-done.3), calls=%async_computation.3 | async-start | bytes 5505024 | tf_op jit(solution)/shard_map/cond/branch_1_fun/all_to_all | solution.py:267
  154.8 2.7 collective-permute-start.5
  157.5 4.5 %collective-permute-start.6 = (bf16[576,128]{1,0:T(8,128)(2,1)S(1)}, bf16[576,128]{1,0:T(8,128)(2,1)S(1)}, u32[]{:S(2)}, u32[]{:S(2)}) collective-permute-start(bf16[576,128]{1,0:T(8,128)(2,1)S(1)} %get-tuple-element.105), channel_id=1, source_target_pairs={{0,2},{1,3},{2,0},{3,1},{4,6},{5,7},{6,4},{7,5},{8,10},{9,11},{10,... | collective-permute-start | bytes 442376 | tf_op jit(solution)/shard_map/cond/branch_1_fun/ppermute | solution.py:379
  162.0 3.0 %collective-permute-start.7 = (bf16[576,128]{1,0:T(8,128)(2,1)S(1)}, bf16[576,128]{1,0:T(8,128)(2,1)S(1)}, u32[]{:S(2)}, u32[]{:S(2)}) collective-permute-start(bf16[576,128]{1,0:T(8,128)(2,1)S(1)} %get-tuple-element.105), channel_id=1, source_target_pairs={{0,3},{1,0},{2,1},{3,2},{4,7},{5,4},{6,5},{7,6},{8,11},{9,8},{10,9... | collective-permute-start | bytes 442376 | tf_op jit(solution)/shard_map/cond/branch_1_fun/ppermute | solution.py:379
  165.0 0.7 constant_dynamic-update-slice_fusion.7
  165.7 4.4 %collective-permute-start.8 = (bf16[128,128]{1,0:T(8,128)(2,1)S(1)}, bf16[128,128]{1,0:T(8,128)(2,1)}, u32[]{:S(2)}, u32[]{:S(2)}) collective-permute-start(bf16[128,128]{1,0:T(8,128)(2,1)S(1)} %get-tuple-element.174), channel_id=1, source_target_pairs={{0,4},{4,8},{8,12},{12,16},{16,20},{20,24},{24,28},{28,32},{32,36}... | collective-permute-start | bytes 98312 | tf_op jit(solution)/shard_map/cond/branch_1_fun/ppermute | solution.py:382
  170.1 1.9 collective-permute-start.9
  172.0 0.7 constant_dynamic-update-slice_fusion.6
  172.7 0.7 constant_dynamic-update-slice_fusion.5
  173.4 0.7 constant_dynamic-update-slice_fusion.4
  174.1 2.3 convolution_multiply_fusion.1
  176.4 9.1 %collective-permute-done.8 = bf16[128,128]{1,0:T(8,128)(2,1)} collective-permute-done((bf16[128,128]{1,0:T(8,128)(2,1)S(1)}, bf16[128,128]{1,0:T(8,128)(2,1)}, u32[]{:S(2)}, u32[]{:S(2)}) %collective-permute-start.8) | collective-permute-done | bytes 32800 | tf_op jit(solution)/shard_map/cond/branch_1_fun/ppermute | solution.py:382
  185.5 2.0 collective-permute-done.9
  187.5 0.7 all-to-all-done.3.returned
  188.2 5.1 %branch_1_fun.5 = bf16[144,128,128]{2,1,0:T(8,128)(2,1)} custom-call(s32[128]{0:T(128)S(1)} %copy-done.16, s32[128]{0:T(128)S(1)} %copy-done.20, s32[128]{0:T(128)S(1)} %copy-done.18, bf16[8,1344,128]{2,1,0:T(8,128)(2,1)S(1)} %all-to-all-done.3.returned), custom_call_target="tpu_custom_call" | custom-call | bytes 10485760 | tf_op jit(solution)/shard_map/cond/branch_1_fun/pallas_call | solution.py:391
  193.4 1.0 dynamic-slice_bitcast_fusion
  194.4 3.5 %collective-permute-start.12 = (f32[4,64,256]{2,1,0:T(8,128)S(1)}, f32[4,64,256]{2,1,0:T(8,128)S(1)}, u32[]{:S(2)}, u32[]{:S(2)}) collective-permute-start(f32[4,64,256]{2,1,0:T(8,128)S(1)} %dynamic-slice_bitcast_fusion), channel_id=1, source_target_pairs={{0,16},{4,20},{8,24},{12,28},{16,0},{20,4},{24,8},{28,12},{1,17},{... | collective-permute-start | bytes 786440 | tf_op jit(solution)/shard_map/ppermute | solution.py:426
  197.9 6.5 %collective-permute-done.12 = f32[4,64,256]{2,1,0:T(8,128)S(1)} collective-permute-done((f32[4,64,256]{2,1,0:T(8,128)S(1)}, f32[4,64,256]{2,1,0:T(8,128)S(1)}, u32[]{:S(2)}, u32[]{:S(2)}) %collective-permute-start.12) | collective-permute-done | bytes 262176 | tf_op jit(solution)/shard_map/ppermute | solution.py:426
  204.4 1.0 bitcast_add_fusion
  205.4 2.6 collective-permute-start.13
  208.0 3.5 %collective-permute-done.13 = f32[2,64,256]{2,1,0:T(8,128)S(1)} collective-permute-done((f32[2,64,256]{2,1,0:T(8,128)S(1)}, f32[2,64,256]{2,1,0:T(8,128)S(1)}, u32[]{:S(2)}, u32[]{:S(2)}) %collective-permute-start.13) | collective-permute-done | bytes 131104 | tf_op jit(solution)/shard_map/ppermute | solution.py:426
  211.5 4.8 %collective-permute-start.14 = (f32[1,64,256]{2,1,0:T(8,128)S(1)}, f32[1,64,256]{2,1,0:T(8,128)S(1)}, u32[]{:S(2)}, u32[]{:S(2)}) collective-permute-start(f32[1,64,256]{2,1,0:T(8,128)S(1)} %constant_dynamic-slice_fusion), channel_id=1, source_target_pairs={{0,4},{4,0},{8,12},{12,8},{16,20},{20,16},{24,28},{28,24},{1,5},{5... | collective-permute-start | bytes 196616 | tf_op jit(solution)/shard_map/ppermute | solution.py:426
  216.3 0.9 collective-permute-done.14
  217.3 17.7 %all_to_all.54 = f32[16,4,256]{2,1,0:T(4,128)S(1)} all-to-all(f32[16,4,256]{2,1,0:T(4,128)S(1)} %reshape.227), channel_id=1, replica_groups=mesh['slab'=16,'lane'=8,'head'=4] {'slab'}, dimensions={0} | all-to-all | bytes 131072 | tf_op jit(solution)/shard_map/all_to_all | solution.py:267
  235.1 16.4 %all_to_all.55 = f32[16,4,256]{2,1,0:T(4,128)S(1)} all-to-all(f32[16,4,256]{2,1,0:T(4,128)S(1)} %broadcast_in_dim.67), channel_id=1, replica_groups=mesh['slab'=16,'lane'=8,'head'=4] {'slab'}, dimensions={0} | all-to-all | bytes 131072 | tf_op jit(solution)/shard_map/all_to_all | solution.py:267
  251.5 0.8 broadcast_in_dim.68
  252.3 6.2 %all-to-all-start.9 = ((f32[8,64,256]{2,1,0:T(8,128)}), f32[8,64,256]{2,1,0:T(8,128)S(1)}, u32[]{:S(2)}, u32[]{:S(2)}) async-start(f32[8,64,256]{2,1,0:T(8,128)} %broadcast_in_dim.68), calls=%async_computation.10 | async-start | bytes 1048576 | tf_op jit(solution)/shard_map/all_to_all | solution.py:267
  258.5 2.1 convolution_convert_fusion
  260.6 7.4 %all-to-all-done.9 = f32[8,64,256]{2,1,0:T(8,128)S(1)} async-done(((f32[8,64,256]{2,1,0:T(8,128)}), f32[8,64,256]{2,1,0:T(8,128)S(1)}, u32[]{:S(2)}, u32[]{:S(2)}) %all-to-all-start.9) | async-done | bytes 524320 | tf_op jit(solution)/shard_map/all_to_all | solution.py:267
  268.0 1.5 gather_fusion.1
  269.5 1.0 copy-done.4
  270.5 1.9 shard_map.110
  (76 shorter events, 0.7 us)
Async XLA Ops:
  7.2 21.4 %copy-start = (bf16[512,256]{1,0:T(8,128)(2,1)S(1)}, bf16[512,256]{1,0:T(8,128)(2,1)}, u32[]{:S(2)}) copy-start(bf16[512,256]{1,0:T(8,128)(2,1)} %param.12) | copy-start | bytes 786436
  7.2 51.9 %copy-start.25 = (s32[128]{0:T(128)S(1)}, s32[128]{0:T(128)}, u32[]{:S(2)}) copy-start(s32[128]{0:T(128)} %param.15) | copy-start | bytes 1540
  7.2 81.5 %all-gather.2.cloned.1.call-start = ((), (), s32[]{:S(2)}) async-start(), calls=%async_computation.11 | async-start | bytes 5013504 | tf_op jit(solution)/shard_map/all_gather | solution.py:287
  9.0 79.7 %copy-start.5 = (bf16[576,128]{1,0:T(8,128)(2,1)S(1)}, bf16[576,128]{1,0:T(8,128)(2,1)}, u32[]{:S(2)}) copy-start(bf16[576,128]{1,0:T(8,128)(2,1)} %param.11) | copy-start | bytes 442372
  9.0 79.7 %copy-start.6 = (bf16[576,128]{1,0:T(8,128)(2,1)S(1)}, bf16[576,128]{1,0:T(8,128)(2,1)}, u32[]{:S(2)}) copy-start(bf16[576,128]{1,0:T(8,128)(2,1)} %param.10) | copy-start | bytes 442372
  9.0 79.7 %copy-start.10 = (bf16[576,256]{1,0:T(8,128)(2,1)S(1)}, bf16[576,256]{1,0:T(8,128)(2,1)}, u32[]{:S(2)}) copy-start(bf16[576,256]{1,0:T(8,128)(2,1)} %param.13) | copy-start | bytes 884740
  9.0 79.7 %copy-start.13 = (bf16[576,128]{1,0:T(8,128)(2,1)S(1)}, bf16[576,128]{1,0:T(8,128)(2,1)}, u32[]{:S(2)}) copy-start(bf16[576,128]{1,0:T(8,128)(2,1)} %param.9) | copy-start | bytes 442372
  12.2 18.8 %all-to-all-start.4 = ((s32[8,1,17]{2,1,0:T(1,128)}), s32[8,1,17]{2,1,0:T(1,128)S(1)}, u32[]{:S(2)}, u32[]{:S(2)}) async-start(s32[8,1,17]{2,1,0:T(1,128)} %bitcast.9), calls=%async_computation.4 | async-start | bytes 8192 | tf_op jit(solution)/shard_map/all_to_all | solution.py:267
  23.1 47.2 %collective-permute-start.10 = (bf16[128,128]{1,0:T(8,128)(2,1)S(1)}, bf16[128,128]{1,0:T(8,128)(2,1)S(1)}, u32[]{:S(2)}, u32[]{:S(2)}) collective-permute-start(bf16[128,128]{1,0:T(8,128)(2,1)S(1)} %get-tuple-element.176), channel_id=1, source_target_pairs={{0,4},{4,8},{8,12},{12,16},{16,20},{20,24},{24,28},{28,32},{32,36}... | collective-permute-start | bytes 98312 | tf_op jit(solution)/shard_map/ppermute | solution.py:321
  26.6 43.7 %collective-permute-start.11 = (bf16[128,128]{1,0:T(8,128)(2,1)S(1)}, bf16[128,128]{1,0:T(8,128)(2,1)S(1)}, u32[]{:S(2)}, u32[]{:S(2)}) collective-permute-start(bf16[128,128]{1,0:T(8,128)(2,1)S(1)} %get-tuple-element.175), channel_id=1, source_target_pairs={{4,0},{8,4},{12,8},{16,12},{20,16},{24,20},{28,24},{32,28},{36,32}... | collective-permute-start | bytes 98312 | tf_op jit(solution)/shard_map/ppermute | solution.py:322
  33.0 22.1 %all-to-all-start.5 = ((s32[16,1,1]{2,1,0:T(1,128)}), s32[16,1,1]{2,1,0:T(1,128)S(1)}, u32[]{:S(2)}, u32[]{:S(2)}) async-start(s32[16,1,1]{2,1,0:T(1,128)} %broadcast_in_dim.62), calls=%async_computation.5 | async-start | bytes 16384 | tf_op jit(solution)/shard_map/all_to_all | solution.py:267
  55.1 15.2 %all-to-all-start.6 = ((f32[4,576,128]{2,1,0:T(8,128)}), f32[4,576,128]{2,1,0:T(8,128)S(1)}, u32[]{:S(2)}, u32[]{:S(2)}) async-start(f32[4,576,128]{2,1,0:T(8,128)} %bitcast.54), calls=%async_computation.6 | async-start | bytes 2359296 | tf_op jit(solution)/shard_map/all_to_all | solution.py:267
  59.1 210.4 %reduce-scatter.2.cloned.1.call-start = ((), (), s32[]{:S(2)}) async-start(), calls=%async_computation.12 | async-start | bytes 5013504 | tf_op jit(solution)/shard_map/reduce_scatter | solution.py:417
  59.1 3.0 %copy-start.21 = (s32[1024]{0:T(1024)}, s32[1024]{0:T(1024)S(1)}, u32[]{:S(2)}) copy-start(s32[1024]{0:T(1024)S(1)} %pad_clamp_fusion) | copy-start | bytes 12292
  88.8 5.0 %copy-start.7 = (bf16[576,128]{1,0:T(8,128)(2,1)}, bf16[576,128]{1,0:T(8,128)(2,1)S(1)}, u32[]{:S(2)}) copy-start(bf16[576,128]{1,0:T(8,128)(2,1)S(1)} %get-tuple-element.95.key) | copy-start | bytes 442372 | tf_op jit(solution)/shard_map/cond
  88.8 5.0 %copy-start.9 = (bf16[576,128]{1,0:T(8,128)(2,1)}, bf16[576,128]{1,0:T(8,128)(2,1)S(1)}, u32[]{:S(2)}) copy-start(bf16[576,128]{1,0:T(8,128)(2,1)S(1)} %get-tuple-element.94.g) | copy-start | bytes 442372 | tf_op jit(solution)/shard_map/cond
  88.8 5.0 %copy-start.11 = (bf16[576,256]{1,0:T(8,128)(2,1)}, bf16[576,256]{1,0:T(8,128)(2,1)S(1)}, u32[]{:S(2)}) copy-start(bf16[576,256]{1,0:T(8,128)(2,1)S(1)} %get-tuple-element.111) | copy-start | bytes 884740 | tf_op jit(solution)/shard_map/cond
  88.8 5.0 %copy-start.14 = (bf16[576,128]{1,0:T(8,128)(2,1)}, bf16[576,128]{1,0:T(8,128)(2,1)S(1)}, u32[]{:S(2)}) copy-start(bf16[576,128]{1,0:T(8,128)(2,1)S(1)} %get-tuple-element.93.q) | copy-start | bytes 442372 | tf_op jit(solution)/shard_map/cond
  88.8 5.0 %copy-start.19 = (s32[128]{0:T(128)}, s32[128]{0:T(128)S(1)}, u32[]{:S(2)}) copy-start(s32[128]{0:T(128)S(1)} %get-tuple-element.102.global_block) | copy-start | bytes 1540 | tf_op jit(solution)/shard_map/cond
  88.8 5.0 %copy-start.22 = (s32[27]{0:T(128)}, s32[27]{0:T(128)S(1)}, u32[]{:S(2)}) copy-start(s32[27]{0:T(128)S(1)} %get-tuple-element.91.names) | copy-start | bytes 328 | tf_op jit(solution)/shard_map/cond
  88.8 5.0 %copy-start.23 = (s32[27]{0:T(128)}, s32[27]{0:T(128)S(1)}, u32[]{:S(2)}) copy-start(s32[27]{0:T(128)S(1)} %get-tuple-element.92.ranks) | copy-start | bytes 328 | tf_op jit(solution)/shard_map/cond
  88.8 5.0 %copy-start.24 = (s32[2]{0:T(128)}, s32[2]{0:T(128)S(1)}, u32[]{:S(2)}) copy-start(s32[2]{0:T(128)S(1)} %get-tuple-element.90.place) | copy-start | bytes 28 | tf_op jit(solution)/shard_map/cond
  88.8 5.0 %copy-start.15 = (s32[128]{0:T(128)}, s32[128]{0:T(128)S(1)}, u32[]{:S(2)}) copy-start(s32[128]{0:T(128)S(1)} %get-tuple-element.101.asked) | copy-start | bytes 1540 | tf_op jit(solution)/shard_map/cond
  88.9 5.0 %copy-start.17 = (s32[128]{0:T(128)}, s32[128]{0:T(128)S(1)}, u32[]{:S(2)}) copy-start(s32[128]{0:T(128)S(1)} %get-tuple-element.103.global_row) | copy-start | bytes 1540 | tf_op jit(solution)/shard_map/cond
  93.9 46.0 %all-to-all-start.2 = ((bf16[8,1344,128]{2,1,0:T(8,128)(2,1)}), bf16[8,1344,128]{2,1,0:T(8,128)(2,1)S(1)}, u32[]{:S(2)}, u32[]{:S(2)}) async-start(bf16[8,1344,128]{2,1,0:T(8,128)(2,1)} %branch_1_fun.3), calls=%async_computation.2 | async-start | bytes 5505024 | tf_op jit(solution)/shard_map/cond/branch_1_fun/all_to_all | solution.py:267
  148.8 1.5 copy-start.3
  150.3 23.9 %copy-start.12 = (bf16[576,256]{1,0:T(8,128)(2,1)S(1)}, bf16[576,256]{1,0:T(8,128)(2,1)}, u32[]{:S(2)}) copy-start(bf16[576,256]{1,0:T(8,128)(2,1)} %copy-done.11) | copy-start | bytes 884740 | tf_op jit(solution)/shard_map/cond
  150.3 37.9 %copy-start.16 = (s32[128]{0:T(128)S(1)}, s32[128]{0:T(128)}, u32[]{:S(2)}) copy-start(s32[128]{0:T(128)} %copy-done.15) | copy-start | bytes 1540 | tf_op jit(solution)/shard_map/cond
  150.3 37.9 %copy-start.18 = (s32[128]{0:T(128)S(1)}, s32[128]{0:T(128)}, u32[]{:S(2)}) copy-start(s32[128]{0:T(128)} %copy-done.17) | copy-start | bytes 1540 | tf_op jit(solution)/shard_map/cond
  150.3 38.0 %copy-start.20 = (s32[128]{0:T(128)S(1)}, s32[128]{0:T(128)}, u32[]{:S(2)}) copy-start(s32[128]{0:T(128)} %copy-done.19) | copy-start | bytes 1540 | tf_op jit(solution)/shard_map/cond
  150.3 37.9 %all-to-all-start.3 = ((bf16[8,1344,128]{2,1,0:T(8,128)(2,1)}), bf16[8,1344,128]{2,1,0:T(8,128)(2,1)S(1)}, u32[]{:S(2)}, u32[]{:S(2)}) async-start(bf16[8,1344,128]{2,1,0:T(8,128)(2,1)} %copy-done.3), calls=%async_computation.3 | async-start | bytes 5505024 | tf_op jit(solution)/shard_map/cond/branch_1_fun/all_to_all | solution.py:267
  154.8 17.2 %collective-permute-start.5 = (bf16[576,128]{1,0:T(8,128)(2,1)S(1)}, bf16[576,128]{1,0:T(8,128)(2,1)S(1)}, u32[]{:S(2)}, u32[]{:S(2)}) collective-permute-start(bf16[576,128]{1,0:T(8,128)(2,1)S(1)} %get-tuple-element.105), channel_id=1, source_target_pairs={{0,1},{1,2},{2,3},{3,0},{4,5},{5,6},{6,7},{7,4},{8,9},{9,10},{10,1... | collective-permute-start | bytes 442376 | tf_op jit(solution)/shard_map/cond/branch_1_fun/ppermute | solution.py:379
  157.5 15.2 %collective-permute-start.6 = (bf16[576,128]{1,0:T(8,128)(2,1)S(1)}, bf16[576,128]{1,0:T(8,128)(2,1)S(1)}, u32[]{:S(2)}, u32[]{:S(2)}) collective-permute-start(bf16[576,128]{1,0:T(8,128)(2,1)S(1)} %get-tuple-element.105), channel_id=1, source_target_pairs={{0,2},{1,3},{2,0},{3,1},{4,6},{5,7},{6,4},{7,5},{8,10},{9,11},{10,... | collective-permute-start | bytes 442376 | tf_op jit(solution)/shard_map/cond/branch_1_fun/ppermute | solution.py:379
  162.0 11.4 %collective-permute-start.7 = (bf16[576,128]{1,0:T(8,128)(2,1)S(1)}, bf16[576,128]{1,0:T(8,128)(2,1)S(1)}, u32[]{:S(2)}, u32[]{:S(2)}) collective-permute-start(bf16[576,128]{1,0:T(8,128)(2,1)S(1)} %get-tuple-element.105), channel_id=1, source_target_pairs={{0,3},{1,0},{2,1},{3,2},{4,7},{5,4},{6,5},{7,6},{8,11},{9,8},{10,9... | collective-permute-start | bytes 442376 | tf_op jit(solution)/shard_map/cond/branch_1_fun/ppermute | solution.py:379
  165.7 19.8 %collective-permute-start.8 = (bf16[128,128]{1,0:T(8,128)(2,1)S(1)}, bf16[128,128]{1,0:T(8,128)(2,1)}, u32[]{:S(2)}, u32[]{:S(2)}) collective-permute-start(bf16[128,128]{1,0:T(8,128)(2,1)S(1)} %get-tuple-element.174), channel_id=1, source_target_pairs={{0,4},{4,8},{8,12},{12,16},{16,20},{20,24},{24,28},{28,32},{32,36}... | collective-permute-start | bytes 98312 | tf_op jit(solution)/shard_map/cond/branch_1_fun/ppermute | solution.py:382
  170.1 17.4 %collective-permute-start.9 = (bf16[128,128]{1,0:T(8,128)(2,1)S(1)}, bf16[128,128]{1,0:T(8,128)(2,1)}, u32[]{:S(2)}, u32[]{:S(2)}) collective-permute-start(bf16[128,128]{1,0:T(8,128)(2,1)S(1)} %get-tuple-element.173), channel_id=1, source_target_pairs={{4,0},{8,4},{12,8},{16,12},{20,16},{24,20},{28,24},{32,28},{36,32}... | collective-permute-start | bytes 98312 | tf_op jit(solution)/shard_map/cond/branch_1_fun/ppermute | solution.py:383
  193.3 65.2 %copy-start.8 = (bf16[4,128,256]{2,1,0:T(8,128)(2,1)S(1)}, bf16[4,128,256]{2,1,0:T(8,128)(2,1)}, u32[]{:S(2)}) copy-start(bf16[4,128,256]{2,1,0:T(8,128)(2,1)} %gather_fusion) | copy-start | bytes 786436
  194.4 10.0 %collective-permute-start.12 = (f32[4,64,256]{2,1,0:T(8,128)S(1)}, f32[4,64,256]{2,1,0:T(8,128)S(1)}, u32[]{:S(2)}, u32[]{:S(2)}) collective-permute-start(f32[4,64,256]{2,1,0:T(8,128)S(1)} %dynamic-slice_bitcast_fusion), channel_id=1, source_target_pairs={{0,16},{4,20},{8,24},{12,28},{16,0},{20,4},{24,8},{28,12},{1,17},{... | collective-permute-start | bytes 786440 | tf_op jit(solution)/shard_map/ppermute | solution.py:426
  205.4 6.1 %collective-permute-start.13 = (f32[2,64,256]{2,1,0:T(8,128)S(1)}, f32[2,64,256]{2,1,0:T(8,128)S(1)}, u32[]{:S(2)}, u32[]{:S(2)}) collective-permute-start(f32[2,64,256]{2,1,0:T(8,128)S(1)} %dynamic-slice_bitcast_fusion.1), channel_id=1, source_target_pairs={{0,8},{4,12},{8,0},{12,4},{16,24},{20,28},{24,16},{28,20},{1,9},{5... | collective-permute-start | bytes 393224 | tf_op jit(solution)/shard_map/ppermute | solution.py:426
  211.5 5.7 %collective-permute-start.14 = (f32[1,64,256]{2,1,0:T(8,128)S(1)}, f32[1,64,256]{2,1,0:T(8,128)S(1)}, u32[]{:S(2)}, u32[]{:S(2)}) collective-permute-start(f32[1,64,256]{2,1,0:T(8,128)S(1)} %constant_dynamic-slice_fusion), channel_id=1, source_target_pairs={{0,4},{4,0},{8,12},{12,8},{16,20},{20,16},{24,28},{28,24},{1,5},{5... | collective-permute-start | bytes 196616 | tf_op jit(solution)/shard_map/ppermute | solution.py:426
  252.3 15.7 %all-to-all-start.9 = ((f32[8,64,256]{2,1,0:T(8,128)}), f32[8,64,256]{2,1,0:T(8,128)S(1)}, u32[]{:S(2)}, u32[]{:S(2)}) async-start(f32[8,64,256]{2,1,0:T(8,128)} %broadcast_in_dim.68), calls=%async_computation.10 | async-start | bytes 1048576 | tf_op jit(solution)/shard_map/all_to_all | solution.py:267
  269.5 1.0 copy-start.4
Sparse Core Ops, SparseCore 0:
  10.7 77.9 all-gather.1
  193.5 71.3 reduce-scatter.1

commit v7 on v6

--- a/solution.py
+++ b/solution.py
@@ -1,3 +1,4 @@
+import functools
 import math
 
 import jax
@@ -13,7 +14,7 @@
 PAIR = 2 * BLOCK
 LANES = 8
 TILE = 16
-FEW = 10
+FEW = (8, 9, 10)
 FEW_ROWS = 32
 R = 3
 GLOBALS = 128
@@ -307,7 +308,8 @@
     heard = exchange(jnp.concatenate([wanted, load], axis=1), "lane")
     asked = heard[:, :slabs].reshape(-1)
     load = jnp.max(spread(jnp.max(heard[:, slabs:]).reshape(1), "slab"))
-    fits = (load <= FEW) & (jnp.max(global_rank) < FEW_ROWS)
+    choice = jnp.sum((load > jnp.array(FEW)).astype(jnp.int32))
+    choice = jnp.where(jnp.max(global_rank) < FEW_ROWS, choice, len(FEW))
 
     partial_grad = lax.dot_general(
         output_grad, out_weight, (((1,), (1,)), ((), ())), preferred_element_type=f32
@@ -324,9 +326,9 @@
     order = (head - jnp.arange(heads)) % heads
     weight_rows = out_weight.reshape(heads, columns, -1).at[order].get(mode="promise_in_bounds")
     weight_rows = weight_rows.reshape(out_weight.shape)
-    beside = (lane_blocks, asked, fits, grad_att, left, right, weight_rows)
+    beside = (lane_blocks, asked, choice, grad_att, left, right, weight_rows)
     beside = lax.optimization_barrier(beside + (global_lane, global_rank, global_block, global_row))
-    lane_blocks, asked, fits, grad_att, left, right, weight_rows = beside[:7]
+    lane_blocks, asked, choice, grad_att, left, right, weight_rows = beside[:7]
     global_lane, global_rank, global_block, global_row = beside[7:]
     place = jnp.stack([position * blocks, seq_count * blocks - 1]).astype(jnp.int32)
     padded = tokens + PAIR
@@ -409,10 +411,10 @@
             lane_grads,
         )
 
-    few = lambda: middle(FEW, FEW_ROWS)
-    all_slots = lambda: middle(slabs, GLOBALS)
+    branches = [functools.partial(middle, slots, FEW_ROWS) for slots in FEW]
+    branches.append(functools.partial(middle, slabs, GLOBALS))
     everywhere, query_grad, key_part, value_part, from_left, from_right, weight_part, lane_grads = (
-        lax.cond(fits, few, all_slots) if FEW < slabs else all_slots()
+        lax.switch(choice, branches)
     )
     others = lax.psum_scatter(lane_grads, "slab", scatter_dimension=0, tiled=True)
 

time: 283 us -> 276 us (0.975)
  waiting for transfers between devices: 99.8 us -> 91.5 us
    all_to_all x6, waiting for transfers between devices: 59.4 us -> 54.4 us  [exchange(): return lax.all_to_all(array, axis, split_axis=0, concat_axis=0, tiled=True)]
    ppermute x1, waiting for transfers between devices: 9.13 us -> 5.76 us  [middle(): from_left = lax.ppermute(rims[1], seq, forth)]
  transfers between devices with their start and end apart: 18 -> 18, of which waited for: 11 -> 11; matrix products, arithmetic and copies ran while one was open for 8% -> 9% of each run, Pallas kernels for 0% -> 0%
where the time goes in v7:
time: 276 us; the launch traced here: 273 us
  waiting for transfers between devices  91.5 us (33%)
  starting transfers between devices  81.6 us (30%)
  blocking collectives  34.3 us (12%)
  Pallas kernels  20.1 us (7%)
  between operations  16.4 us (6%)
  local copies, waits for them, and re-layouts  14.1 us (5%)
  other arithmetic  8.91 us (3%)
  matrix products  5.67 us (2%)
    all_to_all x6, waiting for transfers between devices, exchange(): return lax.all_to_all(array, axis, split_axis=0, concat_axis=0, tiled=True)  54.4 us
    all_to_all x6, starting transfers between devices, exchange(): return lax.all_to_all(array, axis, split_axis=0, concat_axis=0, tiled=True)  48.4 us
    all_to_all x2, blocking collectives, exchange(): return lax.all_to_all(array, axis, split_axis=0, concat_axis=0, tiled=True)  34.3 us
    all_gather x1, waiting for transfers between devices, shards(): lane_blocks = lax.all_gather(own, 'slab', axis=0, tiled=True)  18.3 us
    ppermute x3, waiting for transfers between devices, shards(): other = lax.ppermute(other, 'lane', [(i, i ^ step) for i in range(LANES)])  10.9 us
    ppermute x3, starting transfers between devices, shards(): other = lax.ppermute(other, 'lane', [(i, i ^ step) for i in range(LANES)])  10.8 us
    ppermute x3, starting transfers between devices, middle(): lax.ppermute(attended, 'head', [(i, (i + k) % heads) for i in range(heads)])  10.7 us
    pallas_call x1, Pallas kernels, middle(): call(attention_kernel, (shape((tokens, columns), bf16), shape((tokens, co...  8.33 us
  transfers between devices with their start and end apart: 18, of which 11 were waited for; matrix products, arithmetic and copies ran while one was open for 9% of the time, Pallas kernels for 0%

profile of v7, /device:TPU:1, one launch (start us, length us, event | category | flops | bytes accessed | tf_op | source)
XLA Modules:
  0.0 272.7 jit_solution(3976942302259534887)
XLA Ops:
  7.2 1.8 pad_maximum_fusion
  9.0 0.8 copy.41
  9.9 0.2 convert_reduce_fusion.1
  10.1 0.6 fusion.13
  11.5 0.6 concatenate.19
  12.1 10.1 %all-to-all-start.8 = ((s32[8,1,17]{2,1,0:T(1,128)}), s32[8,1,17]{2,1,0:T(1,128)S(1)}, u32[]{:S(2)}, u32[]{:S(2)}) async-start(s32[8,1,17]{2,1,0:T(1,128)} %bitcast.15), calls=%async_computation.8 | async-start | bytes 8192 | tf_op jit(solution)/shard_map/all_to_all | solution.py:268
  22.2 0.8 fusion.4
  23.0 3.5 %collective-permute-start.20 = (bf16[128,128]{1,0:T(8,128)(2,1)S(1)}, bf16[128,128]{1,0:T(8,128)(2,1)S(1)}, u32[]{:S(2)}, u32[]{:S(2)}) collective-permute-start(bf16[128,128]{1,0:T(8,128)(2,1)S(1)} %get-tuple-element.296), channel_id=1, source_target_pairs={{0,4},{4,8},{8,12},{12,16},{16,20},{20,24},{24,28},{28,32},{32,36}... | collective-permute-start | bytes 98312 | tf_op jit(solution)/shard_map/ppermute | solution.py:323
  26.6 1.9 collective-permute-start.21
  28.5 1.3 convolution_bitcast_fusion
  29.9 1.1 copy.48
  31.0 0.7 slice_reduce_fusion
  31.7 1.2 broadcast_in_dim.62
  33.0 10.8 %all-to-all-start.9 = ((s32[16,1,1]{2,1,0:T(1,128)}), s32[16,1,1]{2,1,0:T(1,128)S(1)}, u32[]{:S(2)}, u32[]{:S(2)}) async-start(s32[16,1,1]{2,1,0:T(1,128)} %broadcast_in_dim.62), calls=%async_computation.9 | async-start | bytes 16384 | tf_op jit(solution)/shard_map/all_to_all | solution.py:268
  43.8 11.3 %all-to-all-done.9 = s32[16,1,1]{2,1,0:T(1,128)S(1)} async-done(((s32[16,1,1]{2,1,0:T(1,128)}), s32[16,1,1]{2,1,0:T(1,128)S(1)}, u32[]{:S(2)}, u32[]{:S(2)}) %all-to-all-start.9) | async-done | bytes 96 | tf_op jit(solution)/shard_map/all_to_all | solution.py:268
  55.0 4.0 %all-to-all-start.10 = ((f32[4,576,128]{2,1,0:T(8,128)}), f32[4,576,128]{2,1,0:T(8,128)S(1)}, u32[]{:S(2)}, u32[]{:S(2)}) async-start(f32[4,576,128]{2,1,0:T(8,128)} %bitcast.70), calls=%async_computation.10 | async-start | bytes 2359296 | tf_op jit(solution)/shard_map/all_to_all | solution.py:268
  59.1 0.2 convert_reduce_fusion
  59.3 0.6 reduce_max.65
  60.6 1.3 gather_fusion
  61.9 0.1 select_reduce_fusion
  62.1 0.7 reduce_max.67
  62.8 1.3 fusion.8
  64.7 5.4 %all-to-all-done.10 = f32[4,576,128]{2,1,0:T(8,128)S(1)} async-done(((f32[4,576,128]{2,1,0:T(8,128)}), f32[4,576,128]{2,1,0:T(8,128)S(1)}, u32[]{:S(2)}, u32[]{:S(2)}) %all-to-all-start.10) | async-done | bytes 1179680 | tf_op jit(solution)/shard_map/all_to_all | solution.py:268
  70.2 18.3 %all-gather.2.cloned.1.call-done = bf16[144,128,128]{2,1,0:T(8,128)(2,1)} async-done(((bf16[9,128,128]{2,1,0:T(8,128)(2,1)}), bf16[144,128,128]{2,1,0:T(8,128)(2,1)}) %all-gather.2.cloned.1.call-update) | async-done | bytes 4718608 | tf_op jit(solution)/shard_map/all_gather | solution.py:288
  88.4 97.9 %conditional.1 = (bf16[576,512]{1,0:T(8,128)(2,1)}, bf16[576,128]{1,0:T(8,128)(2,1)}, f32[704,128]{1,0:T(8,128)}, f32[704,128]{1,0:T(8,128)}, bf16[128,128]{1,0:...) conditional(s32[]{:T(128)} %clamp.3, (s32[128]{0:T(128)S(1)}, ...), branch_computations={%region_11.12_spmd, %region_12.13_spmd, %region_13.14_spmd, %regio... | conditional | flops 1224868096 | bytes 102272792 | solution.py:417
  88.5 4.8 %branch_1_fun.3 = bf16[8,1216,128]{2,1,0:T(8,128)(2,1)} custom-call(s32[128]{0:T(128)S(1)} %get-tuple-element.165.asked, s32[128]{0:T(128)S(1)} %get-tuple-element.166.global_block, s32[128]{0:T(128)S(1)} %get-tuple-element.167.global_row, bf16[144,128,128]{2,1,0:T(8,128)(2,1)} %get-tuple-element.168.lane_blocks), custom_call_target="tpu_custom_call" | custom-call | bytes 8388608 | tf_op jit(solution)/shard_map/cond/branch_1_fun/pallas_call | solution.py:339
  93.4 12.5 %all-to-all-start.2 = ((bf16[8,1216,128]{2,1,0:T(8,128)(2,1)}), bf16[8,1216,128]{2,1,0:T(8,128)(2,1)S(1)}, u32[]{:S(2)}, u32[]{:S(2)}) async-start(bf16[8,1216,128]{2,1,0:T(8,128)(2,1)} %branch_1_fun.3), calls=%async_computation.2 | async-start | bytes 4980736 | tf_op jit(solution)/shard_map/cond/branch_1_fun/all_to_all | solution.py:268
  105.9 0.7 add_bitcast_fusion.1
  106.5 0.1 copy.38.global_place
  106.7 29.8 %all-to-all-done.2.arrived = bf16[8,1216,128]{2,1,0:T(8,128)(2,1)S(1)} async-done(((bf16[8,1216,128]{2,1,0:T(8,128)(2,1)}), bf16[8,1216,128]{2,1,0:T(8,128)(2,1)S(1)}, u32[]{:S(2)}, u32[]{:S(2)}) %all-to-all-start.2) | async-done | bytes 2490400 | tf_op jit(solution)/shard_map/cond/branch_1_fun/all_to_all | solution.py:268
  136.4 8.3 %branch_1_fun.4 = (bf16[576,128]{1,0:T(8,128)(2,1)S(1)}, bf16[576,128]{1,0:T(8,128)(2,1)}, f32[704,128]{1,0:T(8,128)}, f32[704,128]{1,0:T(8,128)}, bf16[2,128,12...) custom-call(s32[2]{0:T(128)S(1)} %get-tuple-element.154.place, s32[27]{0:T(128)S(1)} %copy-done.22, ...), custom_call_target="tpu_custom_call" | custom-call | flops 1073741824 | bytes 12582912 | tf_op jit(solution)/shard_map/cond/branch_1_fun/pallas_call | solution.py:347
  144.7 1.5 copy-done.5
  146.2 4.5 %all-to-all-start.3 = ((bf16[8,1216,128]{2,1,0:T(8,128)(2,1)}), bf16[8,1216,128]{2,1,0:T(8,128)(2,1)S(1)}, u32[]{:S(2)}, u32[]{:S(2)}) async-start(bf16[8,1216,128]{2,1,0:T(8,128)(2,1)} %copy-done.5), calls=%async_computation.3 | async-start | bytes 4980736 | tf_op jit(solution)/shard_map/cond/branch_1_fun/all_to_all | solution.py:268
  150.7 3.1 %collective-permute-start.5 = (bf16[576,128]{1,0:T(8,128)(2,1)S(1)}, bf16[576,128]{1,0:T(8,128)(2,1)S(1)}, u32[]{:S(2)}, u32[]{:S(2)}) collective-permute-start(bf16[576,128]{1,0:T(8,128)(2,1)S(1)} %get-tuple-element.169), channel_id=1, source_target_pairs={{0,1},{1,2},{2,3},{3,0},{4,5},{5,6},{6,7},{7,4},{8,9},{9,10},{10,1... | collective-permute-start | bytes 442376 | tf_op jit(solution)/shard_map/cond/branch_1_fun/ppermute | solution.py:381
  153.9 4.4 %collective-permute-start.6 = (bf16[576,128]{1,0:T(8,128)(2,1)S(1)}, bf16[576,128]{1,0:T(8,128)(2,1)S(1)}, u32[]{:S(2)}, u32[]{:S(2)}) collective-permute-start(bf16[576,128]{1,0:T(8,128)(2,1)S(1)} %get-tuple-element.169), channel_id=1, source_target_pairs={{0,2},{1,3},{2,0},{3,1},{4,6},{5,7},{6,4},{7,5},{8,10},{9,11},{10,... | collective-permute-start | bytes 442376 | tf_op jit(solution)/shard_map/cond/branch_1_fun/ppermute | solution.py:381
  158.2 3.2 %collective-permute-start.7 = (bf16[576,128]{1,0:T(8,128)(2,1)S(1)}, bf16[576,128]{1,0:T(8,128)(2,1)S(1)}, u32[]{:S(2)}, u32[]{:S(2)}) collective-permute-start(bf16[576,128]{1,0:T(8,128)(2,1)S(1)} %get-tuple-element.169), channel_id=1, source_target_pairs={{0,3},{1,0},{2,1},{3,2},{4,7},{5,4},{6,5},{7,6},{8,11},{9,8},{10,9... | collective-permute-start | bytes 442376 | tf_op jit(solution)/shard_map/cond/branch_1_fun/ppermute | solution.py:381
  161.5 0.7 constant_dynamic-update-slice_fusion.7
  162.2 4.4 %collective-permute-start.8 = (bf16[128,128]{1,0:T(8,128)(2,1)S(1)}, bf16[128,128]{1,0:T(8,128)(2,1)}, u32[]{:S(2)}, u32[]{:S(2)}) collective-permute-start(bf16[128,128]{1,0:T(8,128)(2,1)S(1)} %get-tuple-element.290), channel_id=1, source_target_pairs={{0,4},{4,8},{8,12},{12,16},{16,20},{20,24},{24,28},{28,32},{32,36}... | collective-permute-start | bytes 98312 | tf_op jit(solution)/shard_map/cond/branch_1_fun/ppermute | solution.py:384
  166.5 1.9 collective-permute-start.9
  168.5 0.7 constant_dynamic-update-slice_fusion.6
  169.2 0.7 constant_dynamic-update-slice_fusion.5
  169.9 0.7 constant_dynamic-update-slice_fusion.4
  170.6 2.3 convolution_multiply_fusion.1
  172.8 5.8 %collective-permute-done.8 = bf16[128,128]{1,0:T(8,128)(2,1)} collective-permute-done((bf16[128,128]{1,0:T(8,128)(2,1)S(1)}, bf16[128,128]{1,0:T(8,128)(2,1)}, u32[]{:S(2)}, u32[]{:S(2)}) %collective-permute-start.8) | collective-permute-done | bytes 32800 | tf_op jit(solution)/shard_map/cond/branch_1_fun/ppermute | solution.py:384
  178.6 2.1 collective-permute-done.9
  180.7 0.6 all-to-all-done.3.returned
  181.3 5.0 %branch_1_fun.5 = bf16[144,128,128]{2,1,0:T(8,128)(2,1)} custom-call(s32[128]{0:T(128)S(1)} %get-tuple-element.165.asked, s32[128]{0:T(128)S(1)} %get-tuple-element.166.global_block, s32[128]{0:T(128)S(1)} %get-tuple-element.167.global_row, bf16[8,1216,128]{2,1,0:T(8,128)(2,1)S(1)} %all-to-all-done.3.returned), custom_call_target="tpu_custom_call" | custom-call | bytes 10485760 | tf_op jit(solution)/shard_map/cond/branch_1_fun/pallas_call | solution.py:393
  186.4 1.0 dynamic-slice_bitcast_fusion
  187.4 3.5 %collective-permute-start.22 = (f32[4,64,256]{2,1,0:T(8,128)S(1)}, f32[4,64,256]{2,1,0:T(8,128)S(1)}, u32[]{:S(2)}, u32[]{:S(2)}) collective-permute-start(f32[4,64,256]{2,1,0:T(8,128)S(1)} %dynamic-slice_bitcast_fusion), channel_id=1, source_target_pairs={{0,16},{4,20},{8,24},{12,28},{16,0},{20,4},{24,8},{28,12},{1,17},{... | collective-permute-start | bytes 786440 | tf_op jit(solution)/shard_map/ppermute | solution.py:428
  191.0 6.5 %collective-permute-done.22 = f32[4,64,256]{2,1,0:T(8,128)S(1)} collective-permute-done((f32[4,64,256]{2,1,0:T(8,128)S(1)}, f32[4,64,256]{2,1,0:T(8,128)S(1)}, u32[]{:S(2)}, u32[]{:S(2)}) %collective-permute-start.22) | collective-permute-done | bytes 262176 | tf_op jit(solution)/shard_map/ppermute | solution.py:428
  197.4 1.0 bitcast_add_fusion
  198.4 2.5 collective-permute-start.23
  201.0 3.6 %collective-permute-done.23 = f32[2,64,256]{2,1,0:T(8,128)S(1)} collective-permute-done((f32[2,64,256]{2,1,0:T(8,128)S(1)}, f32[2,64,256]{2,1,0:T(8,128)S(1)}, u32[]{:S(2)}, u32[]{:S(2)}) %collective-permute-start.23) | collective-permute-done | bytes 131104 | tf_op jit(solution)/shard_map/ppermute | solution.py:428
  204.6 4.8 %collective-permute-start.24 = (f32[1,64,256]{2,1,0:T(8,128)S(1)}, f32[1,64,256]{2,1,0:T(8,128)S(1)}, u32[]{:S(2)}, u32[]{:S(2)}) collective-permute-start(f32[1,64,256]{2,1,0:T(8,128)S(1)} %constant_dynamic-slice_fusion), channel_id=1, source_target_pairs={{0,4},{4,0},{8,12},{12,8},{16,20},{20,16},{24,28},{28,24},{1,5},{5... | collective-permute-start | bytes 196616 | tf_op jit(solution)/shard_map/ppermute | solution.py:428
  209.4 0.9 collective-permute-done.24
  210.3 18.1 %all_to_all.70 = f32[16,4,256]{2,1,0:T(4,128)S(1)} all-to-all(f32[16,4,256]{2,1,0:T(4,128)S(1)} %reshape.233), channel_id=1, replica_groups=mesh['slab'=16,'lane'=8,'head'=4] {'slab'}, dimensions={0} | all-to-all | bytes 131072 | tf_op jit(solution)/shard_map/all_to_all | solution.py:268
  228.5 16.2 %all_to_all.71 = f32[16,4,256]{2,1,0:T(4,128)S(1)} all-to-all(f32[16,4,256]{2,1,0:T(4,128)S(1)} %broadcast_in_dim.67), channel_id=1, replica_groups=mesh['slab'=16,'lane'=8,'head'=4] {'slab'}, dimensions={0} | all-to-all | bytes 131072 | tf_op jit(solution)/shard_map/all_to_all | solution.py:268
  244.7 0.8 broadcast_in_dim.68
  245.6 6.4 %all-to-all-start.13 = ((f32[8,64,256]{2,1,0:T(8,128)}), f32[8,64,256]{2,1,0:T(8,128)S(1)}, u32[]{:S(2)}, u32[]{:S(2)}) async-start(f32[8,64,256]{2,1,0:T(8,128)} %broadcast_in_dim.68), calls=%async_computation.14 | async-start | bytes 1048576 | tf_op jit(solution)/shard_map/all_to_all | solution.py:268
  252.0 2.1 convolution_convert_fusion
  254.1 7.4 %all-to-all-done.13 = f32[8,64,256]{2,1,0:T(8,128)S(1)} async-done(((f32[8,64,256]{2,1,0:T(8,128)}), f32[8,64,256]{2,1,0:T(8,128)S(1)}, u32[]{:S(2)}, u32[]{:S(2)}) %all-to-all-start.13) | async-done | bytes 524320 | tf_op jit(solution)/shard_map/all_to_all | solution.py:268
  261.5 1.5 gather_fusion.1
  263.0 1.0 copy-done.7
  264.0 1.9 shard_map.119
  (69 shorter events, 0.9 us)
Async XLA Ops:
  7.2 21.3 %copy-start = (bf16[512,256]{1,0:T(8,128)(2,1)S(1)}, bf16[512,256]{1,0:T(8,128)(2,1)}, u32[]{:S(2)}) copy-start(bf16[512,256]{1,0:T(8,128)(2,1)} %param.15) | copy-start | bytes 786436
  7.2 22.6 %copy-start.32 = (s32[128]{0:T(128)S(1)}, s32[128]{0:T(128)}, u32[]{:S(2)}) copy-start(s32[128]{0:T(128)} %param.18) | copy-start | bytes 1540
  7.2 81.2 %all-gather.2.cloned.1.call-start = ((), (), s32[]{:S(2)}) async-start(), calls=%async_computation.15 | async-start | bytes 5013504 | tf_op jit(solution)/shard_map/all_gather | solution.py:288
  9.9 18.6 %copy-start.20 = (s32[27]{0:T(128)}, s32[27]{0:T(128)S(1)}, u32[]{:S(2)}) copy-start(s32[27]{0:T(128)S(1)} %reshape.226) | copy-start | bytes 328
  10.1 0.6 copy-start.25
  12.1 18.9 %all-to-all-start.8 = ((s32[8,1,17]{2,1,0:T(1,128)}), s32[8,1,17]{2,1,0:T(1,128)S(1)}, u32[]{:S(2)}, u32[]{:S(2)}) async-start(s32[8,1,17]{2,1,0:T(1,128)} %bitcast.15), calls=%async_computation.8 | async-start | bytes 8192 | tf_op jit(solution)/shard_map/all_to_all | solution.py:268
  23.0 47.1 %collective-permute-start.20 = (bf16[128,128]{1,0:T(8,128)(2,1)S(1)}, bf16[128,128]{1,0:T(8,128)(2,1)S(1)}, u32[]{:S(2)}, u32[]{:S(2)}) collective-permute-start(bf16[128,128]{1,0:T(8,128)(2,1)S(1)} %get-tuple-element.296), channel_id=1, source_target_pairs={{0,4},{4,8},{8,12},{12,16},{16,20},{20,24},{24,28},{28,32},{32,36}... | collective-permute-start | bytes 98312 | tf_op jit(solution)/shard_map/ppermute | solution.py:323
  26.6 43.6 %collective-permute-start.21 = (bf16[128,128]{1,0:T(8,128)(2,1)S(1)}, bf16[128,128]{1,0:T(8,128)(2,1)S(1)}, u32[]{:S(2)}, u32[]{:S(2)}) collective-permute-start(bf16[128,128]{1,0:T(8,128)(2,1)S(1)} %get-tuple-element.295), channel_id=1, source_target_pairs={{4,0},{8,4},{12,8},{16,12},{20,16},{24,20},{28,24},{32,28},{36,32}... | collective-permute-start | bytes 98312 | tf_op jit(solution)/shard_map/ppermute | solution.py:324
  29.8 33.0 %copy-start.37 = (s32[3]{0:T(128)S(1)}, s32[3]{0:T(128)}, u32[]{:S(2)}) copy-start(s32[3]{0:T(128)} %constant.223.clone) | copy-start | bytes 40
  29.9 58.6 %copy-start.8 = (bf16[576,128]{1,0:T(8,128)(2,1)S(1)}, bf16[576,128]{1,0:T(8,128)(2,1)}, u32[]{:S(2)}) copy-start(bf16[576,128]{1,0:T(8,128)(2,1)} %param.14) | copy-start | bytes 442372
  29.9 58.5 %copy-start.9 = (bf16[576,128]{1,0:T(8,128)(2,1)S(1)}, bf16[576,128]{1,0:T(8,128)(2,1)}, u32[]{:S(2)}) copy-start(bf16[576,128]{1,0:T(8,128)(2,1)} %param.13) | copy-start | bytes 442372
  29.9 58.5 %copy-start.11 = (bf16[576,256]{1,0:T(8,128)(2,1)S(1)}, bf16[576,256]{1,0:T(8,128)(2,1)}, u32[]{:S(2)}) copy-start(bf16[576,256]{1,0:T(8,128)(2,1)} %param.16) | copy-start | bytes 884740
  29.9 58.5 %copy-start.16 = (bf16[576,128]{1,0:T(8,128)(2,1)S(1)}, bf16[576,128]{1,0:T(8,128)(2,1)}, u32[]{:S(2)}) copy-start(bf16[576,128]{1,0:T(8,128)(2,1)} %param.12) | copy-start | bytes 442372
  33.0 22.1 %all-to-all-start.9 = ((s32[16,1,1]{2,1,0:T(1,128)}), s32[16,1,1]{2,1,0:T(1,128)S(1)}, u32[]{:S(2)}, u32[]{:S(2)}) async-start(s32[16,1,1]{2,1,0:T(1,128)} %broadcast_in_dim.62), calls=%async_computation.9 | async-start | bytes 16384 | tf_op jit(solution)/shard_map/all_to_all | solution.py:268
  55.0 15.0 %all-to-all-start.10 = ((f32[4,576,128]{2,1,0:T(8,128)}), f32[4,576,128]{2,1,0:T(8,128)S(1)}, u32[]{:S(2)}, u32[]{:S(2)}) async-start(f32[4,576,128]{2,1,0:T(8,128)} %bitcast.70), calls=%async_computation.10 | async-start | bytes 2359296 | tf_op jit(solution)/shard_map/all_to_all | solution.py:268
  59.1 203.9 %reduce-scatter.2.cloned.1.call-start = ((), (), s32[]{:S(2)}) async-start(), calls=%async_computation.16 | async-start | bytes 5013504 | tf_op jit(solution)/shard_map/reduce_scatter | solution.py:419
  60.6 27.8 %copy-start.19 = (s32[1024]{0:T(1024)}, s32[1024]{0:T(1024)S(1)}, u32[]{:S(2)}) copy-start(s32[1024]{0:T(1024)S(1)} %pad_clamp_fusion) | copy-start | bytes 12292
  88.5 4.9 %copy-start.12 = (bf16[576,256]{1,0:T(8,128)(2,1)}, bf16[576,256]{1,0:T(8,128)(2,1)S(1)}, u32[]{:S(2)}) copy-start(bf16[576,256]{1,0:T(8,128)(2,1)S(1)} %get-tuple-element.175) | copy-start | bytes 884740 | tf_op jit(solution)/shard_map/cond
  88.5 4.8 %copy-start.33 = (s32[128]{0:T(128)}, s32[128]{0:T(128)S(1)}, u32[]{:S(2)}) copy-start(s32[128]{0:T(128)S(1)} %get-tuple-element.163) | copy-start | bytes 1540 | tf_op jit(solution)/shard_map/cond
  88.5 4.8 %copy-start.35 = (s32[128]{0:T(128)}, s32[128]{0:T(128)S(1)}, u32[]{:S(2)}) copy-start(s32[128]{0:T(128)S(1)} %get-tuple-element.164) | copy-start | bytes 1540 | tf_op jit(solution)/shard_map/cond
  93.3 43.1 %copy-start.22 = (s32[27]{0:T(128)S(1)}, s32[27]{0:T(128)}, u32[]{:S(2)}) copy-start(s32[27]{0:T(128)} %get-tuple-element.155.names) | copy-start | bytes 328 | tf_op jit(solution)/shard_map/cond
  93.3 43.1 %copy-start.27 = (s32[27]{0:T(128)S(1)}, s32[27]{0:T(128)}, u32[]{:S(2)}) copy-start(s32[27]{0:T(128)} %get-tuple-element.156.ranks) | copy-start | bytes 328 | tf_op jit(solution)/shard_map/cond
  93.4 43.1 %all-to-all-start.2 = ((bf16[8,1216,128]{2,1,0:T(8,128)(2,1)}), bf16[8,1216,128]{2,1,0:T(8,128)(2,1)S(1)}, u32[]{:S(2)}, u32[]{:S(2)}) async-start(bf16[8,1216,128]{2,1,0:T(8,128)(2,1)} %branch_1_fun.3), calls=%async_computation.2 | async-start | bytes 4980736 | tf_op jit(solution)/shard_map/cond/branch_1_fun/all_to_all | solution.py:268
  144.7 1.5 copy-start.5
  146.2 24.4 %copy-start.13 = (bf16[576,256]{1,0:T(8,128)(2,1)S(1)}, bf16[576,256]{1,0:T(8,128)(2,1)}, u32[]{:S(2)}) copy-start(bf16[576,256]{1,0:T(8,128)(2,1)} %copy-done.12) | copy-start | bytes 884740 | tf_op jit(solution)/shard_map/cond
  146.2 35.1 %all-to-all-start.3 = ((bf16[8,1216,128]{2,1,0:T(8,128)(2,1)}), bf16[8,1216,128]{2,1,0:T(8,128)(2,1)S(1)}, u32[]{:S(2)}, u32[]{:S(2)}) async-start(bf16[8,1216,128]{2,1,0:T(8,128)(2,1)} %copy-done.5), calls=%async_computation.3 | async-start | bytes 4980736 | tf_op jit(solution)/shard_map/cond/branch_1_fun/all_to_all | solution.py:268
  150.7 17.7 %collective-permute-start.5 = (bf16[576,128]{1,0:T(8,128)(2,1)S(1)}, bf16[576,128]{1,0:T(8,128)(2,1)S(1)}, u32[]{:S(2)}, u32[]{:S(2)}) collective-permute-start(bf16[576,128]{1,0:T(8,128)(2,1)S(1)} %get-tuple-element.169), channel_id=1, source_target_pairs={{0,1},{1,2},{2,3},{3,0},{4,5},{5,6},{6,7},{7,4},{8,9},{9,10},{10,1... | collective-permute-start | bytes 442376 | tf_op jit(solution)/shard_map/cond/branch_1_fun/ppermute | solution.py:381
  153.9 15.3 %collective-permute-start.6 = (bf16[576,128]{1,0:T(8,128)(2,1)S(1)}, bf16[576,128]{1,0:T(8,128)(2,1)S(1)}, u32[]{:S(2)}, u32[]{:S(2)}) collective-permute-start(bf16[576,128]{1,0:T(8,128)(2,1)S(1)} %get-tuple-element.169), channel_id=1, source_target_pairs={{0,2},{1,3},{2,0},{3,1},{4,6},{5,7},{6,4},{7,5},{8,10},{9,11},{10,... | collective-permute-start | bytes 442376 | tf_op jit(solution)/shard_map/cond/branch_1_fun/ppermute | solution.py:381
  158.2 11.6 %collective-permute-start.7 = (bf16[576,128]{1,0:T(8,128)(2,1)S(1)}, bf16[576,128]{1,0:T(8,128)(2,1)S(1)}, u32[]{:S(2)}, u32[]{:S(2)}) collective-permute-start(bf16[576,128]{1,0:T(8,128)(2,1)S(1)} %get-tuple-element.169), channel_id=1, source_target_pairs={{0,3},{1,0},{2,1},{3,2},{4,7},{5,4},{6,5},{7,6},{8,11},{9,8},{10,9... | collective-permute-start | bytes 442376 | tf_op jit(solution)/shard_map/cond/branch_1_fun/ppermute | solution.py:381
  162.2 16.5 %collective-permute-start.8 = (bf16[128,128]{1,0:T(8,128)(2,1)S(1)}, bf16[128,128]{1,0:T(8,128)(2,1)}, u32[]{:S(2)}, u32[]{:S(2)}) collective-permute-start(bf16[128,128]{1,0:T(8,128)(2,1)S(1)} %get-tuple-element.290), channel_id=1, source_target_pairs={{0,4},{4,8},{8,12},{12,16},{16,20},{20,24},{24,28},{28,32},{32,36}... | collective-permute-start | bytes 98312 | tf_op jit(solution)/shard_map/cond/branch_1_fun/ppermute | solution.py:384
  166.5 14.2 %collective-permute-start.9 = (bf16[128,128]{1,0:T(8,128)(2,1)S(1)}, bf16[128,128]{1,0:T(8,128)(2,1)}, u32[]{:S(2)}, u32[]{:S(2)}) collective-permute-start(bf16[128,128]{1,0:T(8,128)(2,1)S(1)} %get-tuple-element.289), channel_id=1, source_target_pairs={{4,0},{8,4},{12,8},{16,12},{20,16},{24,20},{28,24},{32,28},{36,32}... | collective-permute-start | bytes 98312 | tf_op jit(solution)/shard_map/cond/branch_1_fun/ppermute | solution.py:385
  186.4 65.6 %copy-start.10 = (bf16[4,128,256]{2,1,0:T(8,128)(2,1)S(1)}, bf16[4,128,256]{2,1,0:T(8,128)(2,1)}, u32[]{:S(2)}) copy-start(bf16[4,128,256]{2,1,0:T(8,128)(2,1)} %gather_fusion) | copy-start | bytes 786436
  187.4 10.0 %collective-permute-start.22 = (f32[4,64,256]{2,1,0:T(8,128)S(1)}, f32[4,64,256]{2,1,0:T(8,128)S(1)}, u32[]{:S(2)}, u32[]{:S(2)}) collective-permute-start(f32[4,64,256]{2,1,0:T(8,128)S(1)} %dynamic-slice_bitcast_fusion), channel_id=1, source_target_pairs={{0,16},{4,20},{8,24},{12,28},{16,0},{20,4},{24,8},{28,12},{1,17},{... | collective-permute-start | bytes 786440 | tf_op jit(solution)/shard_map/ppermute | solution.py:428
  198.4 6.1 %collective-permute-start.23 = (f32[2,64,256]{2,1,0:T(8,128)S(1)}, f32[2,64,256]{2,1,0:T(8,128)S(1)}, u32[]{:S(2)}, u32[]{:S(2)}) collective-permute-start(f32[2,64,256]{2,1,0:T(8,128)S(1)} %dynamic-slice_bitcast_fusion.1), channel_id=1, source_target_pairs={{0,8},{4,12},{8,0},{12,4},{16,24},{20,28},{24,16},{28,20},{1,9},{5... | collective-permute-start | bytes 393224 | tf_op jit(solution)/shard_map/ppermute | solution.py:428
  204.6 5.7 %collective-permute-start.24 = (f32[1,64,256]{2,1,0:T(8,128)S(1)}, f32[1,64,256]{2,1,0:T(8,128)S(1)}, u32[]{:S(2)}, u32[]{:S(2)}) collective-permute-start(f32[1,64,256]{2,1,0:T(8,128)S(1)} %constant_dynamic-slice_fusion), channel_id=1, source_target_pairs={{0,4},{4,0},{8,12},{12,8},{16,20},{20,16},{24,28},{28,24},{1,5},{5... | collective-permute-start | bytes 196616 | tf_op jit(solution)/shard_map/ppermute | solution.py:428
  210.3 55.6 %copy-start.1 = (bf16[512,256]{1,0:T(8,128)(2,1)S(1)}, bf16[512,256]{1,0:T(8,128)(2,1)}, u32[]{:S(2)}) copy-start(bf16[512,256]{1,0:T(8,128)(2,1)} %param.15) | copy-start | bytes 786436
  245.6 15.9 %all-to-all-start.13 = ((f32[8,64,256]{2,1,0:T(8,128)}), f32[8,64,256]{2,1,0:T(8,128)S(1)}, u32[]{:S(2)}, u32[]{:S(2)}) async-start(f32[8,64,256]{2,1,0:T(8,128)} %broadcast_in_dim.68), calls=%async_computation.14 | async-start | bytes 1048576 | tf_op jit(solution)/shard_map/all_to_all | solution.py:268
  263.0 1.0 copy-start.7
Sparse Core Ops, SparseCore 0:
  10.7 77.6 all-gather.1
  186.5 71.9 reduce-scatter.1

commit v8 on v7

--- a/solution.py
+++ b/solution.py
@@ -185,7 +185,7 @@
             send[a, pl.ds(b + BLOCK, BLOCK), :] = dv[first : first + BLOCK].astype(bf16)
         return carry
 
-    lax.fori_loop(0, blocks, one, 0, unroll=R)
+    lax.fori_loop(0, blocks, one, 0, unroll=True)
     for side, rows in enumerate((pl.ds(0, BLOCK), pl.ds(BLOCK + tokens, BLOCK))):
         rims[side, :BLOCK, :] = key_grad[rows, :].astype(bf16)
         rims[side, BLOCK:, :] = value_grad[rows, :].astype(bf16)

time: 276 us -> 279 us (1.011)
  the two profiles are of different devices: /device:TPU:1 before, /device:TPU:14 now
where the time goes in v8:
time: 279 us; the launch traced here: 275 us
  waiting for transfers between devices  105 us (38%)
  starting transfers between devices  68.3 us (24%)
  blocking collectives  36.9 us (13%)
  Pallas kernels  19.6 us (7%)
  between operations  16.4 us (6%)
  local copies, waits for them, and re-layouts  14.1 us (5%)
  other arithmetic  8.91 us (3%)
  matrix products  5.66 us (2%)
    all_to_all x6, waiting for transfers between devices, exchange(): return lax.all_to_all(array, axis, split_axis=0, concat_axis=0, tiled=True)  57 us
    all_to_all x6, starting transfers between devices, exchange(): return lax.all_to_all(array, axis, split_axis=0, concat_axis=0, tiled=True)  39.8 us
    all_to_all x2, blocking collectives, exchange(): return lax.all_to_all(array, axis, split_axis=0, concat_axis=0, tiled=True)  36.9 us
    all_gather x1, waiting for transfers between devices, shards(): lane_blocks = lax.all_gather(own, 'slab', axis=0, tiled=True)  21.8 us
    ppermute x3, waiting for transfers between devices, shards(): other = lax.ppermute(other, 'lane', [(i, i ^ step) for i in range(LANES)])  12.6 us
    ppermute x1, waiting for transfers between devices, middle(): from_left = lax.ppermute(rims[1], seq, forth)  9.28 us
    ppermute x3, starting transfers between devices, middle(): lax.ppermute(attended, 'head', [(i, (i + k) % heads) for i in range(heads)])  8.8 us
    ppermute x3, starting transfers between devices, shards(): other = lax.ppermute(other, 'lane', [(i, i ^ step) for i in range(LANES)])  8.58 us
  transfers between devices with their start and end apart: 18, of which 11 were waited for; matrix products, arithmetic and copies ran while one was open for 9% of the time, Pallas kernels for 0%

profile of v8, /device:TPU:14, one launch (start us, length us, event | category | flops | bytes accessed | tf_op | source)
XLA Modules:
  0.0 274.6 jit_solution(4573359582059341250)
XLA Ops:
  7.2 1.8 pad_maximum_fusion
  9.0 0.8 copy.41
  9.9 0.2 convert_reduce_fusion.1
  10.1 0.6 fusion.13
  11.5 0.6 concatenate.19
  12.1 4.9 %all-to-all-start.8 = ((s32[8,1,17]{2,1,0:T(1,128)}), s32[8,1,17]{2,1,0:T(1,128)S(1)}, u32[]{:S(2)}, u32[]{:S(2)}) async-start(s32[8,1,17]{2,1,0:T(1,128)} %bitcast.15), calls=%async_computation.8 | async-start | bytes 8192 | tf_op jit(solution)/shard_map/all_to_all | solution.py:268
  17.1 0.8 fusion.4
  17.8 2.0 collective-permute-start.20
  19.9 3.5 %collective-permute-start.21 = (bf16[128,128]{1,0:T(8,128)(2,1)S(1)}, bf16[128,128]{1,0:T(8,128)(2,1)S(1)}, u32[]{:S(2)}, u32[]{:S(2)}) collective-permute-start(bf16[128,128]{1,0:T(8,128)(2,1)S(1)} %get-tuple-element.295), channel_id=1, source_target_pairs={{4,0},{8,4},{12,8},{16,12},{20,16},{24,20},{28,24},{32,28},{36,32}... | collective-permute-start | bytes 98312 | tf_op jit(solution)/shard_map/ppermute | solution.py:324
  23.4 1.3 convolution_bitcast_fusion
  24.8 1.1 copy.48
  25.9 0.7 slice_reduce_fusion
  26.6 1.2 broadcast_in_dim.62
  27.9 15.2 %all-to-all-start.9 = ((s32[16,1,1]{2,1,0:T(1,128)}), s32[16,1,1]{2,1,0:T(1,128)S(1)}, u32[]{:S(2)}, u32[]{:S(2)}) async-start(s32[16,1,1]{2,1,0:T(1,128)} %broadcast_in_dim.62), calls=%async_computation.9 | async-start | bytes 16384 | tf_op jit(solution)/shard_map/all_to_all | solution.py:268
  43.1 12.4 %all-to-all-done.9 = s32[16,1,1]{2,1,0:T(1,128)S(1)} async-done(((s32[16,1,1]{2,1,0:T(1,128)}), s32[16,1,1]{2,1,0:T(1,128)S(1)}, u32[]{:S(2)}, u32[]{:S(2)}) %all-to-all-start.9) | async-done | bytes 96 | tf_op jit(solution)/shard_map/all_to_all | solution.py:268
  55.5 4.8 %all-to-all-start.10 = ((f32[4,576,128]{2,1,0:T(8,128)}), f32[4,576,128]{2,1,0:T(8,128)S(1)}, u32[]{:S(2)}, u32[]{:S(2)}) async-start(f32[4,576,128]{2,1,0:T(8,128)} %bitcast.70), calls=%async_computation.10 | async-start | bytes 2359296 | tf_op jit(solution)/shard_map/all_to_all | solution.py:268
  60.3 0.2 convert_reduce_fusion
  60.5 0.6 reduce_max.65
  61.8 1.3 gather_fusion
  63.2 0.1 select_reduce_fusion
  63.4 0.7 reduce_max.67
  64.0 1.3 fusion.8
  65.9 7.4 %all-to-all-done.10 = f32[4,576,128]{2,1,0:T(8,128)S(1)} async-done(((f32[4,576,128]{2,1,0:T(8,128)}), f32[4,576,128]{2,1,0:T(8,128)S(1)}, u32[]{:S(2)}, u32[]{:S(2)}) %all-to-all-start.10) | async-done | bytes 1179680 | tf_op jit(solution)/shard_map/all_to_all | solution.py:268
  73.4 21.8 %all-gather.2.cloned.1.call-done = bf16[144,128,128]{2,1,0:T(8,128)(2,1)} async-done(((bf16[9,128,128]{2,1,0:T(8,128)(2,1)}), bf16[144,128,128]{2,1,0:T(8,128)(2,1)}) %all-gather.2.cloned.1.call-update) | async-done | bytes 4718608 | tf_op jit(solution)/shard_map/all_gather | solution.py:288
  95.2 89.2 %conditional.1 = (bf16[576,512]{1,0:T(8,128)(2,1)}, bf16[576,128]{1,0:T(8,128)(2,1)}, f32[704,128]{1,0:T(8,128)}, f32[704,128]{1,0:T(8,128)}, bf16[128,128]{1,0:...) conditional(s32[]{:T(128)} %clamp.3, (s32[128]{0:T(128)S(1)}, ...), branch_computations={%region_11.12_spmd, %region_12.13_spmd, %region_13.14_spmd, %regio... | conditional | flops 1224868096 | bytes 102272792 | solution.py:417
  95.3 4.8 %branch_1_fun.3 = bf16[8,1216,128]{2,1,0:T(8,128)(2,1)} custom-call(s32[128]{0:T(128)S(1)} %get-tuple-element.165.asked, s32[128]{0:T(128)S(1)} %get-tuple-element.166.global_block, s32[128]{0:T(128)S(1)} %get-tuple-element.167.global_row, bf16[144,128,128]{2,1,0:T(8,128)(2,1)} %get-tuple-element.168.lane_blocks), custom_call_target="tpu_custom_call" | custom-call | bytes 8388608 | tf_op jit(solution)/shard_map/cond/branch_1_fun/pallas_call | solution.py:339
  100.1 4.8 %all-to-all-start.2 = ((bf16[8,1216,128]{2,1,0:T(8,128)(2,1)}), bf16[8,1216,128]{2,1,0:T(8,128)(2,1)S(1)}, u32[]{:S(2)}, u32[]{:S(2)}) async-start(bf16[8,1216,128]{2,1,0:T(8,128)(2,1)} %branch_1_fun.3), calls=%async_computation.2 | async-start | bytes 4980736 | tf_op jit(solution)/shard_map/cond/branch_1_fun/all_to_all | solution.py:268
  104.9 0.7 add_bitcast_fusion.1
  105.5 0.1 copy.38.global_place
  105.6 29.2 %all-to-all-done.2.arrived = bf16[8,1216,128]{2,1,0:T(8,128)(2,1)S(1)} async-done(((bf16[8,1216,128]{2,1,0:T(8,128)(2,1)}), bf16[8,1216,128]{2,1,0:T(8,128)(2,1)S(1)}, u32[]{:S(2)}, u32[]{:S(2)}) %all-to-all-start.2) | async-done | bytes 2490400 | tf_op jit(solution)/shard_map/cond/branch_1_fun/all_to_all | solution.py:268
  134.8 7.9 %branch_1_fun.4 = (bf16[576,128]{1,0:T(8,128)(2,1)S(1)}, bf16[576,128]{1,0:T(8,128)(2,1)}, f32[704,128]{1,0:T(8,128)}, f32[704,128]{1,0:T(8,128)}, bf16[2,128,12...) custom-call(s32[2]{0:T(128)S(1)} %get-tuple-element.154.place, s32[27]{0:T(128)S(1)} %copy-done.22, ...), custom_call_target="tpu_custom_call" | custom-call | flops 1073741824 | bytes 12582912 | tf_op jit(solution)/shard_map/cond/branch_1_fun/pallas_call | solution.py:347
  142.7 1.5 copy-done.5
  144.2 5.1 %all-to-all-start.3 = ((bf16[8,1216,128]{2,1,0:T(8,128)(2,1)}), bf16[8,1216,128]{2,1,0:T(8,128)(2,1)S(1)}, u32[]{:S(2)}, u32[]{:S(2)}) async-start(bf16[8,1216,128]{2,1,0:T(8,128)(2,1)} %copy-done.5), calls=%async_computation.3 | async-start | bytes 4980736 | tf_op jit(solution)/shard_map/cond/branch_1_fun/all_to_all | solution.py:268
  149.3 2.4 collective-permute-start.5
  151.7 4.5 %collective-permute-start.6 = (bf16[576,128]{1,0:T(8,128)(2,1)S(1)}, bf16[576,128]{1,0:T(8,128)(2,1)S(1)}, u32[]{:S(2)}, u32[]{:S(2)}) collective-permute-start(bf16[576,128]{1,0:T(8,128)(2,1)S(1)} %get-tuple-element.169), channel_id=1, source_target_pairs={{0,2},{1,3},{2,0},{3,1},{4,6},{5,7},{6,4},{7,5},{8,10},{9,11},{10,... | collective-permute-start | bytes 442376 | tf_op jit(solution)/shard_map/cond/branch_1_fun/ppermute | solution.py:381
  156.2 1.9 collective-permute-start.7
  158.2 0.7 constant_dynamic-update-slice_fusion.7
  158.8 1.9 collective-permute-start.8
  160.8 3.6 %collective-permute-start.9 = (bf16[128,128]{1,0:T(8,128)(2,1)S(1)}, bf16[128,128]{1,0:T(8,128)(2,1)}, u32[]{:S(2)}, u32[]{:S(2)}) collective-permute-start(bf16[128,128]{1,0:T(8,128)(2,1)S(1)} %get-tuple-element.289), channel_id=1, source_target_pairs={{4,0},{8,4},{12,8},{16,12},{20,16},{24,20},{28,24},{32,28},{36,32}... | collective-permute-start | bytes 98312 | tf_op jit(solution)/shard_map/cond/branch_1_fun/ppermute | solution.py:385
  164.4 0.7 constant_dynamic-update-slice_fusion.6
  165.1 0.7 constant_dynamic-update-slice_fusion.5
  165.8 0.7 constant_dynamic-update-slice_fusion.4
  166.5 2.3 convolution_multiply_fusion.1
  168.8 9.3 %collective-permute-done.8 = bf16[128,128]{1,0:T(8,128)(2,1)} collective-permute-done((bf16[128,128]{1,0:T(8,128)(2,1)S(1)}, bf16[128,128]{1,0:T(8,128)(2,1)}, u32[]{:S(2)}, u32[]{:S(2)}) %collective-permute-start.8) | collective-permute-done | bytes 32800 | tf_op jit(solution)/shard_map/cond/branch_1_fun/ppermute | solution.py:384
  178.1 1.2 all-to-all-done.3.returned
  179.3 5.0 %branch_1_fun.5 = bf16[144,128,128]{2,1,0:T(8,128)(2,1)} custom-call(s32[128]{0:T(128)S(1)} %get-tuple-element.165.asked, s32[128]{0:T(128)S(1)} %get-tuple-element.166.global_block, s32[128]{0:T(128)S(1)} %get-tuple-element.167.global_row, bf16[8,1216,128]{2,1,0:T(8,128)(2,1)S(1)} %all-to-all-done.3.returned), custom_call_target="tpu_custom_call" | custom-call | bytes 10485760 | tf_op jit(solution)/shard_map/cond/branch_1_fun/pallas_call | solution.py:393
  184.4 1.0 dynamic-slice_bitcast_fusion
  185.4 3.3 %collective-permute-start.22 = (f32[4,64,256]{2,1,0:T(8,128)S(1)}, f32[4,64,256]{2,1,0:T(8,128)S(1)}, u32[]{:S(2)}, u32[]{:S(2)}) collective-permute-start(f32[4,64,256]{2,1,0:T(8,128)S(1)} %dynamic-slice_bitcast_fusion), channel_id=1, source_target_pairs={{0,16},{4,20},{8,24},{12,28},{16,0},{20,4},{24,8},{28,12},{1,17},{... | collective-permute-start | bytes 786440 | tf_op jit(solution)/shard_map/ppermute | solution.py:428
  188.8 7.9 %collective-permute-done.22 = f32[4,64,256]{2,1,0:T(8,128)S(1)} collective-permute-done((f32[4,64,256]{2,1,0:T(8,128)S(1)}, f32[4,64,256]{2,1,0:T(8,128)S(1)}, u32[]{:S(2)}, u32[]{:S(2)}) %collective-permute-start.22) | collective-permute-done | bytes 262176 | tf_op jit(solution)/shard_map/ppermute | solution.py:428
  196.7 1.0 bitcast_add_fusion
  197.7 3.3 %collective-permute-start.23 = (f32[2,64,256]{2,1,0:T(8,128)S(1)}, f32[2,64,256]{2,1,0:T(8,128)S(1)}, u32[]{:S(2)}, u32[]{:S(2)}) collective-permute-start(f32[2,64,256]{2,1,0:T(8,128)S(1)} %dynamic-slice_bitcast_fusion.1), channel_id=1, source_target_pairs={{0,8},{4,12},{8,0},{12,4},{16,24},{20,28},{24,16},{28,20},{1,9},{5... | collective-permute-start | bytes 393224 | tf_op jit(solution)/shard_map/ppermute | solution.py:428
  201.1 3.5 %collective-permute-done.23 = f32[2,64,256]{2,1,0:T(8,128)S(1)} collective-permute-done((f32[2,64,256]{2,1,0:T(8,128)S(1)}, f32[2,64,256]{2,1,0:T(8,128)S(1)}, u32[]{:S(2)}, u32[]{:S(2)}) %collective-permute-start.23) | collective-permute-done | bytes 131104 | tf_op jit(solution)/shard_map/ppermute | solution.py:428
  204.6 1.9 collective-permute-start.24
  206.5 1.2 collective-permute-done.24
  207.8 20.4 %all_to_all.70 = f32[16,4,256]{2,1,0:T(4,128)S(1)} all-to-all(f32[16,4,256]{2,1,0:T(4,128)S(1)} %reshape.233), channel_id=1, replica_groups=mesh['slab'=16,'lane'=8,'head'=4] {'slab'}, dimensions={0} | all-to-all | bytes 131072 | tf_op jit(solution)/shard_map/all_to_all | solution.py:268
  228.3 16.5 %all_to_all.71 = f32[16,4,256]{2,1,0:T(4,128)S(1)} all-to-all(f32[16,4,256]{2,1,0:T(4,128)S(1)} %broadcast_in_dim.67), channel_id=1, replica_groups=mesh['slab'=16,'lane'=8,'head'=4] {'slab'}, dimensions={0} | all-to-all | bytes 131072 | tf_op jit(solution)/shard_map/all_to_all | solution.py:268
  244.8 0.8 broadcast_in_dim.68
  245.6 5.0 %all-to-all-start.13 = ((f32[8,64,256]{2,1,0:T(8,128)}), f32[8,64,256]{2,1,0:T(8,128)S(1)}, u32[]{:S(2)}, u32[]{:S(2)}) async-start(f32[8,64,256]{2,1,0:T(8,128)} %broadcast_in_dim.68), calls=%async_computation.14 | async-start | bytes 1048576 | tf_op jit(solution)/shard_map/all_to_all | solution.py:268
  250.6 2.1 convolution_convert_fusion
  252.7 6.8 %all-to-all-done.13 = f32[8,64,256]{2,1,0:T(8,128)S(1)} async-done(((f32[8,64,256]{2,1,0:T(8,128)}), f32[8,64,256]{2,1,0:T(8,128)S(1)}, u32[]{:S(2)}, u32[]{:S(2)}) %all-to-all-start.13) | async-done | bytes 524320 | tf_op jit(solution)/shard_map/all_to_all | solution.py:268
  259.5 1.5 gather_fusion.1
  261.0 3.9 %reduce-scatter.2.cloned.1.call-done.others = bf16[9,128,128]{2,1,0:T(8,128)(2,1)} async-done(((bf16[144,128,128]{2,1,0:T(8,128)(2,1)}), bf16[9,128,128]{2,1,0:T(8,128)(2,1)}) %reduce-scatter.2.cloned.1.call-update) | async-done | bytes 294928 | tf_op jit(solution)/shard_map/reduce_scatter | solution.py:419
  264.9 1.0 copy-done.7
  265.9 1.9 shard_map.119
  (69 shorter events, 0.9 us)
Async XLA Ops:
  7.2 16.3 %copy-start = (bf16[512,256]{1,0:T(8,128)(2,1)S(1)}, bf16[512,256]{1,0:T(8,128)(2,1)}, u32[]{:S(2)}) copy-start(bf16[512,256]{1,0:T(8,128)(2,1)} %param.15) | copy-start | bytes 786436
  7.2 17.6 %copy-start.32 = (s32[128]{0:T(128)S(1)}, s32[128]{0:T(128)}, u32[]{:S(2)}) copy-start(s32[128]{0:T(128)} %param.18) | copy-start | bytes 1540
  7.2 88.0 %all-gather.2.cloned.1.call-start = ((), (), s32[]{:S(2)}) async-start(), calls=%async_computation.15 | async-start | bytes 5013504 | tf_op jit(solution)/shard_map/all_gather | solution.py:288
  9.9 13.5 %copy-start.20 = (s32[27]{0:T(128)}, s32[27]{0:T(128)S(1)}, u32[]{:S(2)}) copy-start(s32[27]{0:T(128)S(1)} %reshape.226) | copy-start | bytes 328
  10.1 0.6 copy-start.25
  12.1 13.8 %all-to-all-start.8 = ((s32[8,1,17]{2,1,0:T(1,128)}), s32[8,1,17]{2,1,0:T(1,128)S(1)}, u32[]{:S(2)}, u32[]{:S(2)}) async-start(s32[8,1,17]{2,1,0:T(1,128)} %bitcast.15), calls=%async_computation.8 | async-start | bytes 8192 | tf_op jit(solution)/shard_map/all_to_all | solution.py:268
  17.8 55.5 %collective-permute-start.20 = (bf16[128,128]{1,0:T(8,128)(2,1)S(1)}, bf16[128,128]{1,0:T(8,128)(2,1)S(1)}, u32[]{:S(2)}, u32[]{:S(2)}) collective-permute-start(bf16[128,128]{1,0:T(8,128)(2,1)S(1)} %get-tuple-element.296), channel_id=1, source_target_pairs={{0,4},{4,8},{8,12},{12,16},{16,20},{20,24},{24,28},{28,32},{32,36}... | collective-permute-start | bytes 98312 | tf_op jit(solution)/shard_map/ppermute | solution.py:323
  19.9 53.5 %collective-permute-start.21 = (bf16[128,128]{1,0:T(8,128)(2,1)S(1)}, bf16[128,128]{1,0:T(8,128)(2,1)S(1)}, u32[]{:S(2)}, u32[]{:S(2)}) collective-permute-start(bf16[128,128]{1,0:T(8,128)(2,1)S(1)} %get-tuple-element.295), channel_id=1, source_target_pairs={{4,0},{8,4},{12,8},{16,12},{20,16},{24,20},{28,24},{32,28},{36,32}... | collective-permute-start | bytes 98312 | tf_op jit(solution)/shard_map/ppermute | solution.py:324
  24.7 39.3 %copy-start.37 = (s32[3]{0:T(128)S(1)}, s32[3]{0:T(128)}, u32[]{:S(2)}) copy-start(s32[3]{0:T(128)} %constant.223.clone) | copy-start | bytes 40
  24.8 70.4 %copy-start.8 = (bf16[576,128]{1,0:T(8,128)(2,1)S(1)}, bf16[576,128]{1,0:T(8,128)(2,1)}, u32[]{:S(2)}) copy-start(bf16[576,128]{1,0:T(8,128)(2,1)} %param.14) | copy-start | bytes 442372
  24.8 70.4 %copy-start.9 = (bf16[576,128]{1,0:T(8,128)(2,1)S(1)}, bf16[576,128]{1,0:T(8,128)(2,1)}, u32[]{:S(2)}) copy-start(bf16[576,128]{1,0:T(8,128)(2,1)} %param.13) | copy-start | bytes 442372
  24.8 70.4 %copy-start.11 = (bf16[576,256]{1,0:T(8,128)(2,1)S(1)}, bf16[576,256]{1,0:T(8,128)(2,1)}, u32[]{:S(2)}) copy-start(bf16[576,256]{1,0:T(8,128)(2,1)} %param.16) | copy-start | bytes 884740
  24.8 70.4 %copy-start.16 = (bf16[576,128]{1,0:T(8,128)(2,1)S(1)}, bf16[576,128]{1,0:T(8,128)(2,1)}, u32[]{:S(2)}) copy-start(bf16[576,128]{1,0:T(8,128)(2,1)} %param.12) | copy-start | bytes 442372
  27.9 27.6 %all-to-all-start.9 = ((s32[16,1,1]{2,1,0:T(1,128)}), s32[16,1,1]{2,1,0:T(1,128)S(1)}, u32[]{:S(2)}, u32[]{:S(2)}) async-start(s32[16,1,1]{2,1,0:T(1,128)} %broadcast_in_dim.62), calls=%async_computation.9 | async-start | bytes 16384 | tf_op jit(solution)/shard_map/all_to_all | solution.py:268
  55.5 17.8 %all-to-all-start.10 = ((f32[4,576,128]{2,1,0:T(8,128)}), f32[4,576,128]{2,1,0:T(8,128)S(1)}, u32[]{:S(2)}, u32[]{:S(2)}) async-start(f32[4,576,128]{2,1,0:T(8,128)} %bitcast.70), calls=%async_computation.10 | async-start | bytes 2359296 | tf_op jit(solution)/shard_map/all_to_all | solution.py:268
  60.3 204.6 %reduce-scatter.2.cloned.1.call-start = ((), (), s32[]{:S(2)}) async-start(), calls=%async_computation.16 | async-start | bytes 5013504 | tf_op jit(solution)/shard_map/reduce_scatter | solution.py:419
  61.8 33.4 %copy-start.19 = (s32[1024]{0:T(1024)}, s32[1024]{0:T(1024)S(1)}, u32[]{:S(2)}) copy-start(s32[1024]{0:T(1024)S(1)} %pad_clamp_fusion) | copy-start | bytes 12292
  95.2 4.8 %copy-start.12 = (bf16[576,256]{1,0:T(8,128)(2,1)}, bf16[576,256]{1,0:T(8,128)(2,1)S(1)}, u32[]{:S(2)}) copy-start(bf16[576,256]{1,0:T(8,128)(2,1)S(1)} %get-tuple-element.175) | copy-start | bytes 884740 | tf_op jit(solution)/shard_map/cond
  95.2 4.8 %copy-start.33 = (s32[128]{0:T(128)}, s32[128]{0:T(128)S(1)}, u32[]{:S(2)}) copy-start(s32[128]{0:T(128)S(1)} %get-tuple-element.163) | copy-start | bytes 1540 | tf_op jit(solution)/shard_map/cond
  95.2 4.8 %copy-start.35 = (s32[128]{0:T(128)}, s32[128]{0:T(128)S(1)}, u32[]{:S(2)}) copy-start(s32[128]{0:T(128)S(1)} %get-tuple-element.164) | copy-start | bytes 1540 | tf_op jit(solution)/shard_map/cond
  100.0 34.8 %copy-start.22 = (s32[27]{0:T(128)S(1)}, s32[27]{0:T(128)}, u32[]{:S(2)}) copy-start(s32[27]{0:T(128)} %get-tuple-element.155.names) | copy-start | bytes 328 | tf_op jit(solution)/shard_map/cond
  100.0 34.8 %copy-start.27 = (s32[27]{0:T(128)S(1)}, s32[27]{0:T(128)}, u32[]{:S(2)}) copy-start(s32[27]{0:T(128)} %get-tuple-element.156.ranks) | copy-start | bytes 328 | tf_op jit(solution)/shard_map/cond
  100.1 34.8 %all-to-all-start.2 = ((bf16[8,1216,128]{2,1,0:T(8,128)(2,1)}), bf16[8,1216,128]{2,1,0:T(8,128)(2,1)S(1)}, u32[]{:S(2)}, u32[]{:S(2)}) async-start(bf16[8,1216,128]{2,1,0:T(8,128)(2,1)} %branch_1_fun.3), calls=%async_computation.2 | async-start | bytes 4980736 | tf_op jit(solution)/shard_map/cond/branch_1_fun/all_to_all | solution.py:268
  142.7 1.5 copy-start.5
  144.2 22.3 %copy-start.13 = (bf16[576,256]{1,0:T(8,128)(2,1)S(1)}, bf16[576,256]{1,0:T(8,128)(2,1)}, u32[]{:S(2)}) copy-start(bf16[576,256]{1,0:T(8,128)(2,1)} %copy-done.12) | copy-start | bytes 884740 | tf_op jit(solution)/shard_map/cond
  144.2 35.1 %all-to-all-start.3 = ((bf16[8,1216,128]{2,1,0:T(8,128)(2,1)}), bf16[8,1216,128]{2,1,0:T(8,128)(2,1)S(1)}, u32[]{:S(2)}, u32[]{:S(2)}) async-start(bf16[8,1216,128]{2,1,0:T(8,128)(2,1)} %copy-done.5), calls=%async_computation.3 | async-start | bytes 4980736 | tf_op jit(solution)/shard_map/cond/branch_1_fun/all_to_all | solution.py:268
  149.3 15.1 %collective-permute-start.5 = (bf16[576,128]{1,0:T(8,128)(2,1)S(1)}, bf16[576,128]{1,0:T(8,128)(2,1)S(1)}, u32[]{:S(2)}, u32[]{:S(2)}) collective-permute-start(bf16[576,128]{1,0:T(8,128)(2,1)S(1)} %get-tuple-element.169), channel_id=1, source_target_pairs={{0,1},{1,2},{2,3},{3,0},{4,5},{5,6},{6,7},{7,4},{8,9},{9,10},{10,1... | collective-permute-start | bytes 442376 | tf_op jit(solution)/shard_map/cond/branch_1_fun/ppermute | solution.py:381
  151.7 13.4 %collective-permute-start.6 = (bf16[576,128]{1,0:T(8,128)(2,1)S(1)}, bf16[576,128]{1,0:T(8,128)(2,1)S(1)}, u32[]{:S(2)}, u32[]{:S(2)}) collective-permute-start(bf16[576,128]{1,0:T(8,128)(2,1)S(1)} %get-tuple-element.169), channel_id=1, source_target_pairs={{0,2},{1,3},{2,0},{3,1},{4,6},{5,7},{6,4},{7,5},{8,10},{9,11},{10,... | collective-permute-start | bytes 442376 | tf_op jit(solution)/shard_map/cond/branch_1_fun/ppermute | solution.py:381
  156.2 9.6 %collective-permute-start.7 = (bf16[576,128]{1,0:T(8,128)(2,1)S(1)}, bf16[576,128]{1,0:T(8,128)(2,1)S(1)}, u32[]{:S(2)}, u32[]{:S(2)}) collective-permute-start(bf16[576,128]{1,0:T(8,128)(2,1)S(1)} %get-tuple-element.169), channel_id=1, source_target_pairs={{0,3},{1,0},{2,1},{3,2},{4,7},{5,4},{6,5},{7,6},{8,11},{9,8},{10,9... | collective-permute-start | bytes 442376 | tf_op jit(solution)/shard_map/cond/branch_1_fun/ppermute | solution.py:381
  158.8 19.2 %collective-permute-start.8 = (bf16[128,128]{1,0:T(8,128)(2,1)S(1)}, bf16[128,128]{1,0:T(8,128)(2,1)}, u32[]{:S(2)}, u32[]{:S(2)}) collective-permute-start(bf16[128,128]{1,0:T(8,128)(2,1)S(1)} %get-tuple-element.290), channel_id=1, source_target_pairs={{0,4},{4,8},{8,12},{12,16},{16,20},{20,24},{24,28},{28,32},{32,36}... | collective-permute-start | bytes 98312 | tf_op jit(solution)/shard_map/cond/branch_1_fun/ppermute | solution.py:384
  160.8 17.3 %collective-permute-start.9 = (bf16[128,128]{1,0:T(8,128)(2,1)S(1)}, bf16[128,128]{1,0:T(8,128)(2,1)}, u32[]{:S(2)}, u32[]{:S(2)}) collective-permute-start(bf16[128,128]{1,0:T(8,128)(2,1)S(1)} %get-tuple-element.289), channel_id=1, source_target_pairs={{4,0},{8,4},{12,8},{16,12},{20,16},{24,20},{28,24},{32,28},{36,32}... | collective-permute-start | bytes 98312 | tf_op jit(solution)/shard_map/cond/branch_1_fun/ppermute | solution.py:385
  184.4 66.3 %copy-start.10 = (bf16[4,128,256]{2,1,0:T(8,128)(2,1)S(1)}, bf16[4,128,256]{2,1,0:T(8,128)(2,1)}, u32[]{:S(2)}) copy-start(bf16[4,128,256]{2,1,0:T(8,128)(2,1)} %gather_fusion) | copy-start | bytes 786436
  185.4 11.3 %collective-permute-start.22 = (f32[4,64,256]{2,1,0:T(8,128)S(1)}, f32[4,64,256]{2,1,0:T(8,128)S(1)}, u32[]{:S(2)}, u32[]{:S(2)}) collective-permute-start(f32[4,64,256]{2,1,0:T(8,128)S(1)} %dynamic-slice_bitcast_fusion), channel_id=1, source_target_pairs={{0,16},{4,20},{8,24},{12,28},{16,0},{20,4},{24,8},{28,12},{1,17},{... | collective-permute-start | bytes 786440 | tf_op jit(solution)/shard_map/ppermute | solution.py:428
  197.7 6.9 %collective-permute-start.23 = (f32[2,64,256]{2,1,0:T(8,128)S(1)}, f32[2,64,256]{2,1,0:T(8,128)S(1)}, u32[]{:S(2)}, u32[]{:S(2)}) collective-permute-start(f32[2,64,256]{2,1,0:T(8,128)S(1)} %dynamic-slice_bitcast_fusion.1), channel_id=1, source_target_pairs={{0,8},{4,12},{8,0},{12,4},{16,24},{20,28},{24,16},{28,20},{1,9},{5... | collective-permute-start | bytes 393224 | tf_op jit(solution)/shard_map/ppermute | solution.py:428
  204.6 3.1 %collective-permute-start.24 = (f32[1,64,256]{2,1,0:T(8,128)S(1)}, f32[1,64,256]{2,1,0:T(8,128)S(1)}, u32[]{:S(2)}, u32[]{:S(2)}) collective-permute-start(f32[1,64,256]{2,1,0:T(8,128)S(1)} %constant_dynamic-slice_fusion), channel_id=1, source_target_pairs={{0,4},{4,0},{8,12},{12,8},{16,20},{20,16},{24,28},{28,24},{1,5},{5... | collective-permute-start | bytes 196616 | tf_op jit(solution)/shard_map/ppermute | solution.py:428
  207.8 60.0 %copy-start.1 = (bf16[512,256]{1,0:T(8,128)(2,1)S(1)}, bf16[512,256]{1,0:T(8,128)(2,1)}, u32[]{:S(2)}) copy-start(bf16[512,256]{1,0:T(8,128)(2,1)} %param.15) | copy-start | bytes 786436
  245.6 13.9 %all-to-all-start.13 = ((f32[8,64,256]{2,1,0:T(8,128)}), f32[8,64,256]{2,1,0:T(8,128)S(1)}, u32[]{:S(2)}, u32[]{:S(2)}) async-start(f32[8,64,256]{2,1,0:T(8,128)} %broadcast_in_dim.68), calls=%async_computation.14 | async-start | bytes 1048576 | tf_op jit(solution)/shard_map/all_to_all | solution.py:268
  264.9 1.0 copy-start.7
Sparse Core Ops, SparseCore 0:
  10.7 84.4 all-gather.1
  184.5 80.3 reduce-scatter.1
